TPU v7x, 512 devices: a whole 4x8x8 slice. The times are simulated.
512 devices in a mesh: node: 4 (over z_lo, core), group: 32 (over x, y), fsdp: 4 (over z_hi).
Axes of the slice: x: 4, y: 8, z: 8 (z_hi: 4, z_lo: 2; z = z_hi * 2 + z_lo), core: 2. Of those that a mesh axis runs over, the one named last changes fastest.
Arguments:
- grad_values: bfloat16 [4, 32, 4, 128, 12288], P('node', 'group', 'fsdp'), may hold values from -6 to 6
- grad_scales: bfloat16 [4, 32, 4, 128, 96], P('node', 'group', 'fsdp'), may hold values from 0.5 to 4
- master: float32 [4, 128, 12288], P('fsdp', 'group'), may hold values from -6 to 6
- first_moment: bfloat16 [4, 128, 12288], P('fsdp', 'group'), may hold values from -1 to 1
- first_scale: float32 [4, 128, 96], P('fsdp', 'group'), may hold values from 0.5 to 2
- second_moment: bfloat16 [4, 128, 12288], P('fsdp', 'group'), may hold values from 0.049804688 to 1
- second_scale: float32 [4, 128, 96], P('fsdp', 'group'), may hold values from 10 to 100
Outputs:
- new_master: float32 [4, 128, 12288], P('fsdp', 'group')
- new_first: bfloat16 [4, 128, 12288], P('fsdp', 'group')
- new_first_scale: float32 [4, 128, 96], P('fsdp', 'group')
- new_second: bfloat16 [4, 128, 12288], P('fsdp', 'group')
- new_second_scale: float32 [4, 128, 96], P('fsdp', 'group')
- weights: bfloat16 [4, 128, 12288], P('fsdp')
- transposed: bfloat16 [4, 12288, 128], P('fsdp')
All inputs are finite; a program needn't handle non-finite values. Where the computation divides by a largest or mean magnitude, that divisor is 1e-20 or more.
Results may differ from a plain program's by a relative error of at most 0.001.
Values may be sent and summed in bfloat16 or wider, within the bound.
No kernel may reach another device: no remote copies, remote signals or barrier semaphores. Data moves between devices by JAX's collectives and lax.ppermute only.
A program may use at most 128 MiB of HBM per device.

v0:
```python
import jax
import jax.numpy as jnp
from jax import lax
from jax.sharding import PartitionSpec as P

BLOCK = 128


beta_one = 0.9
beta_two = 0.95
rate = 0.02
adam_eps = 1e-08
scale_eps = 1e-06
corr_one = 1.0 - 0.9**10
corr_two = 1.0 - 0.95**10


def expand(values, scales):
    shape = values.shape
    blocks = values.astype(jnp.float32).reshape(shape[:-1] + (shape[-1] // BLOCK, BLOCK))
    return (blocks * scales.astype(jnp.float32)[..., None]).reshape(shape)


def quantize(values, signed):
    shape = values.shape
    blocks = values.reshape(shape[:-1] + (shape[-1] // BLOCK, BLOCK))
    if signed:
        peak = jnp.max(jnp.abs(blocks), axis=-1) + scale_eps
    else:
        peak = jnp.max(blocks, axis=-1) + scale_eps
    coded = (blocks / peak[..., None]).astype(jnp.bfloat16).reshape(shape)
    return (coded, peak)


def adam_step(gradient, master, first_moment, first_scale, second_moment, second_scale):
    first = beta_one * expand(first_moment, first_scale) + (1.0 - beta_one) * gradient
    second = beta_two * expand(second_moment, second_scale) + (1.0 - beta_two) * gradient * gradient
    direction = first / corr_one / (jnp.sqrt(second / corr_two) + adam_eps)
    updated = master - rate * direction
    first_coded, first_peak = quantize(first, True)
    second_coded, second_peak = quantize(second, False)
    return (
        updated,
        first_coded,
        first_peak,
        second_coded,
        second_peak,
        updated.astype(jnp.bfloat16),
    )


def on_device(
    grad_values, grad_scales, master, first_moment, first_scale, second_moment, second_scale
):
    arrived, arrived_scales = (
        lax.all_to_all(grad_values, "group", split_axis=3, concat_axis=1, tiled=True),
        lax.all_to_all(grad_scales, "group", split_axis=3, concat_axis=1, tiled=True),
    )
    partial_sum = jnp.sum(expand(arrived, arrived_scales), axis=1)
    partial_sum = partial_sum.reshape(master.shape)
    gradient = lax.psum(partial_sum, "node")
    result = adam_step(gradient, master, first_moment, first_scale, second_moment, second_scale)
    updated, first_coded, first_peak, second_coded, second_peak, low_weights = result
    weights = lax.all_gather(low_weights, "group", axis=1, tiled=True)
    transposed = jnp.swapaxes(weights, 1, 2)
    return (updated, first_coded, first_peak, second_coded, second_peak, weights, transposed)


def solution(mesh):
    placed = (
        P("node", "group", "fsdp", None, None),
        P("node", "group", "fsdp", None, None),
        P("fsdp", "group", None),
        P("fsdp", "group", None),
        P("fsdp", "group", None),
        P("fsdp", "group", None),
        P("fsdp", "group", None),
    )
    return jax.shard_map(
        on_device,
        mesh=mesh,
        in_specs=placed,
        out_specs=(
            P("fsdp", "group", None),
            P("fsdp", "group", None),
            P("fsdp", "group", None),
            P("fsdp", "group", None),
            P("fsdp", "group", None),
            P("fsdp", None, None),
            P("fsdp", None, None),
        ),
        check_vma=False,
    )
```

profile of v0, /device:TPU:1, one launch (start us, length us, event | category | flops | bytes accessed | tf_op | source)
XLA Modules:
  0.0 331.2 jit_solution(7683410294636461108)
XLA Ops:
  7.2 0.9 copy.20
  8.0 0.5 broadcast.70
  8.5 0.8 reduce.6
  9.4 0.7 reshape.163
  10.1 10.5 %all-to-all-start.1 = ((bf16[32,2,192]{2,1,0:T(2,128)(2,1)}), bf16[32,2,192]{2,1,0:T(2,128)(2,1)S(1)}, u32[]{:S(2)}, u32[]{:S(2)}) async-start(bf16[32,2,192]{2,1,0:T(2,128)(2,1)} %reshape.163), calls=%async_computation.1 | async-start | bytes 65536 | tf_op jit(solution)/shard_map/all_to_all | solution.py:57
  20.6 8.6 %copy.48 = bf16[1,1,1,128,12288]{4,2,1,0,3:T(2,128)(2,1)} copy(bf16[1,1,1,128,12288]{4,3,2,1,0:T(8,128)(2,1)} %param.7) | data formatting | bytes 6291456 | tf_op args[0]
  29.2 19.0 %reduce.5 = bf16[128,12288]{1,0:T(8,128)(2,1)S(1)} reduce(bf16[128,1,1,1,12288]{4,3,2,1,0:T(2,128)(2,1)} %bitcast.26, bf16[]{:T(256)} %broadcast.70), dimensions={1,2,3}, to_apply=%bitcast.23.reduce_sub_computation | reduce | bytes 6291458
  48.2 3.6 %reshape.161 = bf16[32,2,24576]{2,1,0:T(2,128)(2,1)} reshape(bf16[128,12288]{1,0:T(8,128)(2,1)S(1)} %reduce.5) | data formatting | bytes 6291456
  51.8 0.0 all-to-all-done.1
  51.8 9.2 %all-to-all-start = ((bf16[32,2,24576]{2,1,0:T(2,128)(2,1)}), bf16[32,2,24576]{2,1,0:T(2,128)(2,1)S(1)}, u32[]{:S(2)}, u32[]{:S(2)}) async-start(bf16[32,2,24576]{2,1,0:T(2,128)(2,1)} %reshape.161), calls=%async_computation | async-start | bytes 6291456 | tf_op jit(solution)/shard_map/all_to_all | solution.py:56
  61.1 0.0 all-reduce.2.cloned.1.call-start
  61.1 0.1 reshape.164
  61.2 71.0 %all-to-all-done = bf16[32,2,24576]{2,1,0:T(2,128)(2,1)S(1)} async-done(((bf16[32,2,24576]{2,1,0:T(2,128)(2,1)}), bf16[32,2,24576]{2,1,0:T(2,128)(2,1)S(1)}, u32[]{:S(2)}, u32[]{:S(2)}) %all-to-all-start) | async-done | bytes 3145760 | tf_op jit(solution)/shard_map/all_to_all | solution.py:56
  132.2 12.4 %reshape.162 = bf16[128,1,1,1,12288]{4,3,2,1,0:T(2,128)(2,1)} reshape(bf16[32,2,24576]{2,1,0:T(2,128)(2,1)S(1)} %all-to-all-done) | data formatting | bytes 6291456
  144.6 7.8 %bitcast_convert_fusion = f32[1,1,1,128,12288]{4,2,1,0,3:T(1,128)S(1)} fusion(bf16[128,1,1,1,12288]{4,3,2,1,0:T(2,128)(2,1)} %reshape.162), kind=kLoop, calls=%fused_computation.19 | loop fusion | flops 1572864 | bytes 9437184 | tf_op jit(solution)/shard_map/convert_element_type | solution.py:20
  152.4 0.0 copy-start.3
  152.4 0.0 copy-start.4
  152.4 0.0 copy-start
  152.4 0.0 copy-start.1
  152.5 0.0 copy-start.2
  152.5 2.6 multiply_reduce_fusion
  155.1 0.0 all-reduce.2.cloned.1.call-update
  155.1 0.2 all-gather.2.cloned.1.call-start
  155.4 50.4 %all-reduce.2.cloned.1.call-done = f32[1,4,12288]{2,0,1:T(1,128)} async-done(((f32[1,4,12288]{2,0,1:T(1,128)}), f32[1,4,12288]{2,0,1:T(1,128)}) %all-reduce.2.cloned.1.call-update) | async-done | bytes 196624 | tf_op jit(solution)/shard_map/psum | solution.py:61
  205.8 0.0 copy-done.3
  205.8 0.1 mul.86
  205.9 0.0 copy-done.4
  205.9 0.1 mul.96
  206.0 0.0 copy-done
  206.0 0.0 copy-done.1
  206.0 0.0 copy-done.2
  206.0 3.0 fusion.8
  209.0 0.0 all-gather.2.cloned.1.call-update
  209.0 0.8 copy.24
  209.8 0.2 abs.17
  210.1 0.1 reduce_max.19
  210.2 0.1 reduce_max.18
  210.4 0.6 fusion.7
  210.9 0.6 fusion.6
  211.5 0.1 div.49
  211.6 0.1 div.46
  211.7 0.4 divide_convert_fusion
  212.2 0.8 copy.25
  212.9 0.8 copy.26
  213.7 89.4 %all-gather.2.cloned.1.call-done = bf16[1,128,12288]{2,0,1:T(2,128)(2,1)} async-done(((bf16[1,4,12288]{2,0,1:T(2,128)(2,1)}), bf16[1,128,12288]{2,0,1:T(2,128)(2,1)}) %all-gather.2.cloned.1.call-update) | async-done | bytes 3145744 | tf_op jit(solution)/shard_map/all_gather | solution.py:64
  303.2 13.4 %copy.28 = bf16[1,12288,128]{2,1,0:T(8,128)(2,1)} copy(bf16[1,12288,128]{1,0,2:T(2,128)(2,1)} %bitcast.24) | data formatting | bytes 6291456
  316.5 7.8 %copy.27 = bf16[1,128,12288]{2,1,0:T(8,128)(2,1)} copy(bf16[1,128,12288]{2,0,1:T(2,128)(2,1)} %all-gather.2.cloned.1.call-done) | data formatting | bytes 6291456
  (2 shorter events, 0.0 us)
Async XLA Ops:
  10.1 41.7 %all-to-all-start.1 = ((bf16[32,2,192]{2,1,0:T(2,128)(2,1)}), bf16[32,2,192]{2,1,0:T(2,128)(2,1)S(1)}, u32[]{:S(2)}, u32[]{:S(2)}) async-start(bf16[32,2,192]{2,1,0:T(2,128)(2,1)} %reshape.163), calls=%async_computation.1 | async-start | bytes 65536 | tf_op jit(solution)/shard_map/all_to_all | solution.py:57
  51.8 80.4 %all-to-all-start = ((bf16[32,2,24576]{2,1,0:T(2,128)(2,1)}), bf16[32,2,24576]{2,1,0:T(2,128)(2,1)S(1)}, u32[]{:S(2)}, u32[]{:S(2)}) async-start(bf16[32,2,24576]{2,1,0:T(2,128)(2,1)} %reshape.161), calls=%async_computation | async-start | bytes 6291456 | tf_op jit(solution)/shard_map/all_to_all | solution.py:56
  61.1 144.7 %all-reduce.2.cloned.1.call-start = ((), (), s32[]{:S(2)}) async-start(), calls=%async_computation.2 | async-start | bytes 393216 | tf_op jit(solution)/shard_map/psum | solution.py:61
  152.4 53.4 %copy-start.3 = (f32[1,4,96]{2,1,0:T(4,128)S(1)}, f32[1,4,96]{2,1,0:T(4,128)}, u32[]{:S(2)}) copy-start(f32[1,4,96]{2,1,0:T(4,128)} %param.11) | copy-start | bytes 4612
  152.4 53.5 %copy-start.4 = (f32[1,4,96]{2,1,0:T(4,128)S(1)}, f32[1,4,96]{2,1,0:T(4,128)}, u32[]{:S(2)}) copy-start(f32[1,4,96]{2,1,0:T(4,128)} %param.13) | copy-start | bytes 4612
  152.4 53.6 %copy-start = (f32[1,4,12288]{2,1,0:T(4,128)S(1)}, f32[1,4,12288]{2,1,0:T(4,128)}, u32[]{:S(2)}) copy-start(f32[1,4,12288]{2,1,0:T(4,128)} %param.9) | copy-start | bytes 589828
  152.4 53.6 %copy-start.1 = (bf16[1,4,12288]{2,1,0:T(4,128)(2,1)S(1)}, bf16[1,4,12288]{2,1,0:T(4,128)(2,1)}, u32[]{:S(2)}) copy-start(bf16[1,4,12288]{2,1,0:T(4,128)(2,1)} %param.10) | copy-start | bytes 294916
  152.5 53.6 %copy-start.2 = (bf16[1,4,12288]{2,1,0:T(4,128)(2,1)S(1)}, bf16[1,4,12288]{2,1,0:T(4,128)(2,1)}, u32[]{:S(2)}) copy-start(bf16[1,4,12288]{2,1,0:T(4,128)(2,1)} %param.12) | copy-start | bytes 294916
  155.1 148.0 %all-gather.2.cloned.1.call-start = ((), (), s32[]{:S(2)}) async-start(), calls=%async_computation.3 | async-start | bytes 6488064 | tf_op jit(solution)/shard_map/all_gather | solution.py:64
Sparse Core Ops, SparseCore 0:
  155.3 50.4 all-reduce.1
  210.0 93.1 all-gather.1
where the time goes:
time: 332 us; the launch traced here: 331 us
  waiting for transfers between devices  211 us (64%)
  local copies, waits for them, and re-layouts  50.8 us (15%)
  other arithmetic  35.3 us (11%)
  starting transfers between devices  20 us (6%)
  between operations  14.2 us (4%)
    all_gather x1, waiting for transfers between devices, on_device(): weights = lax.all_gather(low_weights, 'group', axis=1, tiled=True)  89.4 us
    all_to_all x1, waiting for transfers between devices, on_device(): lax.all_to_all(grad_values, 'group', split_axis=3, concat_axis=1, tiled=T...  71 us
    psum x1, waiting for transfers between devices, on_device(): gradient = lax.psum(partial_sum, 'node')  50.4 us
    unnamed x22, local copies, waits for them, and re-layouts  50.4 us
    unnamed x2, other arithmetic  19.8 us
    all_to_all x1, starting transfers between devices, on_device(): lax.all_to_all(grad_scales, 'group', split_axis=3, concat_axis=1, tiled=T...  10.5 us
    all_to_all x1, starting transfers between devices, on_device(): lax.all_to_all(grad_values, 'group', split_axis=3, concat_axis=1, tiled=T...  9.23 us
    convert_element_type x1, other arithmetic, expand(): values.astype(jnp.float32).reshape(shape[:-1] + (shape[-1] // BLOCK, BLOCK))  7.77 us
  transfers between devices with their start and end apart: 4, of which 3 were waited for; matrix products, arithmetic and copies ran while one was open for 11% of the time, Pallas kernels for 0%

commit v1 on v0

v1 whole, which is shorter than its diff:
```python
import functools

import jax
import jax.numpy as jnp
from jax import lax
from jax.experimental import pallas as pl
from jax.experimental.pallas import tpu as pltpu
from jax.sharding import Mesh, PartitionSpec as P

D = 12288
HALF = D // 2
BLOCK = 128
NB = D // BLOCK
HB = NB // 2
ROWS = 128
NX, NY, NZ = 4, 8, 2
XR = ROWS // NX
YR = XR // NY
PAD = D + BLOCK
CH = 1024

beta_one = 0.9
beta_two = 0.95
rate = 0.02
adam_eps = 1e-08
scale_eps = 1e-06
corr_one = 1.0 - 0.9**10
corr_two = 1.0 - 0.95**10

f32 = jnp.float32
bf16 = jnp.bfloat16


def params(mib=48):
    return pltpu.CompilerParams(vmem_limit_bytes=mib * 1024 * 1024)


def cost(flops, nbytes):
    return pl.CostEstimate(flops=flops, bytes_accessed=nbytes, transcendentals=0)


def pack_kernel(idx, values, scales, out):
    out[:, :D] = values[...]
    out[:, D : D + NB] = scales[...]
    out[:, D + NB :] = jnp.zeros((XR, PAD - D - NB), bf16)


def pack(block, values, scales):
    return pl.pallas_call(
        pack_kernel,
        grid_spec=pltpu.PrefetchScalarGridSpec(
            num_scalar_prefetch=1,
            grid=(1,),
            in_specs=[
                pl.BlockSpec((XR, D), lambda i, s: (s[0], 0)),
                pl.BlockSpec((XR, NB), lambda i, s: (s[0], 0)),
            ],
            out_specs=pl.BlockSpec((XR, PAD), lambda i, s: (0, 0)),
        ),
        out_shape=jax.ShapeDtypeStruct((XR, PAD), bf16),
        compiler_params=params(),
        cost_estimate=cost(0, 2 * XR * D * 2),
        name="pack_rows",
    )(block, values, scales)


def sum_kernel(idx, v0, s0, v1, s1, v2, s2, v3, s3, out):
    first_half = idx[1] == 0
    scales = []
    for ref in (s0, s1, s2, s3):
        both = ref[...].astype(f32)
        scales.append(jnp.where(first_half, both[:, :HB], both[:, HB:NB]))
    for b in range(HB):
        cols = slice(b * BLOCK, (b + 1) * BLOCK)
        total = None
        for ref, scale in zip((v0, v1, v2, v3), scales):
            term = ref[:, cols].astype(f32) * scale[:, b : b + 1]
            total = term if total is None else total + term
        for i in range(NY):
            out[i, :, cols] = total[i * YR : (i + 1) * YR, :]


def sum_half(idx, values, scales, arrived):
    value_spec = pl.BlockSpec((XR, HALF), lambda i, s: (0, s[1]))
    scale_spec = pl.BlockSpec((XR, BLOCK), lambda i, s: (0, NB))
    ins = [
        pl.BlockSpec((XR, HALF), lambda i, s: (s[0], s[1])),
        pl.BlockSpec((XR, NB), lambda i, s: (s[0], 0)),
    ]
    args = [values, scales]
    for a in arrived:
        ins += [value_spec, scale_spec]
        args += [a, a]
    return pl.pallas_call(
        sum_kernel,
        grid_spec=pltpu.PrefetchScalarGridSpec(
            num_scalar_prefetch=1,
            grid=(1,),
            in_specs=ins,
            out_specs=pl.BlockSpec((NY, YR, HALF), lambda i, s: (0, 0, 0)),
        ),
        out_shape=jax.ShapeDtypeStruct((NY, YR, HALF), f32),
        compiler_params=params(),
        cost_estimate=cost(8 * XR * HALF, 12 * XR * HALF),
        name="sum_over_x",
    )(idx, *args)


def adam(gradient, master, first_old, second_old):
    first = beta_one * first_old + (1.0 - beta_one) * gradient
    second = beta_two * second_old + (1.0 - beta_two) * gradient * gradient
    direction = first / corr_one / (jnp.sqrt(second / corr_two) + adam_eps)
    return first, second, master - rate * direction


def low_kernel(idx, g0, g1, master, fm, fs, sm, ss, grad_out, low_out):
    first_half = idx[0] == 0
    fsv, ssv = fs[...], ss[...]
    fscale = jnp.where(first_half, fsv[:, :HB], fsv[:, HB:])
    sscale = jnp.where(first_half, ssv[:, :HB], ssv[:, HB:])
    for b in range(HB):
        cols = slice(b * BLOCK, (b + 1) * BLOCK)
        gradient = g0[:, cols] + g1[:, cols]
        grad_out[:, cols] = gradient
        first_old = fm[:, cols].astype(f32) * fscale[:, b : b + 1]
        second_old = sm[:, cols].astype(f32) * sscale[:, b : b + 1]
        _, _, updated = adam(gradient, master[:, cols], first_old, second_old)
        low = updated.astype(bf16)
        for i in range(NY):
            low_out[i, :, cols] = low


def low_weights(core, g0, g1, master, fm, fs, sm, ss):
    half = pl.BlockSpec((YR, HALF), lambda i, s: (0, s[0]))
    whole = pl.BlockSpec((YR, HALF), lambda i, s: (0, 0))
    scale = pl.BlockSpec((YR, NB), lambda i, s: (0, 0))
    return pl.pallas_call(
        low_kernel,
        grid_spec=pltpu.PrefetchScalarGridSpec(
            num_scalar_prefetch=1,
            grid=(1,),
            in_specs=[whole, whole, half, half, scale, half, scale],
            out_specs=[whole, pl.BlockSpec((NY, YR, HALF), lambda i, s: (0, 0, 0))],
        ),
        out_shape=[
            jax.ShapeDtypeStruct((YR, HALF), f32),
            jax.ShapeDtypeStruct((NY, YR, HALF), bf16),
        ],
        compiler_params=params(),
        cost_estimate=cost(30 * YR * HALF, 40 * YR * HALF),
        name="low_weights",
    )(core, g0, g1, master, fm, fs, sm, ss)


def state_kernel(idx, mine, other, master, fm, fs, sm, ss, om, of, ofs, os, oss):
    first_half = idx[0] == 0
    fsv, ssv = fs[...], ss[...]
    lane = lax.broadcasted_iota(jnp.int32, (YR, NB), 1)
    fpeaks = jnp.zeros((YR, NB), f32)
    speaks = jnp.zeros((YR, NB), f32)
    for b in range(NB):
        cols = slice(b * BLOCK, (b + 1) * BLOCK)
        inner = slice((b % HB) * BLOCK, (b % HB + 1) * BLOCK)
        one, two = (mine, other) if b < HB else (other, mine)
        gradient = jnp.where(first_half, one[:, inner], two[:, inner])
        first_old = fm[:, cols].astype(f32) * fsv[:, b : b + 1]
        second_old = sm[:, cols].astype(f32) * ssv[:, b : b + 1]
        first, second, updated = adam(gradient, master[:, cols], first_old, second_old)
        om[:, cols] = updated
        fpeak = jnp.max(jnp.abs(first), axis=1, keepdims=True) + scale_eps
        speak = jnp.max(second, axis=1, keepdims=True) + scale_eps
        of[:, cols] = (first / fpeak).astype(bf16)
        os[:, cols] = (second / speak).astype(bf16)
        fpeaks = jnp.where(lane == b, fpeak, fpeaks)
        speaks = jnp.where(lane == b, speak, speaks)
    ofs[...] = fpeaks
    oss[...] = speaks


def states(core, mine, other, master, fm, fs, sm, ss):
    half = pl.BlockSpec((YR, HALF), lambda i, s: (0, 0))
    whole = pl.BlockSpec((YR, D), lambda i, s: (0, 0))
    scale = pl.BlockSpec((YR, NB), lambda i, s: (0, 0))
    shape = jax.ShapeDtypeStruct
    return pl.pallas_call(
        state_kernel,
        grid_spec=pltpu.PrefetchScalarGridSpec(
            num_scalar_prefetch=1,
            grid=(1,),
            in_specs=[half, half, whole, whole, scale, whole, scale],
            out_specs=[whole, whole, scale, whole, scale],
        ),
        out_shape=[
            shape((YR, D), f32),
            shape((YR, D), bf16),
            shape((YR, NB), f32),
            shape((YR, D), bf16),
            shape((YR, NB), f32),
        ],
        compiler_params=params(),
        cost_estimate=cost(60 * YR * D, 20 * YR * D),
        name="new_states",
    )(core, mine, other, master, fm, fs, sm, ss)


def place_kernel(idx, *refs):
    pieces, (weights, transposed, rows) = refs[:8], refs[8:]
    x = idx[0]

    def place(group):
        for shift, ref in enumerate(group):
            start = pl.multiple_of(lax.rem(x + NX - shift, NX) * XR, XR)
            rows[pl.ds(start, XR), :] = ref[...].astype(f32).reshape(XR, CH)

    @pl.when(pl.program_id(0) == 0)
    def _():
        place(pieces[:4])

    @pl.when(pl.program_id(0) == 1)
    def _():
        place(pieces[4:])

    low = rows[...]
    weights[...] = low.astype(bf16)
    transposed[...] = low.T.astype(bf16)


def place_all(idx, mine, other):
    steps = HALF // CH
    first = pl.BlockSpec(
        (NY, YR, CH), lambda h, j, s: (0, 0, jnp.where(h == 0, j, steps - 1))
    )
    second = pl.BlockSpec((NY, YR, CH), lambda h, j, s: (0, 0, jnp.where(h == 0, 0, j)))

    def column(h, j, s):
        return jnp.where(h == 0, s[1], 1 - s[1]) * steps + j

    return pl.pallas_call(
        place_kernel,
        grid_spec=pltpu.PrefetchScalarGridSpec(
            num_scalar_prefetch=1,
            grid=(2, steps),
            in_specs=[first] * 4 + [second] * 4,
            out_specs=[
                pl.BlockSpec((ROWS, CH), lambda h, j, s: (0, column(h, j, s))),
                pl.BlockSpec((CH, ROWS), lambda h, j, s: (column(h, j, s), 0)),
            ],
            scratch_shapes=[pltpu.VMEM((ROWS, CH), f32)],
        ),
        out_shape=[
            jax.ShapeDtypeStruct((ROWS, D), bf16),
            jax.ShapeDtypeStruct((D, ROWS), bf16),
        ],
        compiler_params=params(),
        cost_estimate=cost(0, 3 * ROWS * D * 2),
        name="place_weights",
    )(idx, *mine, *other)


def shift_x(value, shift):
    return lax.ppermute(value, "x", [(i, (i + shift) % NX) for i in range(NX)])


def swap(value, axis):
    return lax.ppermute(value, axis, [(0, 1), (1, 0)])


def on_device(gv, gs, master, fm, fs, sm, ss):
    gv, gs = gv.reshape(ROWS, D), gs.reshape(ROWS, NB)
    master, fm, sm = master.reshape(YR, D), fm.reshape(YR, D), sm.reshape(YR, D)
    fs, ss = fs.reshape(YR, NB), ss.reshape(YR, NB)
    x = lax.axis_index("x").astype(jnp.int32)
    core = lax.axis_index("c").astype(jnp.int32)

    arrived = []
    for shift in (2, 1, 3):
        block = lax.rem(x + shift, NX).reshape(1)
        arrived.append(shift_x(pack(block, gv, gs), shift))
    theirs = sum_half(jnp.stack([x, 1 - core]), gv, gs, arrived)
    from_core = swap(theirs, "c")
    ours = sum_half(jnp.stack([x, core]), gv, gs, arrived)
    chip = ours + from_core
    plane = jnp.sum(lax.all_to_all(chip, "y", 0, 0, tiled=True), axis=0)
    from_z = swap(plane, "zl")
    gradient, low = low_weights(
        core.reshape(1), plane, from_z, master, fm, fs, sm, ss
    )
    low_y = lax.all_to_all(low, "y", 0, 0, tiled=True)
    other_gradient = swap(gradient, "c")
    new = states(core.reshape(1), gradient, other_gradient, master, fm, fs, sm, ss)
    mine = [low_y, shift_x(low_y, 1), shift_x(low_y, 2), shift_x(low_y, 3)]
    other = [swap(piece, "c") for piece in mine]
    weights, transposed = place_all(jnp.stack([x, core]), mine, other)
    om, of, ofs, os, oss = [a[None] for a in new]
    return om, of, ofs, os, oss, weights[None], transposed[None]


def solution(mesh):
    fine = Mesh(
        mesh.devices.reshape(NZ, 2, NX, NY, mesh.devices.shape[-1]),
        ("zl", "c", "x", "y", "zh"),
    )
    grads = P(("zl", "c"), ("x", "y"), "zh", None, None)
    rows = P("zh", ("x", "y"), None)
    shard = P("zh", None, None)
    return jax.shard_map(
        on_device,
        mesh=fine,
        in_specs=(grads, grads, rows, rows, rows, rows, rows),
        out_specs=(rows,) * 5 + (shard, shard),
        check_vma=False,
    )
```

time: 332 us -> 156 us (0.47)
  waiting for transfers between devices: 211 us -> 34.8 us
  local copies, waits for them, and re-layouts: 50.8 us -> 2.77 us
  blocking collectives: 0 us -> 47.4 us
  other arithmetic: 35.3 us -> 0.49 us
  starting transfers between devices: 20 us -> 46.3 us
  Pallas kernels: 0 us -> 22.4 us
  between operations: 14.2 us -> 0.91 us
    all_gather x1 -> x0, waiting for transfers between devices: 89.4 us -> none  [on_device(): weights = lax.all_gather(low_weights, 'group', axis=1, tiled=True)]
    all_to_all x2 -> x0, waiting for transfers between devices: 71 us -> none  [the longest x1 71 us: on_device(): lax.all_to_all(grad_values, 'group', split_axis=3, concat_axis=1, tiled=T...]
    psum x1 -> x0, waiting for transfers between devices: 50.4 us -> none  [on_device(): gradient = lax.psum(partial_sum, 'node')]
    unnamed x22 -> x15, local copies, waits for them, and re-layouts: 50.4 us -> 2.77 us
    all_to_all x0 -> x2, blocking collectives: none -> 47.4 us  [the longest x1 31.5 us: on_device(): plane = jnp.sum(lax.all_to_all(chip, 'y', 0, 0, tiled=True), axis=0)]
    ppermute x0 -> x13, starting transfers between devices: none -> 46.3 us  [the longest x7 24.9 us: swap(): return lax.ppermute(value, axis, [(0, 1), (1, 0)])]
    ppermute x0 -> x13, waiting for transfers between devices: none -> 34.8 us  [the longest x6 31.1 us: shift_x(): return lax.ppermute(value, 'x', [(i, (i + shift) % NX) for i in range(NX)])]
    pallas_call x0 -> x8, Pallas kernels: none -> 22.4 us  [the longest x1 7.81 us: states(): pl.pallas_call(state_kernel, grid_spec=pltpu.PrefetchScalarGridSpec(num_s...]
  transfers between devices with their start and end apart: 4 -> 13, of which waited for: 3 -> 6; matrix products, arithmetic and copies ran while one was open for 11% -> 0% of each run, Pallas kernels for 0% -> 8%
where the time goes in v1:
time: 156 us; the launch traced here: 155 us
  blocking collectives  47.4 us (30%)
  starting transfers between devices  46.3 us (30%)
  waiting for transfers between devices  34.8 us (22%)
  Pallas kernels  22.4 us (14%)
  local copies, waits for them, and re-layouts  2.77 us (2%)
    all_to_all x1, blocking collectives, on_device(): plane = jnp.sum(lax.all_to_all(chip, 'y', 0, 0, tiled=True), axis=0)  31.5 us
    ppermute x6, waiting for transfers between devices, shift_x(): return lax.ppermute(value, 'x', [(i, (i + shift) % NX) for i in range(NX)])  31.1 us
    ppermute x7, starting transfers between devices, swap(): return lax.ppermute(value, axis, [(0, 1), (1, 0)])  24.9 us
    ppermute x6, starting transfers between devices, shift_x(): return lax.ppermute(value, 'x', [(i, (i + shift) % NX) for i in range(NX)])  21.4 us
    all_to_all x1, blocking collectives, on_device(): low_y = lax.all_to_all(low, 'y', 0, 0, tiled=True)  15.9 us
    pallas_call x1, Pallas kernels, states(): pl.pallas_call(state_kernel, grid_spec=pltpu.PrefetchScalarGridSpec(num_s...  7.81 us
    pallas_call x1, Pallas kernels, place_all(): pl.pallas_call(place_kernel, grid_spec=pltpu.PrefetchScalarGridSpec(num_s...  6.53 us
    pallas_call x2, Pallas kernels, sum_half(): pl.pallas_call(sum_kernel, grid_spec=pltpu.PrefetchScalarGridSpec(num_sca...  4.91 us
  transfers between devices with their start and end apart: 13, of which 6 were waited for; matrix products, arithmetic and copies ran while one was open for 0% of the time, Pallas kernels for 8%

profile of v1, /device:TPU:1, one launch (start us, length us, event | category | flops | bytes accessed | tf_op | source)
XLA Modules:
  0.0 155.1 jit_solution(10892991369601562474)
XLA Ops:
  0.6 0.8 copy.14
  1.5 0.0 copy-start
  1.5 1.9 %copy-done = bf16[1,1,1,128,12288]{4,3,2,1,0:T(8,128)(2,1)S(1)} copy-done((bf16[1,1,1,128,12288]{4,3,2,1,0:T(8,128)(2,1)S(1)}, bf16[1,1,1,128,12288]{4,3,2,1,0:T(8,128)(2,1)}, u32[]{:S(2)}) %copy-start) | copy-done | bytes 3145752
  3.4 0.0 copy-start.1
  3.4 0.9 pack_rows.4
  4.3 4.1 %collective-permute-start.1 = (bf16[32,12416]{1,0:T(8,128)(2,1)}, bf16[32,12416]{1,0:T(8,128)(2,1)}, u32[]{:S(2)}, u32[]{:S(2)}) collective-permute-start(bf16[32,12416]{1,0:T(8,128)(2,1)} %pack_rows.4), channel_id=1, source_target_pairs={{0,32},{32,64},{64,96},{96,0},{1,33},{33,65},{65,97},{97,1},{2,34}... | collective-permute-start | bytes 2383880 | tf_op jit(solution)/shard_map/ppermute | solution.py:261
  8.4 0.0 copy-done.1
  8.4 0.9 pack_rows.5
  9.4 3.2 %collective-permute-start.2 = (bf16[32,12416]{1,0:T(8,128)(2,1)}, bf16[32,12416]{1,0:T(8,128)(2,1)}, u32[]{:S(2)}, u32[]{:S(2)}) collective-permute-start(bf16[32,12416]{1,0:T(8,128)(2,1)} %pack_rows.5), channel_id=1, source_target_pairs={{0,96},{32,0},{64,32},{96,64},{1,97},{33,1},{65,33},{97,65},{2,98}... | collective-permute-start | bytes 2383880 | tf_op jit(solution)/shard_map/ppermute | solution.py:261
  12.6 0.9 pack_rows.3
  13.5 3.6 %collective-permute-start = (bf16[32,12416]{1,0:T(8,128)(2,1)}, bf16[32,12416]{1,0:T(8,128)(2,1)S(1)}, u32[]{:S(2)}, u32[]{:S(2)}) collective-permute-start(bf16[32,12416]{1,0:T(8,128)(2,1)} %pack_rows.3), channel_id=1, source_target_pairs={{0,64},{32,96},{64,0},{96,32},{1,65},{33,97},{65,1},{97,33},{2,66}... | collective-permute-start | bytes 2383880 | tf_op jit(solution)/shard_map/ppermute | solution.py:261
  17.1 0.1 pad_add_fusion.1.idx
  17.2 4.3 %collective-permute-done.1.v2.s2 = bf16[32,12416]{1,0:T(8,128)(2,1)} collective-permute-done((bf16[32,12416]{1,0:T(8,128)(2,1)}, bf16[32,12416]{1,0:T(8,128)(2,1)}, u32[]{:S(2)}, u32[]{:S(2)}) %collective-permute-start.1) | collective-permute-done | bytes 794656 | tf_op jit(solution)/shard_map/ppermute | solution.py:261
  21.5 4.4 %collective-permute-done.2.v3.s3 = bf16[32,12416]{1,0:T(8,128)(2,1)} collective-permute-done((bf16[32,12416]{1,0:T(8,128)(2,1)}, bf16[32,12416]{1,0:T(8,128)(2,1)}, u32[]{:S(2)}, u32[]{:S(2)}) %collective-permute-start.2) | collective-permute-done | bytes 794656 | tf_op jit(solution)/shard_map/ppermute | solution.py:261
  25.9 19.3 %collective-permute-done.v1.s1 = bf16[32,12416]{1,0:T(8,128)(2,1)S(1)} collective-permute-done((bf16[32,12416]{1,0:T(8,128)(2,1)}, bf16[32,12416]{1,0:T(8,128)(2,1)S(1)}, u32[]{:S(2)}, u32[]{:S(2)}) %collective-permute-start) | collective-permute-done | bytes 794656 | tf_op jit(solution)/shard_map/ppermute | solution.py:261
  45.2 2.5 %sum_over_x.3 = f32[8,4,6144]{2,1,0:T(4,128)S(1)} custom-call(s32[2]{0:T(128)S(1)} %pad_add_fusion.1.idx, bf16[128,12288]{1,0:T(8,128)(2,1)} %bitcast.20, bf16[128,96]{1,0:T(8,128)(2,1)S(1)} %bitcast.28, bf16[32,12416]{1,0:T(8,128)(2,1)S(1)} %collective-permute-done.v1.s1, bf16[32,12416]{1,0:T(8,128)(2,1)S(1)} %collective-permute-done.v1.s1, ...), custom_call_target="tpu_custom_call" | custom-call | flops 1572864 | bytes 2359296 | tf_op jit(solution)/shard_map/sum_over_x/pallas_call | solution.py:94
  47.6 3.5 %collective-permute-start.3 = (f32[8,4,6144]{2,1,0:T(4,128)S(1)}, f32[8,4,6144]{2,1,0:T(4,128)S(1)}, u32[]{:S(2)}, u32[]{:S(2)}) collective-permute-start(f32[8,4,6144]{2,1,0:T(4,128)S(1)} %sum_over_x.3), channel_id=1, source_target_pairs={{0,128},{128,0},{1,129},{129,1},{2,130},{130,2},{3,131},{131,3},{4... | collective-permute-start | bytes 2359304 | tf_op jit(solution)/shard_map/ppermute | solution.py:265
  51.1 0.1 pad_add_fusion.idx
  51.2 2.5 %sum_over_x.2 = f32[8,4,6144]{2,1,0:T(4,128)S(1)} custom-call(s32[2]{0:T(128)S(1)} %pad_add_fusion.idx, bf16[128,12288]{1,0:T(8,128)(2,1)} %bitcast.21, bf16[128,96]{1,0:T(8,128)(2,1)S(1)} %bitcast.29, bf16[32,12416]{1,0:T(8,128)(2,1)S(1)} %collective-permute-done.v1.s1, bf16[32,12416]{1,0:T(8,128)(2,1)S(1)} %collective-permute-done.v1.s1, ...), custom_call_target="tpu_custom_call" | custom-call | flops 1572864 | bytes 2359296 | tf_op jit(solution)/shard_map/sum_over_x/pallas_call | solution.py:94
  53.6 0.0 copy-start.2
  53.7 0.0 copy-start.3
  53.7 0.0 copy-start.4
  53.7 0.0 copy-start.5
  53.7 0.0 copy-start.6
  53.7 0.0 collective-permute-done.3
  53.7 0.2 add.15
  53.9 31.5 %all_to_all.10 = f32[8,4,6144]{2,1,0:T(4,128)S(1)} all-to-all(f32[8,4,6144]{2,1,0:T(4,128)S(1)} %add.15), channel_id=1, replica_groups=mesh['zl'=2,'c'=2,'x'=4,'y'=8,'zh'=4] {'y'}, dimensions={0} | all-to-all | bytes 1572864 | tf_op jit(solution)/shard_map/all_to_all | solution.py:283
  85.4 0.1 reduce_sum.9.g0
  85.6 4.0 %collective-permute-start.4 = (f32[4,6144]{1,0:T(4,128)S(1)}, f32[4,6144]{1,0:T(4,128)S(1)}, u32[]{:S(2)}, u32[]{:S(2)}) collective-permute-start(f32[4,6144]{1,0:T(4,128)S(1)} %reduce_sum.9.g0), channel_id=1, source_target_pairs={{0,256},{256,0},{1,257},{257,1},{2,258},{258,2},{3,259},{259,3},{4... | collective-permute-start | bytes 294920 | tf_op jit(solution)/shard_map/ppermute | solution.py:265
  89.6 2.7 %collective-permute-done.4.g1 = f32[4,6144]{1,0:T(4,128)S(1)} collective-permute-done((f32[4,6144]{1,0:T(4,128)S(1)}, f32[4,6144]{1,0:T(4,128)S(1)}, u32[]{:S(2)}, u32[]{:S(2)}) %collective-permute-start.4) | collective-permute-done | bytes 98336 | tf_op jit(solution)/shard_map/ppermute | solution.py:265
  92.3 0.0 copy-done.2
  92.3 0.0 copy-done.3
  92.3 0.0 copy-done.4
  92.3 0.0 copy-done.5
  92.3 0.0 copy-done.6
  92.4 0.4 low_weights.1
  92.7 15.9 %all_to_all.11.refs_0_ = bf16[8,4,6144]{2,1,0:T(4,128)(2,1)S(1)} all-to-all(bf16[8,4,6144]{2,1,0:T(4,128)(2,1)S(1)} %get-tuple-element.22), channel_id=1, replica_groups=mesh['zl'=2,'c'=2,'x'=4,'y'=8,'zh'=4] {'y'}, dimensions={0} | all-to-all | bytes 786432 | tf_op jit(solution)/shard_map/all_to_all | solution.py:288
  108.6 4.3 %collective-permute-start.6 = (bf16[8,4,6144]{2,1,0:T(4,128)(2,1)S(1)}, bf16[8,4,6144]{2,1,0:T(4,128)(2,1)S(1)}, u32[]{:S(2)}, u32[]{:S(2)}) collective-permute-start(bf16[8,4,6144]{2,1,0:T(4,128)(2,1)S(1)} %all_to_all.11.refs_0_), channel_id=1, source_target_pairs={{0,32},{32,64},{64,96},{96,0},{1,33},{33,65},{65,97},{97,1},{2,34}... | collective-permute-start | bytes 1179656 | tf_op jit(solution)/shard_map/ppermute | solution.py:261
  112.9 4.0 %collective-permute-start.7 = (bf16[8,4,6144]{2,1,0:T(4,128)(2,1)S(1)}, bf16[8,4,6144]{2,1,0:T(4,128)(2,1)S(1)}, u32[]{:S(2)}, u32[]{:S(2)}) collective-permute-start(bf16[8,4,6144]{2,1,0:T(4,128)(2,1)S(1)} %all_to_all.11.refs_0_), channel_id=1, source_target_pairs={{0,64},{32,96},{64,0},{96,32},{1,65},{33,97},{65,1},{97,33},{2,66}... | collective-permute-start | bytes 1179656 | tf_op jit(solution)/shard_map/ppermute | solution.py:261
  117.0 2.2 %collective-permute-start.8 = (bf16[8,4,6144]{2,1,0:T(4,128)(2,1)S(1)}, bf16[8,4,6144]{2,1,0:T(4,128)(2,1)S(1)}, u32[]{:S(2)}, u32[]{:S(2)}) collective-permute-start(bf16[8,4,6144]{2,1,0:T(4,128)(2,1)S(1)} %all_to_all.11.refs_0_), channel_id=1, source_target_pairs={{0,96},{32,0},{64,32},{96,64},{1,97},{33,1},{65,33},{97,65},{2,98}... | collective-permute-start | bytes 1179656 | tf_op jit(solution)/shard_map/ppermute | solution.py:261
  119.2 4.6 %collective-permute-start.9 = (bf16[8,4,6144]{2,1,0:T(4,128)(2,1)S(1)}, bf16[8,4,6144]{2,1,0:T(4,128)(2,1)S(1)}, u32[]{:S(2)}, u32[]{:S(2)}) collective-permute-start(bf16[8,4,6144]{2,1,0:T(4,128)(2,1)S(1)} %all_to_all.11.refs_0_), channel_id=1, source_target_pairs={{0,128},{128,0},{1,129},{129,1},{2,130},{130,2},{3,131},{131,3},{4... | collective-permute-start | bytes 1179656 | tf_op jit(solution)/shard_map/ppermute | solution.py:265
  123.8 0.0 collective-permute-done.6.refs_1_
  123.8 3.5 %collective-permute-start.10 = (bf16[8,4,6144]{2,1,0:T(4,128)(2,1)S(1)}, bf16[8,4,6144]{2,1,0:T(4,128)(2,1)S(1)}, u32[]{:S(2)}, u32[]{:S(2)}) collective-permute-start(bf16[8,4,6144]{2,1,0:T(4,128)(2,1)S(1)} %collective-permute-done.6.refs_1_), channel_id=1, source_target_pairs={{0,128},{128,0},{1,129},{129,1},{2,130},{130,2},{3,131},{131,3},{4... | collective-permute-start | bytes 1179656 | tf_op jit(solution)/shard_map/ppermute | solution.py:265
  127.3 3.1 %collective-permute-done.7.refs_2_ = bf16[8,4,6144]{2,1,0:T(4,128)(2,1)S(1)} collective-permute-done((bf16[8,4,6144]{2,1,0:T(4,128)(2,1)S(1)}, bf16[8,4,6144]{2,1,0:T(4,128)(2,1)S(1)}, u32[]{:S(2)}, u32[]{:S(2)}) %collective-permute-start.7) | collective-permute-done | bytes 393248 | tf_op jit(solution)/shard_map/ppermute | solution.py:261
  130.4 5.0 %collective-permute-start.11 = (bf16[8,4,6144]{2,1,0:T(4,128)(2,1)S(1)}, bf16[8,4,6144]{2,1,0:T(4,128)(2,1)S(1)}, u32[]{:S(2)}, u32[]{:S(2)}) collective-permute-start(bf16[8,4,6144]{2,1,0:T(4,128)(2,1)S(1)} %collective-permute-done.7.refs_2_), channel_id=1, source_target_pairs={{0,128},{128,0},{1,129},{129,1},{2,130},{130,2},{3,131},{131,3},{4... | collective-permute-start | bytes 1179656 | tf_op jit(solution)/shard_map/ppermute | solution.py:265
  135.4 0.0 collective-permute-done.8.refs_3_
  135.4 1.9 %collective-permute-start.12 = (bf16[8,4,6144]{2,1,0:T(4,128)(2,1)S(1)}, bf16[8,4,6144]{2,1,0:T(4,128)(2,1)S(1)}, u32[]{:S(2)}, u32[]{:S(2)}) collective-permute-start(bf16[8,4,6144]{2,1,0:T(4,128)(2,1)S(1)} %collective-permute-done.8.refs_3_), channel_id=1, source_target_pairs={{0,128},{128,0},{1,129},{129,1},{2,130},{130,2},{3,131},{131,3},{4... | collective-permute-start | bytes 1179656 | tf_op jit(solution)/shard_map/ppermute | solution.py:265
  137.4 2.4 %collective-permute-start.5 = (f32[4,6144]{1,0:T(4,128)S(1)}, f32[4,6144]{1,0:T(4,128)S(1)}, u32[]{:S(2)}, u32[]{:S(2)}) collective-permute-start(f32[4,6144]{1,0:T(4,128)S(1)} %get-tuple-element.16.mine), channel_id=1, source_target_pairs={{0,128},{128,0},{1,129},{129,1},{2,130},{130,2},{3,131},{131,3},{4... | collective-permute-start | bytes 294920 | tf_op jit(solution)/shard_map/ppermute | solution.py:265
  139.8 0.9 collective-permute-done.5.other
  140.7 7.8 %new_states.1 = (f32[4,12288]{1,0:T(4,128)}, bf16[4,12288]{1,0:T(4,128)(2,1)}, f32[4,96]{1,0:T(4,128)}, bf16[4,12288]{1,0:T(4,128)(2,1)}, f32[4,96]{1,0:T(4,128)}) custom-call(s32[1]{0:T(128)} %bitcast.idx, f32[4,6144]{1,0:T(4,128)S(1)} %get-tuple-element.16.mine, f32[4,6144]{1,0:T(4,128)S(1)} %collective-permute-done.5.other, f32[4,12288]{1,0:T(4,128)S(1)} %bitcast.31, ...), custom_call_target="tpu_custom_call" | custom-call | flops 2949120 | bytes 983040 | tf_op jit(solution)/shard_map/new_states/pallas_call | solution.py:185
  148.5 0.0 collective-permute-done.9.refs_4_
  148.5 0.0 collective-permute-done.10.refs_5_
  148.5 0.0 collective-permute-done.11.refs_6_
  148.5 0.0 collective-permute-done.12.refs_7_
  148.5 6.5 %place_weights.1 = (bf16[128,12288]{1,0:T(8,128)(2,1)}, bf16[12288,128]{1,0:T(8,128)(2,1)}) custom-call(s32[2]{0:T(128)S(1)} %pad_add_fusion.idx, bf16[8,4,6144]{2,1,0:T(4,128)(2,1)S(1)} %all_to_all.11.refs_0_, bf16[8,4,6144]{2,1,0:T(4,128)(2,1)S(1)} %collective-permute-done.6.refs_1_, bf16[8,4,6144]{2,1,0:T(4,128)(2,1)S(1)} %collective-permute-done.7.refs_2_, ...), custom_call_target="tpu_custom_call" | custom-call | bytes 9437184 | tf_op jit(solution)/shard_map/place_weights/pallas_call | solution.py:238
Async XLA Ops:
  1.5 1.9 %copy-start = (bf16[1,1,1,128,12288]{4,3,2,1,0:T(8,128)(2,1)S(1)}, bf16[1,1,1,128,12288]{4,3,2,1,0:T(8,128)(2,1)}, u32[]{:S(2)}) copy-start(bf16[1,1,1,128,12288]{4,3,2,1,0:T(8,128)(2,1)} %param.7) | copy-start | bytes 9437188
  3.4 5.0 %copy-start.1 = (bf16[1,1,1,128,12288]{4,3,2,1,0:T(8,128)(2,1)S(1)}, bf16[1,1,1,128,12288]{4,3,2,1,0:T(8,128)(2,1)}, u32[]{:S(2)}) copy-start(bf16[1,1,1,128,12288]{4,3,2,1,0:T(8,128)(2,1)} %param.7) | copy-start | bytes 9437188
  4.3 17.2 %collective-permute-start.1 = (bf16[32,12416]{1,0:T(8,128)(2,1)}, bf16[32,12416]{1,0:T(8,128)(2,1)}, u32[]{:S(2)}, u32[]{:S(2)}) collective-permute-start(bf16[32,12416]{1,0:T(8,128)(2,1)} %pack_rows.4), channel_id=1, source_target_pairs={{0,32},{32,64},{64,96},{96,0},{1,33},{33,65},{65,97},{97,1},{2,34}... | collective-permute-start | bytes 2383880 | tf_op jit(solution)/shard_map/ppermute | solution.py:261
  9.4 16.6 %collective-permute-start.2 = (bf16[32,12416]{1,0:T(8,128)(2,1)}, bf16[32,12416]{1,0:T(8,128)(2,1)}, u32[]{:S(2)}, u32[]{:S(2)}) collective-permute-start(bf16[32,12416]{1,0:T(8,128)(2,1)} %pack_rows.5), channel_id=1, source_target_pairs={{0,96},{32,0},{64,32},{96,64},{1,97},{33,1},{65,33},{97,65},{2,98}... | collective-permute-start | bytes 2383880 | tf_op jit(solution)/shard_map/ppermute | solution.py:261
  13.5 31.7 %collective-permute-start = (bf16[32,12416]{1,0:T(8,128)(2,1)}, bf16[32,12416]{1,0:T(8,128)(2,1)S(1)}, u32[]{:S(2)}, u32[]{:S(2)}) collective-permute-start(bf16[32,12416]{1,0:T(8,128)(2,1)} %pack_rows.3), channel_id=1, source_target_pairs={{0,64},{32,96},{64,0},{96,32},{1,65},{33,97},{65,1},{97,33},{2,66}... | collective-permute-start | bytes 2383880 | tf_op jit(solution)/shard_map/ppermute | solution.py:261
  47.6 6.1 %collective-permute-start.3 = (f32[8,4,6144]{2,1,0:T(4,128)S(1)}, f32[8,4,6144]{2,1,0:T(4,128)S(1)}, u32[]{:S(2)}, u32[]{:S(2)}) collective-permute-start(f32[8,4,6144]{2,1,0:T(4,128)S(1)} %sum_over_x.3), channel_id=1, source_target_pairs={{0,128},{128,0},{1,129},{129,1},{2,130},{130,2},{3,131},{131,3},{4... | collective-permute-start | bytes 2359304 | tf_op jit(solution)/shard_map/ppermute | solution.py:265
  53.6 38.7 %copy-start.2 = (f32[1,4,12288]{2,1,0:T(4,128)S(1)}, f32[1,4,12288]{2,1,0:T(4,128)}, u32[]{:S(2)}) copy-start(f32[1,4,12288]{2,1,0:T(4,128)} %param.9) | copy-start | bytes 589828
  53.7 38.7 %copy-start.3 = (bf16[1,4,12288]{2,1,0:T(4,128)(2,1)S(1)}, bf16[1,4,12288]{2,1,0:T(4,128)(2,1)}, u32[]{:S(2)}) copy-start(bf16[1,4,12288]{2,1,0:T(4,128)(2,1)} %param.10) | copy-start | bytes 294916
  53.7 38.7 %copy-start.4 = (bf16[1,4,12288]{2,1,0:T(4,128)(2,1)S(1)}, bf16[1,4,12288]{2,1,0:T(4,128)(2,1)}, u32[]{:S(2)}) copy-start(bf16[1,4,12288]{2,1,0:T(4,128)(2,1)} %param.12) | copy-start | bytes 294916
  53.7 38.7 %copy-start.5 = (f32[1,4,96]{2,1,0:T(4,128)S(1)}, f32[1,4,96]{2,1,0:T(4,128)}, u32[]{:S(2)}) copy-start(f32[1,4,96]{2,1,0:T(4,128)} %param.11) | copy-start | bytes 4612
  53.7 38.6 %copy-start.6 = (f32[1,4,96]{2,1,0:T(4,128)S(1)}, f32[1,4,96]{2,1,0:T(4,128)}, u32[]{:S(2)}) copy-start(f32[1,4,96]{2,1,0:T(4,128)} %param.13) | copy-start | bytes 4612
  85.6 6.7 %collective-permute-start.4 = (f32[4,6144]{1,0:T(4,128)S(1)}, f32[4,6144]{1,0:T(4,128)S(1)}, u32[]{:S(2)}, u32[]{:S(2)}) collective-permute-start(f32[4,6144]{1,0:T(4,128)S(1)} %reduce_sum.9.g0), channel_id=1, source_target_pairs={{0,256},{256,0},{1,257},{257,1},{2,258},{258,2},{3,259},{259,3},{4... | collective-permute-start | bytes 294920 | tf_op jit(solution)/shard_map/ppermute | solution.py:265
  108.6 15.2 %collective-permute-start.6 = (bf16[8,4,6144]{2,1,0:T(4,128)(2,1)S(1)}, bf16[8,4,6144]{2,1,0:T(4,128)(2,1)S(1)}, u32[]{:S(2)}, u32[]{:S(2)}) collective-permute-start(bf16[8,4,6144]{2,1,0:T(4,128)(2,1)S(1)} %all_to_all.11.refs_0_), channel_id=1, source_target_pairs={{0,32},{32,64},{64,96},{96,0},{1,33},{33,65},{65,97},{97,1},{2,34}... | collective-permute-start | bytes 1179656 | tf_op jit(solution)/shard_map/ppermute | solution.py:261
  112.9 17.5 %collective-permute-start.7 = (bf16[8,4,6144]{2,1,0:T(4,128)(2,1)S(1)}, bf16[8,4,6144]{2,1,0:T(4,128)(2,1)S(1)}, u32[]{:S(2)}, u32[]{:S(2)}) collective-permute-start(bf16[8,4,6144]{2,1,0:T(4,128)(2,1)S(1)} %all_to_all.11.refs_0_), channel_id=1, source_target_pairs={{0,64},{32,96},{64,0},{96,32},{1,65},{33,97},{65,1},{97,33},{2,66}... | collective-permute-start | bytes 1179656 | tf_op jit(solution)/shard_map/ppermute | solution.py:261
  117.0 18.5 %collective-permute-start.8 = (bf16[8,4,6144]{2,1,0:T(4,128)(2,1)S(1)}, bf16[8,4,6144]{2,1,0:T(4,128)(2,1)S(1)}, u32[]{:S(2)}, u32[]{:S(2)}) collective-permute-start(bf16[8,4,6144]{2,1,0:T(4,128)(2,1)S(1)} %all_to_all.11.refs_0_), channel_id=1, source_target_pairs={{0,96},{32,0},{64,32},{96,64},{1,97},{33,1},{65,33},{97,65},{2,98}... | collective-permute-start | bytes 1179656 | tf_op jit(solution)/shard_map/ppermute | solution.py:261
  119.2 29.4 %collective-permute-start.9 = (bf16[8,4,6144]{2,1,0:T(4,128)(2,1)S(1)}, bf16[8,4,6144]{2,1,0:T(4,128)(2,1)S(1)}, u32[]{:S(2)}, u32[]{:S(2)}) collective-permute-start(bf16[8,4,6144]{2,1,0:T(4,128)(2,1)S(1)} %all_to_all.11.refs_0_), channel_id=1, source_target_pairs={{0,128},{128,0},{1,129},{129,1},{2,130},{130,2},{3,131},{131,3},{4... | collective-permute-start | bytes 1179656 | tf_op jit(solution)/shard_map/ppermute | solution.py:265
  123.8 24.7 %collective-permute-start.10 = (bf16[8,4,6144]{2,1,0:T(4,128)(2,1)S(1)}, bf16[8,4,6144]{2,1,0:T(4,128)(2,1)S(1)}, u32[]{:S(2)}, u32[]{:S(2)}) collective-permute-start(bf16[8,4,6144]{2,1,0:T(4,128)(2,1)S(1)} %collective-permute-done.6.refs_1_), channel_id=1, source_target_pairs={{0,128},{128,0},{1,129},{129,1},{2,130},{130,2},{3,131},{131,3},{4... | collective-permute-start | bytes 1179656 | tf_op jit(solution)/shard_map/ppermute | solution.py:265
  130.4 18.1 %collective-permute-start.11 = (bf16[8,4,6144]{2,1,0:T(4,128)(2,1)S(1)}, bf16[8,4,6144]{2,1,0:T(4,128)(2,1)S(1)}, u32[]{:S(2)}, u32[]{:S(2)}) collective-permute-start(bf16[8,4,6144]{2,1,0:T(4,128)(2,1)S(1)} %collective-permute-done.7.refs_2_), channel_id=1, source_target_pairs={{0,128},{128,0},{1,129},{129,1},{2,130},{130,2},{3,131},{131,3},{4... | collective-permute-start | bytes 1179656 | tf_op jit(solution)/shard_map/ppermute | solution.py:265
  135.4 13.1 %collective-permute-start.12 = (bf16[8,4,6144]{2,1,0:T(4,128)(2,1)S(1)}, bf16[8,4,6144]{2,1,0:T(4,128)(2,1)S(1)}, u32[]{:S(2)}, u32[]{:S(2)}) collective-permute-start(bf16[8,4,6144]{2,1,0:T(4,128)(2,1)S(1)} %collective-permute-done.8.refs_3_), channel_id=1, source_target_pairs={{0,128},{128,0},{1,129},{129,1},{2,130},{130,2},{3,131},{131,3},{4... | collective-permute-start | bytes 1179656 | tf_op jit(solution)/shard_map/ppermute | solution.py:265
  137.4 3.3 %collective-permute-start.5 = (f32[4,6144]{1,0:T(4,128)S(1)}, f32[4,6144]{1,0:T(4,128)S(1)}, u32[]{:S(2)}, u32[]{:S(2)}) collective-permute-start(f32[4,6144]{1,0:T(4,128)S(1)} %get-tuple-element.16.mine), channel_id=1, source_target_pairs={{0,128},{128,0},{1,129},{129,1},{2,130},{130,2},{3,131},{131,3},{4... | collective-permute-start | bytes 294920 | tf_op jit(solution)/shard_map/ppermute | solution.py:265

commit v2 on v1

--- a/solution.py
+++ b/solution.py
@@ -16,8 +16,10 @@
 NX, NY, NZ = 4, 8, 2
 XR = ROWS // NX
 YR = XR // NY
-PAD = D + BLOCK
-CH = 1024
+PAD = HALF + BLOCK
+SPAN = 172.0
+OFFSET = 86.0
+CH = 3072
 
 beta_one = 0.9
 beta_two = 0.95
@@ -39,71 +41,171 @@
     return pl.CostEstimate(flops=flops, bytes_accessed=nbytes, transcendentals=0)
 
 
+def encode(value, factor):
+    size = jnp.exp(jnp.abs(value) * factor - OFFSET)
+    return jnp.where(value < 0, -size, size)
+
+
+def decode(code, step):
+    size = (jnp.log(jnp.abs(code)) + OFFSET) * step
+    return jnp.where(code < 0, -size, size)
+
+
+def scale_of(peak):
+    return jnp.maximum(peak * (1.0 + 2.0**-7), 1e-30).astype(bf16)
+
+
+def half_of(scales, first_half):
+    return jnp.where(first_half, scales[:, :HB], scales[:, HB:NB])
+
+
 def pack_kernel(idx, values, scales, out):
-    out[:, :D] = values[...]
-    out[:, D : D + NB] = scales[...]
-    out[:, D + NB :] = jnp.zeros((XR, PAD - D - NB), bf16)
-
-
-def pack(block, values, scales):
+    out[:, :HALF] = values[...]
+    both = scales[...].astype(f32)
+    chosen = half_of(both, idx[0] == 0).astype(bf16)
+    out[:, HALF : HALF + HB] = chosen
+    out[:, HALF + HB :] = jnp.zeros((XR, BLOCK - HB), bf16)
+
+
+def pack(half, values, scales):
     return pl.pallas_call(
         pack_kernel,
+        grid_spec=pltpu.PrefetchScalarGridSpec(
+            num_scalar_prefetch=1,
+            grid=(NX,),
+            in_specs=[
+                pl.BlockSpec((XR, HALF), lambda i, s: (i, s[0])),
+                pl.BlockSpec((XR, NB), lambda i, s: (i, 0)),
+            ],
+            out_specs=pl.BlockSpec((XR, PAD), lambda i, s: (i, 0)),
+        ),
+        out_shape=jax.ShapeDtypeStruct((ROWS, PAD), bf16),
+        compiler_params=params(62),
+        cost_estimate=cost(0, 2 * ROWS * HALF * 2),
+        name="pack_rows",
+    )(half, values, scales)
+
+
+def chip_kernel(idx, values, scales, there, there_scales, out, totals):
+    mine = half_of(scales[...].astype(f32), idx[1] == 0)
+    theirs = there_scales[...].astype(f32)
+    peak = jnp.zeros((XR, BLOCK), f32)
+    for b in range(HB):
+        cols = slice(b * BLOCK, (b + 1) * BLOCK)
+        total = values[:, cols].astype(f32) * mine[:, b : b + 1]
+        total = total + there[:, cols].astype(f32) * theirs[:, b : b + 1]
+        totals[:, cols] = total
+        peak = jnp.maximum(peak, jnp.abs(total))
+    scale = scale_of(peak)
+    out[:, HALF:] = scale
+    factor = SPAN / scale.astype(f32)
+    for b in range(HB):
+        cols = slice(b * BLOCK, (b + 1) * BLOCK)
+        out[:, cols] = encode(totals[:, cols], factor).astype(bf16)
+
+
+def chip_sum(idx, values, scales, there):
+    return pl.pallas_call(
+        chip_kernel,
         grid_spec=pltpu.PrefetchScalarGridSpec(
             num_scalar_prefetch=1,
             grid=(1,),
             in_specs=[
-                pl.BlockSpec((XR, D), lambda i, s: (s[0], 0)),
+                pl.BlockSpec((XR, HALF), lambda i, s: (s[0], s[1])),
                 pl.BlockSpec((XR, NB), lambda i, s: (s[0], 0)),
+                pl.BlockSpec((XR, HALF), lambda i, s: (s[0], 0)),
+                pl.BlockSpec((XR, BLOCK), lambda i, s: (s[0], HB)),
             ],
             out_specs=pl.BlockSpec((XR, PAD), lambda i, s: (0, 0)),
+            scratch_shapes=[pltpu.VMEM((XR, HALF), f32)],
         ),
         out_shape=jax.ShapeDtypeStruct((XR, PAD), bf16),
         compiler_params=params(),
-        cost_estimate=cost(0, 2 * XR * D * 2),
-        name="pack_rows",
-    )(block, values, scales)
-
-
-def sum_kernel(idx, v0, s0, v1, s1, v2, s2, v3, s3, out):
-    first_half = idx[1] == 0
-    scales = []
-    for ref in (s0, s1, s2, s3):
-        both = ref[...].astype(f32)
-        scales.append(jnp.where(first_half, both[:, :HB], both[:, HB:NB]))
-    for b in range(HB):
-        cols = slice(b * BLOCK, (b + 1) * BLOCK)
-        total = None
-        for ref, scale in zip((v0, v1, v2, v3), scales):
-            term = ref[:, cols].astype(f32) * scale[:, b : b + 1]
-            total = term if total is None else total + term
-        for i in range(NY):
-            out[i, :, cols] = total[i * YR : (i + 1) * YR, :]
-
-
-def sum_half(idx, values, scales, arrived):
-    value_spec = pl.BlockSpec((XR, HALF), lambda i, s: (0, s[1]))
-    scale_spec = pl.BlockSpec((XR, BLOCK), lambda i, s: (0, NB))
+        cost_estimate=cost(20 * XR * HALF, 6 * XR * HALF),
+        name="sum_on_chip",
+    )(idx, values, scales, there, there)
+
+
+def row_kernel(
+    idx, values, scales, there, there_scales, c1, s1, c2, s2, c3, s3, out, totals
+):
+    mine = half_of(scales[...].astype(f32), idx[1] == 0)
+    theirs = there_scales[...].astype(f32)
+    coded = [
+        (ref, scale[...].astype(f32) * (1.0 / SPAN))
+        for ref, scale in ((c1, s1), (c2, s2), (c3, s3))
+    ]
+    peak = jnp.zeros((XR, BLOCK), f32)
+    for b in range(HB):
+        cols = slice(b * BLOCK, (b + 1) * BLOCK)
+        total = values[:, cols].astype(f32) * mine[:, b : b + 1]
+        total = total + there[:, cols].astype(f32) * theirs[:, b : b + 1]
+        for ref, step in coded:
+            total = total + decode(ref[:, cols].astype(f32), step)
+        totals[:, cols] = total
+        peak = jnp.maximum(peak, jnp.abs(total))
+    scale = scale_of(peak).astype(f32)
+    out[:, :, HALF:] = scale.reshape(NY, YR, BLOCK).astype(bf16)
+    factor = SPAN / scale
+    for b in range(HB):
+        cols = slice(b * BLOCK, (b + 1) * BLOCK)
+        code = encode(totals[:, cols], factor)
+        out[:, :, cols] = code.reshape(NY, YR, BLOCK).astype(bf16)
+
+
+def row_sum(idx, values, scales, there, arrived):
     ins = [
         pl.BlockSpec((XR, HALF), lambda i, s: (s[0], s[1])),
         pl.BlockSpec((XR, NB), lambda i, s: (s[0], 0)),
+        pl.BlockSpec((XR, HALF), lambda i, s: (s[0], 0)),
+        pl.BlockSpec((XR, BLOCK), lambda i, s: (s[0], HB)),
     ]
-    args = [values, scales]
+    args = [values, scales, there, there]
     for a in arrived:
-        ins += [value_spec, scale_spec]
+        ins += [
+            pl.BlockSpec((XR, HALF), lambda i, s: (0, 0)),
+            pl.BlockSpec((XR, BLOCK), lambda i, s: (0, HB)),
+        ]
         args += [a, a]
     return pl.pallas_call(
-        sum_kernel,
+        row_kernel,
         grid_spec=pltpu.PrefetchScalarGridSpec(
             num_scalar_prefetch=1,
             grid=(1,),
             in_specs=ins,
-            out_specs=pl.BlockSpec((NY, YR, HALF), lambda i, s: (0, 0, 0)),
-        ),
-        out_shape=jax.ShapeDtypeStruct((NY, YR, HALF), f32),
-        compiler_params=params(),
-        cost_estimate=cost(8 * XR * HALF, 12 * XR * HALF),
+            out_specs=pl.BlockSpec((NY, YR, PAD), lambda i, s: (0, 0, 0)),
+            scratch_shapes=[pltpu.VMEM((XR, HALF), f32)],
+        ),
+        out_shape=jax.ShapeDtypeStruct((NY, YR, PAD), bf16),
+        compiler_params=params(),
+        cost_estimate=cost(60 * XR * HALF, 12 * XR * HALF),
         name="sum_over_x",
     )(idx, *args)
+
+
+def plane_kernel(codes, scales, out):
+    step = scales[...].astype(f32).reshape(XR, BLOCK) * (1.0 / SPAN)
+    for b in range(HB):
+        cols = slice(b * BLOCK, (b + 1) * BLOCK)
+        code = codes[:, :, cols].astype(f32).reshape(XR, BLOCK)
+        term = decode(code, step)
+        out[:, cols] = jnp.sum(term.reshape(NY, YR, BLOCK), axis=0)
+
+
+def plane_sum(codes):
+    return pl.pallas_call(
+        plane_kernel,
+        grid=(1,),
+        in_specs=[
+            pl.BlockSpec((NY, YR, HALF), lambda i: (0, 0, 0)),
+            pl.BlockSpec((NY, YR, BLOCK), lambda i: (0, 0, HB)),
+        ],
+        out_specs=pl.BlockSpec((YR, HALF), lambda i: (0, 0)),
+        out_shape=jax.ShapeDtypeStruct((YR, HALF), f32),
+        compiler_params=params(),
+        cost_estimate=cost(20 * XR * HALF, 3 * XR * HALF),
+        name="sum_over_y",
+    )(codes, codes)
 
 
 def adam(gradient, master, first_old, second_old):
@@ -210,7 +312,7 @@
     def place(group):
         for shift, ref in enumerate(group):
             start = pl.multiple_of(lax.rem(x + NX - shift, NX) * XR, XR)
-            rows[pl.ds(start, XR), :] = ref[...].astype(f32).reshape(XR, CH)
+            rows[pl.ds(start, XR), :] = ref[...].astype(f32).reshape(XR, CH).astype(bf16)
 
     @pl.when(pl.program_id(0) == 0)
     def _():
@@ -221,8 +323,8 @@
         place(pieces[4:])
 
     low = rows[...]
-    weights[...] = low.astype(bf16)
-    transposed[...] = low.T.astype(bf16)
+    weights[...] = low
+    transposed[...] = low.T
 
 
 def place_all(idx, mine, other):
@@ -245,7 +347,7 @@
                 pl.BlockSpec((ROWS, CH), lambda h, j, s: (0, column(h, j, s))),
                 pl.BlockSpec((CH, ROWS), lambda h, j, s: (column(h, j, s), 0)),
             ],
-            scratch_shapes=[pltpu.VMEM((ROWS, CH), f32)],
+            scratch_shapes=[pltpu.VMEM((ROWS, CH), bf16)],
         ),
         out_shape=[
             jax.ShapeDtypeStruct((ROWS, D), bf16),
@@ -272,23 +374,22 @@
     x = lax.axis_index("x").astype(jnp.int32)
     core = lax.axis_index("c").astype(jnp.int32)
 
+    there = swap(pack(1 - core.reshape(1), gv, gs), "c")
     arrived = []
     for shift in (2, 1, 3):
-        block = lax.rem(x + shift, NX).reshape(1)
-        arrived.append(shift_x(pack(block, gv, gs), shift))
-    theirs = sum_half(jnp.stack([x, 1 - core]), gv, gs, arrived)
-    from_core = swap(theirs, "c")
-    ours = sum_half(jnp.stack([x, core]), gv, gs, arrived)
-    chip = ours + from_core
-    plane = jnp.sum(lax.all_to_all(chip, "y", 0, 0, tiled=True), axis=0)
+        target = jnp.stack([lax.rem(x + shift, NX), core])
+        arrived.append(shift_x(chip_sum(target, gv, gs, there), shift))
+    codes = row_sum(jnp.stack([x, core]), gv, gs, there, arrived)
+    plane = plane_sum(lax.all_to_all(codes, "y", 0, 0, tiled=True))
     from_z = swap(plane, "zl")
     gradient, low = low_weights(
         core.reshape(1), plane, from_z, master, fm, fs, sm, ss
     )
     low_y = lax.all_to_all(low, "y", 0, 0, tiled=True)
+    mine = [low_y, shift_x(low_y, 1), shift_x(low_y, 2), shift_x(low_y, 3)]
     other_gradient = swap(gradient, "c")
     new = states(core.reshape(1), gradient, other_gradient, master, fm, fs, sm, ss)
-    mine = [low_y, shift_x(low_y, 1), shift_x(low_y, 2), shift_x(low_y, 3)]
+    mine[1], new = lax.optimization_barrier((mine[1], new))
     other = [swap(piece, "c") for piece in mine]
     weights, transposed = place_all(jnp.stack([x, core]), mine, other)
     om, of, ofs, os, oss = [a[None] for a in new]

time: 156 us -> 124 us (0.79)
  blocking collectives: 47.4 us -> 30.8 us
  waiting for transfers between devices: 34.8 us -> 21.2 us
  starting transfers between devices: 46.3 us -> 43.3 us
    ppermute x6, waiting for transfers between devices: 31.1 us -> 12.2 us  [shift_x(): return lax.ppermute(value, 'x', [(i, (i + shift) % NX) for i in range(NX)])]
    all_to_all x1, blocking collectives: 31.5 us -> 16.9 us  [on_device(): plane = plane_sum(lax.all_to_all(codes, 'y', 0, 0, tiled=True))]
    ppermute x7, waiting for transfers between devices: 3.68 us -> 8.91 us  [swap(): return lax.ppermute(value, axis, [(0, 1), (1, 0)])]
    ppermute x6, starting transfers between devices: 21.4 us -> 16.9 us  [shift_x(): return lax.ppermute(value, 'x', [(i, (i + shift) % NX) for i in range(NX)])]
    pallas_call x2 -> x5, Pallas kernels: 4.91 us -> 7.33 us  [the longest x3 3.67 us: chip_sum(): pl.pallas_call(chip_kernel, grid_spec=pltpu.PrefetchScalarGridSpec(num_sc...]
    pallas_call x1, Pallas kernels: 6.53 us -> 4.24 us  [place_all(): pl.pallas_call(place_kernel, grid_spec=pltpu.PrefetchScalarGridSpec(num_s...]
    all_to_all x1, blocking collectives: 15.9 us -> 13.9 us  [on_device(): low_y = lax.all_to_all(low, 'y', 0, 0, tiled=True)]
    pallas_call x3 -> x1, Pallas kernels: 2.82 us -> 3.68 us  [pack(): pl.pallas_call(pack_kernel, grid_spec=pltpu.PrefetchScalarGridSpec(num_sc...]
where the time goes in v2:
time: 124 us; the launch traced here: 123 us
  starting transfers between devices  43.3 us (35%)
  blocking collectives  30.8 us (25%)
  Pallas kernels  23.4 us (19%)
  waiting for transfers between devices  21.2 us (17%)
  local copies, waits for them, and re-layouts  3.37 us (3%)
    ppermute x7, starting transfers between devices, swap(): return lax.ppermute(value, axis, [(0, 1), (1, 0)])  26.5 us
    all_to_all x1, blocking collectives, on_device(): plane = plane_sum(lax.all_to_all(codes, 'y', 0, 0, tiled=True))  16.9 us
    ppermute x6, starting transfers between devices, shift_x(): return lax.ppermute(value, 'x', [(i, (i + shift) % NX) for i in range(NX)])  16.9 us
    all_to_all x1, blocking collectives, on_device(): low_y = lax.all_to_all(low, 'y', 0, 0, tiled=True)  13.9 us
    ppermute x6, waiting for transfers between devices, shift_x(): return lax.ppermute(value, 'x', [(i, (i + shift) % NX) for i in range(NX)])  12.2 us
    ppermute x7, waiting for transfers between devices, swap(): return lax.ppermute(value, axis, [(0, 1), (1, 0)])  8.91 us
    pallas_call x1, Pallas kernels, states(): pl.pallas_call(state_kernel, grid_spec=pltpu.PrefetchScalarGridSpec(num_s...  7.81 us
    pallas_call x1, Pallas kernels, place_all(): pl.pallas_call(place_kernel, grid_spec=pltpu.PrefetchScalarGridSpec(num_s...  4.24 us
  transfers between devices with their start and end apart: 13, of which 6 were waited for; matrix products, arithmetic and copies ran while one was open for 0% of the time, Pallas kernels for 8%

profile of v2, /device:TPU:1, one launch (start us, length us, event | category | flops | bytes accessed | tf_op | source)
XLA Modules:
  0.0 123.3 jit_solution(16784450533939486901)
XLA Ops:
  0.6 1.5 %copy.14 = bf16[1,1,1,128,96]{4,3,2,1,0:T(8,128)(2,1)} copy(bf16[1,1,1,128,96]{3,4,2,1,0:T(8,128)(2,1)} %param.8) | data formatting | bytes 49152 | tf_op args[1]
  2.1 0.0 copy-start.1
  2.1 3.7 %pack_rows.1 = bf16[128,6272]{1,0:T(8,128)(2,1)} custom-call(s32[1]{0:T(128)S(6)} %sub.3.idx, bf16[128,12288]{1,0:T(8,128)(2,1)} %bitcast.19, bf16[128,96]{1,0:T(8,128)(2,1)} %bitcast.24), custom_call_target="tpu_custom_call" | custom-call | bytes 3145728 | tf_op jit(solution)/shard_map/pack_rows/pallas_call | solution.py:71
  5.8 8.8 %collective-permute-start = (bf16[128,6272]{1,0:T(8,128)(2,1)}, bf16[128,6272]{1,0:T(8,128)(2,1)S(1)}, u32[]{:S(2)}, u32[]{:S(2)}) collective-permute-start(bf16[128,6272]{1,0:T(8,128)(2,1)} %pack_rows.1), channel_id=1, source_target_pairs={{0,128},{128,0},{1,129},{129,1},{2,130},{130,2},{3,131},{131,3},{4... | collective-permute-start | bytes 4816904 | tf_op jit(solution)/shard_map/ppermute | solution.py:367
  14.6 0.1 pad_add_fusion.1.idx
  14.6 0.1 pad_add_fusion.2.idx
  14.7 0.1 pad_add_fusion.3.idx
  14.8 3.0 %collective-permute-done.there.there_scales = bf16[128,6272]{1,0:T(8,128)(2,1)S(1)} collective-permute-done((bf16[128,6272]{1,0:T(8,128)(2,1)}, bf16[128,6272]{1,0:T(8,128)(2,1)S(1)}, u32[]{:S(2)}, u32[]{:S(2)}) %collective-permute-start) | collective-permute-done | bytes 1605664 | tf_op jit(solution)/shard_map/ppermute | solution.py:367
  17.8 0.0 copy-done.1
  17.8 0.0 copy-start
  17.8 1.9 %copy-done = bf16[1,1,1,128,12288]{4,3,2,1,0:T(8,128)(2,1)S(1)} copy-done((bf16[1,1,1,128,12288]{4,3,2,1,0:T(8,128)(2,1)S(1)}, bf16[1,1,1,128,12288]{4,3,2,1,0:T(8,128)(2,1)}, u32[]{:S(2)}) %copy-start) | copy-done | bytes 3145752
  19.7 1.2 sum_on_chip.3
  20.9 1.9 %collective-permute-start.1 = (bf16[32,6272]{1,0:T(8,128)(2,1)S(1)}, bf16[32,6272]{1,0:T(8,128)(2,1)S(1)}, u32[]{:S(2)}, u32[]{:S(2)}) collective-permute-start(bf16[32,6272]{1,0:T(8,128)(2,1)S(1)} %sum_on_chip.3), channel_id=1, source_target_pairs={{0,64},{32,96},{64,0},{96,32},{1,65},{33,97},{65,1},{97,33},{2,66}... | collective-permute-start | bytes 1204232 | tf_op jit(solution)/shard_map/ppermute | solution.py:363
  22.9 1.2 sum_on_chip.4
  24.1 1.9 %collective-permute-start.2 = (bf16[32,6272]{1,0:T(8,128)(2,1)S(1)}, bf16[32,6272]{1,0:T(8,128)(2,1)S(1)}, u32[]{:S(2)}, u32[]{:S(2)}) collective-permute-start(bf16[32,6272]{1,0:T(8,128)(2,1)S(1)} %sum_on_chip.4), channel_id=1, source_target_pairs={{0,32},{32,64},{64,96},{96,0},{1,33},{33,65},{65,97},{97,1},{2,34}... | collective-permute-start | bytes 1204232 | tf_op jit(solution)/shard_map/ppermute | solution.py:363
  26.0 1.2 sum_on_chip.5
  27.3 4.6 %collective-permute-start.3 = (bf16[32,6272]{1,0:T(8,128)(2,1)S(1)}, bf16[32,6272]{1,0:T(8,128)(2,1)S(1)}, u32[]{:S(2)}, u32[]{:S(2)}) collective-permute-start(bf16[32,6272]{1,0:T(8,128)(2,1)S(1)} %sum_on_chip.5), channel_id=1, source_target_pairs={{0,96},{32,0},{64,32},{96,64},{1,97},{33,1},{65,33},{97,65},{2,98}... | collective-permute-start | bytes 1204232 | tf_op jit(solution)/shard_map/ppermute | solution.py:363
  31.8 0.1 pad_add_fusion.idx
  31.9 0.0 copy-start.2
  31.9 0.0 copy-start.3
  31.9 0.0 copy-start.4
  31.9 0.0 copy-start.5
  31.9 0.0 copy-start.6
  31.9 2.9 %collective-permute-done.1.c1.s1 = bf16[32,6272]{1,0:T(8,128)(2,1)S(1)} collective-permute-done((bf16[32,6272]{1,0:T(8,128)(2,1)S(1)}, bf16[32,6272]{1,0:T(8,128)(2,1)S(1)}, u32[]{:S(2)}, u32[]{:S(2)}) %collective-permute-start.1) | collective-permute-done | bytes 401440 | tf_op jit(solution)/shard_map/ppermute | solution.py:363
  34.9 9.3 %collective-permute-done.2.c2.s2 = bf16[32,6272]{1,0:T(8,128)(2,1)S(1)} collective-permute-done((bf16[32,6272]{1,0:T(8,128)(2,1)S(1)}, bf16[32,6272]{1,0:T(8,128)(2,1)S(1)}, u32[]{:S(2)}, u32[]{:S(2)}) %collective-permute-start.2) | collective-permute-done | bytes 401440 | tf_op jit(solution)/shard_map/ppermute | solution.py:363
  44.2 0.0 collective-permute-done.3.c3.s3
  44.2 3.1 %sum_over_x.1 = bf16[8,4,6272]{2,1,0:T(4,128)(2,1)S(1)} custom-call(s32[2]{0:T(128)S(1)} %pad_add_fusion.idx, bf16[128,12288]{1,0:T(8,128)(2,1)} %bitcast.20, bf16[128,96]{1,0:T(8,128)(2,1)S(1)} %bitcast.28, bf16[128,6272]{1,0:T(8,128)(2,1)S(1)} %collective-permute-done.there.there_scales, bf16[128,6272]{1,0:T(8,128)(2,1)S(1)} %collective-permute-done.there.there_scales, ...), custom_call_target="tpu_custom_call" | custom-call | flops 11796480 | bytes 2359296 | tf_op jit(solution)/shard_map/sum_over_x/pallas_call | solution.py:170
  47.3 16.9 %all_to_all.10.codes.scales = bf16[8,4,6272]{2,1,0:T(4,128)(2,1)S(1)} all-to-all(bf16[8,4,6272]{2,1,0:T(4,128)(2,1)S(1)} %sum_over_x.1), channel_id=1, replica_groups=mesh['zl'=2,'c'=2,'x'=4,'y'=8,'zh'=4] {'y'}, dimensions={0} | all-to-all | bytes 802816 | tf_op jit(solution)/shard_map/all_to_all | solution.py:383
  64.2 0.6 sum_over_y.1.g0
  64.8 1.9 %collective-permute-start.4 = (f32[4,6144]{1,0:T(4,128)S(1)}, f32[4,6144]{1,0:T(4,128)S(1)}, u32[]{:S(2)}, u32[]{:S(2)}) collective-permute-start(f32[4,6144]{1,0:T(4,128)S(1)} %sum_over_y.1.g0), channel_id=1, source_target_pairs={{0,256},{256,0},{1,257},{257,1},{2,258},{258,2},{3,259},{259,3},{4... | collective-permute-start | bytes 294920 | tf_op jit(solution)/shard_map/ppermute | solution.py:367
  66.7 3.4 %collective-permute-done.4.g1 = f32[4,6144]{1,0:T(4,128)S(1)} collective-permute-done((f32[4,6144]{1,0:T(4,128)S(1)}, f32[4,6144]{1,0:T(4,128)S(1)}, u32[]{:S(2)}, u32[]{:S(2)}) %collective-permute-start.4) | collective-permute-done | bytes 98336 | tf_op jit(solution)/shard_map/ppermute | solution.py:367
  70.1 0.0 copy-done.2
  70.1 0.0 copy-done.3
  70.1 0.0 copy-done.4
  70.1 0.0 copy-done.5
  70.1 0.0 copy-done.6
  70.1 0.4 low_weights.1
  70.5 13.9 %all_to_all.11.refs_0_ = bf16[8,4,6144]{2,1,0:T(4,128)(2,1)S(1)} all-to-all(bf16[8,4,6144]{2,1,0:T(4,128)(2,1)S(1)} %get-tuple-element.22), channel_id=1, replica_groups=mesh['zl'=2,'c'=2,'x'=4,'y'=8,'zh'=4] {'y'}, dimensions={0} | all-to-all | bytes 786432 | tf_op jit(solution)/shard_map/all_to_all | solution.py:388
  84.4 1.9 %collective-permute-start.5 = (bf16[8,4,6144]{2,1,0:T(4,128)(2,1)S(1)}, bf16[8,4,6144]{2,1,0:T(4,128)(2,1)S(1)}, u32[]{:S(2)}, u32[]{:S(2)}) collective-permute-start(bf16[8,4,6144]{2,1,0:T(4,128)(2,1)S(1)} %all_to_all.11.refs_0_), channel_id=1, source_target_pairs={{0,32},{32,64},{64,96},{96,0},{1,33},{33,65},{65,97},{97,1},{2,34}... | collective-permute-start | bytes 1179656 | tf_op jit(solution)/shard_map/ppermute | solution.py:363
  86.3 4.6 %collective-permute-start.8 = (bf16[8,4,6144]{2,1,0:T(4,128)(2,1)S(1)}, bf16[8,4,6144]{2,1,0:T(4,128)(2,1)S(1)}, u32[]{:S(2)}, u32[]{:S(2)}) collective-permute-start(bf16[8,4,6144]{2,1,0:T(4,128)(2,1)S(1)} %all_to_all.11.refs_0_), channel_id=1, source_target_pairs={{0,96},{32,0},{64,32},{96,64},{1,97},{33,1},{65,33},{97,65},{2,98}... | collective-permute-start | bytes 1179656 | tf_op jit(solution)/shard_map/ppermute | solution.py:363
  90.9 2.0 %collective-permute-start.7 = (bf16[8,4,6144]{2,1,0:T(4,128)(2,1)S(1)}, bf16[8,4,6144]{2,1,0:T(4,128)(2,1)S(1)}, u32[]{:S(2)}, u32[]{:S(2)}) collective-permute-start(bf16[8,4,6144]{2,1,0:T(4,128)(2,1)S(1)} %all_to_all.11.refs_0_), channel_id=1, source_target_pairs={{0,64},{32,96},{64,0},{96,32},{1,65},{33,97},{65,1},{97,33},{2,66}... | collective-permute-start | bytes 1179656 | tf_op jit(solution)/shard_map/ppermute | solution.py:363
  92.9 7.1 %collective-permute-start.6 = (f32[4,6144]{1,0:T(4,128)S(1)}, f32[4,6144]{1,0:T(4,128)S(1)}, u32[]{:S(2)}, u32[]{:S(2)}) collective-permute-start(f32[4,6144]{1,0:T(4,128)S(1)} %get-tuple-element.23.mine), channel_id=1, source_target_pairs={{0,128},{128,0},{1,129},{129,1},{2,130},{130,2},{3,131},{131,3},{4... | collective-permute-start | bytes 294920 | tf_op jit(solution)/shard_map/ppermute | solution.py:367
  100.0 0.9 collective-permute-done.6.other
  101.0 7.8 %new_states.1 = (f32[4,12288]{1,0:T(4,128)}, bf16[4,12288]{1,0:T(4,128)(2,1)}, f32[4,96]{1,0:T(4,128)}, bf16[4,12288]{1,0:T(4,128)(2,1)}, f32[4,96]{1,0:T(4,128)}) custom-call(s32[1]{0:T(128)} %bitcast.idx, f32[4,6144]{1,0:T(4,128)S(1)} %get-tuple-element.23.mine, f32[4,6144]{1,0:T(4,128)S(1)} %collective-permute-done.6.other, f32[4,12288]{1,0:T(4,128)S(1)} %bitcast.30, ...), custom_call_target="tpu_custom_call" | custom-call | flops 2949120 | bytes 983040 | tf_op jit(solution)/shard_map/new_states/pallas_call | solution.py:287
  108.8 2.3 %collective-permute-start.9 = (bf16[8,4,6144]{2,1,0:T(4,128)(2,1)S(1)}, bf16[8,4,6144]{2,1,0:T(4,128)(2,1)S(1)}, u32[]{:S(2)}, u32[]{:S(2)}) collective-permute-start(bf16[8,4,6144]{2,1,0:T(4,128)(2,1)S(1)} %all_to_all.11.refs_0_), channel_id=1, source_target_pairs={{0,128},{128,0},{1,129},{129,1},{2,130},{130,2},{3,131},{131,3},{4... | collective-permute-start | bytes 1179656 | tf_op jit(solution)/shard_map/ppermute | solution.py:367
  111.0 0.0 collective-permute-done.5.refs_1_
  111.0 0.0 collective-permute-done.8.refs_3_
  111.1 2.1 %collective-permute-start.12 = (bf16[8,4,6144]{2,1,0:T(4,128)(2,1)S(1)}, bf16[8,4,6144]{2,1,0:T(4,128)(2,1)S(1)}, u32[]{:S(2)}, u32[]{:S(2)}) collective-permute-start(bf16[8,4,6144]{2,1,0:T(4,128)(2,1)S(1)} %collective-permute-done.8.refs_3_), channel_id=1, source_target_pairs={{0,128},{128,0},{1,129},{129,1},{2,130},{130,2},{3,131},{131,3},{4... | collective-permute-start | bytes 1179656 | tf_op jit(solution)/shard_map/ppermute | solution.py:367
  113.1 0.0 collective-permute-done.7.refs_2_
  113.1 2.3 %collective-permute-start.11 = (bf16[8,4,6144]{2,1,0:T(4,128)(2,1)S(1)}, bf16[8,4,6144]{2,1,0:T(4,128)(2,1)S(1)}, u32[]{:S(2)}, u32[]{:S(2)}) collective-permute-start(bf16[8,4,6144]{2,1,0:T(4,128)(2,1)S(1)} %collective-permute-done.7.refs_2_), channel_id=1, source_target_pairs={{0,128},{128,0},{1,129},{129,1},{2,130},{130,2},{3,131},{131,3},{4... | collective-permute-start | bytes 1179656 | tf_op jit(solution)/shard_map/ppermute | solution.py:367
  115.4 2.1 %collective-permute-start.10 = (bf16[8,4,6144]{2,1,0:T(4,128)(2,1)S(1)}, bf16[8,4,6144]{2,1,0:T(4,128)(2,1)S(1)}, u32[]{:S(2)}, u32[]{:S(2)}) collective-permute-start(bf16[8,4,6144]{2,1,0:T(4,128)(2,1)S(1)} %collective-permute-done.5.refs_1_), channel_id=1, source_target_pairs={{0,128},{128,0},{1,129},{129,1},{2,130},{130,2},{3,131},{131,3},{4... | collective-permute-start | bytes 1179656 | tf_op jit(solution)/shard_map/ppermute | solution.py:367
  117.5 0.0 collective-permute-done.9.refs_4_
  117.5 0.0 collective-permute-done.12.refs_7_
  117.5 0.0 collective-permute-done.11.refs_6_
  117.5 1.5 %collective-permute-done.10.refs_5_ = bf16[8,4,6144]{2,1,0:T(4,128)(2,1)S(1)} collective-permute-done((bf16[8,4,6144]{2,1,0:T(4,128)(2,1)S(1)}, bf16[8,4,6144]{2,1,0:T(4,128)(2,1)S(1)}, u32[]{:S(2)}, u32[]{:S(2)}) %collective-permute-start.10) | collective-permute-done | bytes 393248 | tf_op jit(solution)/shard_map/ppermute | solution.py:367
  119.0 4.2 %place_weights.1 = (bf16[128,12288]{1,0:T(8,128)(2,1)}, bf16[12288,128]{1,0:T(8,128)(2,1)}) custom-call(s32[2]{0:T(128)S(1)} %pad_add_fusion.idx, bf16[8,4,6144]{2,1,0:T(4,128)(2,1)S(1)} %all_to_all.11.refs_0_, bf16[8,4,6144]{2,1,0:T(4,128)(2,1)S(1)} %collective-permute-done.5.refs_1_, bf16[8,4,6144]{2,1,0:T(4,128)(2,1)S(1)} %collective-permute-done.7.refs_2_, ...), custom_call_target="tpu_custom_call" | custom-call | bytes 9437184 | tf_op jit(solution)/shard_map/place_weights/pallas_call | solution.py:340
Async XLA Ops:
  2.1 15.7 %copy-start.1 = (bf16[1,1,1,128,96]{4,3,2,1,0:T(8,128)(2,1)S(1)}, bf16[1,1,1,128,96]{4,3,2,1,0:T(8,128)(2,1)}, u32[]{:S(2)}) copy-start(bf16[1,1,1,128,96]{4,3,2,1,0:T(8,128)(2,1)} %copy.14) | copy-start | bytes 73732
  5.8 12.1 %collective-permute-start = (bf16[128,6272]{1,0:T(8,128)(2,1)}, bf16[128,6272]{1,0:T(8,128)(2,1)S(1)}, u32[]{:S(2)}, u32[]{:S(2)}) collective-permute-start(bf16[128,6272]{1,0:T(8,128)(2,1)} %pack_rows.1), channel_id=1, source_target_pairs={{0,128},{128,0},{1,129},{129,1},{2,130},{130,2},{3,131},{131,3},{4... | collective-permute-start | bytes 4816904 | tf_op jit(solution)/shard_map/ppermute | solution.py:367
  17.8 1.9 %copy-start = (bf16[1,1,1,128,12288]{4,3,2,1,0:T(8,128)(2,1)S(1)}, bf16[1,1,1,128,12288]{4,3,2,1,0:T(8,128)(2,1)}, u32[]{:S(2)}) copy-start(bf16[1,1,1,128,12288]{4,3,2,1,0:T(8,128)(2,1)} %param.7) | copy-start | bytes 9437188
  20.9 13.9 %collective-permute-start.1 = (bf16[32,6272]{1,0:T(8,128)(2,1)S(1)}, bf16[32,6272]{1,0:T(8,128)(2,1)S(1)}, u32[]{:S(2)}, u32[]{:S(2)}) collective-permute-start(bf16[32,6272]{1,0:T(8,128)(2,1)S(1)} %sum_on_chip.3), channel_id=1, source_target_pairs={{0,64},{32,96},{64,0},{96,32},{1,65},{33,97},{65,1},{97,33},{2,66}... | collective-permute-start | bytes 1204232 | tf_op jit(solution)/shard_map/ppermute | solution.py:363
  24.1 20.1 %collective-permute-start.2 = (bf16[32,6272]{1,0:T(8,128)(2,1)S(1)}, bf16[32,6272]{1,0:T(8,128)(2,1)S(1)}, u32[]{:S(2)}, u32[]{:S(2)}) collective-permute-start(bf16[32,6272]{1,0:T(8,128)(2,1)S(1)} %sum_on_chip.4), channel_id=1, source_target_pairs={{0,32},{32,64},{64,96},{96,0},{1,33},{33,65},{65,97},{97,1},{2,34}... | collective-permute-start | bytes 1204232 | tf_op jit(solution)/shard_map/ppermute | solution.py:363
  27.3 16.9 %collective-permute-start.3 = (bf16[32,6272]{1,0:T(8,128)(2,1)S(1)}, bf16[32,6272]{1,0:T(8,128)(2,1)S(1)}, u32[]{:S(2)}, u32[]{:S(2)}) collective-permute-start(bf16[32,6272]{1,0:T(8,128)(2,1)S(1)} %sum_on_chip.5), channel_id=1, source_target_pairs={{0,96},{32,0},{64,32},{96,64},{1,97},{33,1},{65,33},{97,65},{2,98}... | collective-permute-start | bytes 1204232 | tf_op jit(solution)/shard_map/ppermute | solution.py:363
  31.9 38.2 %copy-start.2 = (f32[1,4,12288]{2,1,0:T(4,128)S(1)}, f32[1,4,12288]{2,1,0:T(4,128)}, u32[]{:S(2)}) copy-start(f32[1,4,12288]{2,1,0:T(4,128)} %param.9) | copy-start | bytes 589828
  31.9 38.2 %copy-start.3 = (bf16[1,4,12288]{2,1,0:T(4,128)(2,1)S(1)}, bf16[1,4,12288]{2,1,0:T(4,128)(2,1)}, u32[]{:S(2)}) copy-start(bf16[1,4,12288]{2,1,0:T(4,128)(2,1)} %param.10) | copy-start | bytes 294916
  31.9 38.2 %copy-start.4 = (bf16[1,4,12288]{2,1,0:T(4,128)(2,1)S(1)}, bf16[1,4,12288]{2,1,0:T(4,128)(2,1)}, u32[]{:S(2)}) copy-start(bf16[1,4,12288]{2,1,0:T(4,128)(2,1)} %param.12) | copy-start | bytes 294916
  31.9 38.2 %copy-start.5 = (f32[1,4,96]{2,1,0:T(4,128)S(1)}, f32[1,4,96]{2,1,0:T(4,128)}, u32[]{:S(2)}) copy-start(f32[1,4,96]{2,1,0:T(4,128)} %param.11) | copy-start | bytes 4612
  31.9 38.2 %copy-start.6 = (f32[1,4,96]{2,1,0:T(4,128)S(1)}, f32[1,4,96]{2,1,0:T(4,128)}, u32[]{:S(2)}) copy-start(f32[1,4,96]{2,1,0:T(4,128)} %param.13) | copy-start | bytes 4612
  64.8 5.4 %collective-permute-start.4 = (f32[4,6144]{1,0:T(4,128)S(1)}, f32[4,6144]{1,0:T(4,128)S(1)}, u32[]{:S(2)}, u32[]{:S(2)}) collective-permute-start(f32[4,6144]{1,0:T(4,128)S(1)} %sum_over_y.1.g0), channel_id=1, source_target_pairs={{0,256},{256,0},{1,257},{257,1},{2,258},{258,2},{3,259},{259,3},{4... | collective-permute-start | bytes 294920 | tf_op jit(solution)/shard_map/ppermute | solution.py:367
  84.4 26.6 %collective-permute-start.5 = (bf16[8,4,6144]{2,1,0:T(4,128)(2,1)S(1)}, bf16[8,4,6144]{2,1,0:T(4,128)(2,1)S(1)}, u32[]{:S(2)}, u32[]{:S(2)}) collective-permute-start(bf16[8,4,6144]{2,1,0:T(4,128)(2,1)S(1)} %all_to_all.11.refs_0_), channel_id=1, source_target_pairs={{0,32},{32,64},{64,96},{96,0},{1,33},{33,65},{65,97},{97,1},{2,34}... | collective-permute-start | bytes 1179656 | tf_op jit(solution)/shard_map/ppermute | solution.py:363
  86.3 24.7 %collective-permute-start.8 = (bf16[8,4,6144]{2,1,0:T(4,128)(2,1)S(1)}, bf16[8,4,6144]{2,1,0:T(4,128)(2,1)S(1)}, u32[]{:S(2)}, u32[]{:S(2)}) collective-permute-start(bf16[8,4,6144]{2,1,0:T(4,128)(2,1)S(1)} %all_to_all.11.refs_0_), channel_id=1, source_target_pairs={{0,96},{32,0},{64,32},{96,64},{1,97},{33,1},{65,33},{97,65},{2,98}... | collective-permute-start | bytes 1179656 | tf_op jit(solution)/shard_map/ppermute | solution.py:363
  90.9 22.2 %collective-permute-start.7 = (bf16[8,4,6144]{2,1,0:T(4,128)(2,1)S(1)}, bf16[8,4,6144]{2,1,0:T(4,128)(2,1)S(1)}, u32[]{:S(2)}, u32[]{:S(2)}) collective-permute-start(bf16[8,4,6144]{2,1,0:T(4,128)(2,1)S(1)} %all_to_all.11.refs_0_), channel_id=1, source_target_pairs={{0,64},{32,96},{64,0},{96,32},{1,65},{33,97},{65,1},{97,33},{2,66}... | collective-permute-start | bytes 1179656 | tf_op jit(solution)/shard_map/ppermute | solution.py:363
  92.9 8.1 %collective-permute-start.6 = (f32[4,6144]{1,0:T(4,128)S(1)}, f32[4,6144]{1,0:T(4,128)S(1)}, u32[]{:S(2)}, u32[]{:S(2)}) collective-permute-start(f32[4,6144]{1,0:T(4,128)S(1)} %get-tuple-element.23.mine), channel_id=1, source_target_pairs={{0,128},{128,0},{1,129},{129,1},{2,130},{130,2},{3,131},{131,3},{4... | collective-permute-start | bytes 294920 | tf_op jit(solution)/shard_map/ppermute | solution.py:367
  108.8 8.7 %collective-permute-start.9 = (bf16[8,4,6144]{2,1,0:T(4,128)(2,1)S(1)}, bf16[8,4,6144]{2,1,0:T(4,128)(2,1)S(1)}, u32[]{:S(2)}, u32[]{:S(2)}) collective-permute-start(bf16[8,4,6144]{2,1,0:T(4,128)(2,1)S(1)} %all_to_all.11.refs_0_), channel_id=1, source_target_pairs={{0,128},{128,0},{1,129},{129,1},{2,130},{130,2},{3,131},{131,3},{4... | collective-permute-start | bytes 1179656 | tf_op jit(solution)/shard_map/ppermute | solution.py:367
  111.1 6.4 %collective-permute-start.12 = (bf16[8,4,6144]{2,1,0:T(4,128)(2,1)S(1)}, bf16[8,4,6144]{2,1,0:T(4,128)(2,1)S(1)}, u32[]{:S(2)}, u32[]{:S(2)}) collective-permute-start(bf16[8,4,6144]{2,1,0:T(4,128)(2,1)S(1)} %collective-permute-done.8.refs_3_), channel_id=1, source_target_pairs={{0,128},{128,0},{1,129},{129,1},{2,130},{130,2},{3,131},{131,3},{4... | collective-permute-start | bytes 1179656 | tf_op jit(solution)/shard_map/ppermute | solution.py:367
  113.1 4.4 %collective-permute-start.11 = (bf16[8,4,6144]{2,1,0:T(4,128)(2,1)S(1)}, bf16[8,4,6144]{2,1,0:T(4,128)(2,1)S(1)}, u32[]{:S(2)}, u32[]{:S(2)}) collective-permute-start(bf16[8,4,6144]{2,1,0:T(4,128)(2,1)S(1)} %collective-permute-done.7.refs_2_), channel_id=1, source_target_pairs={{0,128},{128,0},{1,129},{129,1},{2,130},{130,2},{3,131},{131,3},{4... | collective-permute-start | bytes 1179656 | tf_op jit(solution)/shard_map/ppermute | solution.py:367
  115.4 3.6 %collective-permute-start.10 = (bf16[8,4,6144]{2,1,0:T(4,128)(2,1)S(1)}, bf16[8,4,6144]{2,1,0:T(4,128)(2,1)S(1)}, u32[]{:S(2)}, u32[]{:S(2)}) collective-permute-start(bf16[8,4,6144]{2,1,0:T(4,128)(2,1)S(1)} %collective-permute-done.5.refs_1_), channel_id=1, source_target_pairs={{0,128},{128,0},{1,129},{129,1},{2,130},{130,2},{3,131},{131,3},{4... | collective-permute-start | bytes 1179656 | tf_op jit(solution)/shard_map/ppermute | solution.py:367

commit v3 on v2

v3 whole, which is shorter than its diff:
```python
import functools

import jax
import jax.numpy as jnp
from jax import lax
from jax.experimental import pallas as pl
from jax.experimental.pallas import tpu as pltpu
from jax.sharding import Mesh, PartitionSpec as P

D = 12288
HALF = D // 2
BLOCK = 128
NB = D // BLOCK
HB = NB // 2
ROWS = 128
NX, NY, NZ = 4, 8, 2
XR = ROWS // NX
YR = XR // NY
QUARTER = D // 4
QB = NB // 4
PAD = HALF + BLOCK
QPAD = QUARTER + BLOCK
SPAN = 172.0
OFFSET = 86.0

beta_one = 0.9
beta_two = 0.95
rate = 0.02
adam_eps = 1e-08
scale_eps = 1e-06
corr_one = 1.0 - 0.9**10
corr_two = 1.0 - 0.95**10

f32 = jnp.float32
bf16 = jnp.bfloat16


def params(mib=24):
    return pltpu.CompilerParams(vmem_limit_bytes=mib * 1024 * 1024)


def cost(flops, nbytes):
    return pl.CostEstimate(flops=flops, bytes_accessed=nbytes, transcendentals=0)


def encode(value, factor):
    size = jnp.exp(jnp.abs(value) * factor - OFFSET)
    return jnp.where(value < 0, -size, size)


def decode(code, step):
    size = (jnp.log(jnp.abs(code)) + OFFSET) * step
    return jnp.where(code < 0, -size, size)


def scale_of(peak):
    return jnp.maximum(peak * (1.0 + 2.0**-7), 1e-30).astype(bf16)


def pack_kernel(idx, values, scales, out, own):
    rows = scales[...].astype(f32).T
    low, high = rows[:, :HB], rows[:, HB:NB]
    pad = jnp.zeros((ROWS, BLOCK - HB), bf16)
    first = idx[0] == 0
    out[:, :HALF] = values[...]
    out[:, HALF : HALF + HB] = jnp.where(first, low, high).astype(bf16)
    out[:, HALF + HB :] = pad
    own[:, :HB] = jnp.where(first, high, low).astype(bf16)
    own[:, HB:] = pad


def pack(half, values, scales):
    return pl.pallas_call(
        pack_kernel,
        grid_spec=pltpu.PrefetchScalarGridSpec(
            num_scalar_prefetch=1,
            grid=(1,),
            in_specs=[
                pl.BlockSpec((ROWS, HALF), lambda i, s: (0, s[0])),
                pl.BlockSpec((NB, ROWS), lambda i, s: (0, 0)),
            ],
            out_specs=[
                pl.BlockSpec((ROWS, PAD), lambda i, s: (0, 0)),
                pl.BlockSpec((ROWS, BLOCK), lambda i, s: (0, 0)),
            ],
        ),
        out_shape=[
            jax.ShapeDtypeStruct((ROWS, PAD), bf16),
            jax.ShapeDtypeStruct((ROWS, BLOCK), bf16),
        ],
        compiler_params=params(),
        cost_estimate=cost(0, 2 * ROWS * HALF * 2),
        name="pack_rows",
    )(half, values, scales)


def add_cores(values, scales, there, there_scales, totals):
    mine = scales[...].astype(f32)
    theirs = there_scales[...].astype(f32)
    peak = jnp.zeros((XR, BLOCK), f32)
    for b in range(HB):
        cols = slice(b * BLOCK, (b + 1) * BLOCK)
        total = values[:, cols].astype(f32) * mine[:, b : b + 1]
        total = total + there[:, cols].astype(f32) * theirs[:, b : b + 1]
        totals[:, cols] = total
        peak = jnp.maximum(peak, jnp.abs(total))
    return peak


def code_kernel(idx, values, scales, there, there_scales, out, totals):
    scale = scale_of(add_cores(values, scales, there, there_scales, totals))
    out[:, HALF:] = scale
    factor = SPAN / scale.astype(f32)
    for b in range(HB):
        cols = slice(b * BLOCK, (b + 1) * BLOCK)
        out[:, cols] = encode(totals[:, cols], factor).astype(bf16)


def own_kernel(idx, values, scales, there, there_scales, out):
    add_cores(values, scales, there, there_scales, out)


def chip_sum(idx, values, scales, there, coded):
    if coded:
        kernel, width, kind, name = code_kernel, PAD, bf16, "coded_chip_sum"
        scratch = [pltpu.VMEM((XR, HALF), f32)]
    else:
        kernel, width, kind, name = own_kernel, HALF, f32, "own_chip_sum"
        scratch = []
    return pl.pallas_call(
        kernel,
        grid_spec=pltpu.PrefetchScalarGridSpec(
            num_scalar_prefetch=1,
            grid=(1,),
            in_specs=[
                pl.BlockSpec((XR, HALF), lambda i, s: (s[0], s[1])),
                pl.BlockSpec((XR, BLOCK), lambda i, s: (s[0], 0)),
                pl.BlockSpec((XR, HALF), lambda i, s: (s[0], 0)),
                pl.BlockSpec((XR, BLOCK), lambda i, s: (s[0], HB)),
            ],
            out_specs=pl.BlockSpec((XR, width), lambda i, s: (0, 0)),
            scratch_shapes=scratch,
        ),
        out_shape=jax.ShapeDtypeStruct((XR, width), kind),
        compiler_params=params(),
        cost_estimate=cost(20 * XR * HALF, 6 * XR * HALF),
        name=name,
    )(idx, values, scales, there, there)


def row_kernel(own, c1, s1, c2, s2, c3, s3, out, totals):
    coded = [
        (ref, scale[...].astype(f32) * (1.0 / SPAN))
        for ref, scale in ((c1, s1), (c2, s2), (c3, s3))
    ]
    peak = jnp.zeros((XR, BLOCK), f32)
    for b in range(HB):
        cols = slice(b * BLOCK, (b + 1) * BLOCK)
        total = own[:, cols]
        for ref, step in coded:
            total = total + decode(ref[:, cols].astype(f32), step)
        totals[:, cols] = total
        peak = jnp.maximum(peak, jnp.abs(total))
    scale = scale_of(peak).astype(f32)
    for z in range(NZ):
        planes = slice(z * NY, (z + 1) * NY)
        out[planes, :, QUARTER:] = scale.reshape(NY, YR, BLOCK).astype(bf16)
    factor = SPAN / scale
    for b in range(HB):
        cols = slice(b * BLOCK, (b + 1) * BLOCK)
        z, inner = b // QB, slice(b % QB * BLOCK, (b % QB + 1) * BLOCK)
        code = encode(totals[:, cols], factor)
        out[z * NY : (z + 1) * NY, :, inner] = code.reshape(NY, YR, BLOCK).astype(bf16)


def row_sum(own, arrived):
    ins = [pl.BlockSpec((XR, HALF), lambda i: (0, 0))]
    args = [own]
    for a in arrived:
        ins += [
            pl.BlockSpec((XR, HALF), lambda i: (0, 0)),
            pl.BlockSpec((XR, BLOCK), lambda i: (0, HB)),
        ]
        args += [a, a]
    return pl.pallas_call(
        row_kernel,
        grid=(1,),
        in_specs=ins,
        out_specs=pl.BlockSpec((NZ * NY, YR, QPAD), lambda i: (0, 0, 0)),
        scratch_shapes=[pltpu.VMEM((XR, HALF), f32)],
        out_shape=jax.ShapeDtypeStruct((NZ * NY, YR, QPAD), bf16),
        compiler_params=params(),
        cost_estimate=cost(60 * XR * HALF, 12 * XR * HALF),
        name="sum_over_x",
    )(*args)


def last_kernel(codes, scales, out):
    parts = NZ * NY * YR
    step = scales[...].astype(f32).reshape(parts, BLOCK) * (1.0 / SPAN)
    for b in range(QB):
        cols = slice(b * BLOCK, (b + 1) * BLOCK)
        code = codes[:, :, cols].astype(f32).reshape(parts, BLOCK)
        term = decode(code, step)
        out[:, cols] = jnp.sum(term.reshape(NZ * NY, YR, BLOCK), axis=0)


def last_sum(codes):
    return pl.pallas_call(
        last_kernel,
        grid=(1,),
        in_specs=[
            pl.BlockSpec((NZ * NY, YR, QUARTER), lambda i: (0, 0, 0)),
            pl.BlockSpec((NZ * NY, YR, BLOCK), lambda i: (0, 0, QB)),
        ],
        out_specs=pl.BlockSpec((YR, QUARTER), lambda i: (0, 0)),
        out_shape=jax.ShapeDtypeStruct((YR, QUARTER), f32),
        compiler_params=params(),
        cost_estimate=cost(20 * XR * HALF, 3 * XR * HALF),
        name="sum_over_zy",
    )(codes, codes)


def adam(gradient, master, first_old, second_old):
    first = beta_one * first_old + (1.0 - beta_one) * gradient
    second = beta_two * second_old + (1.0 - beta_two) * gradient * gradient
    direction = first / corr_one / (jnp.sqrt(second / corr_two) + adam_eps)
    return first, second, master - rate * direction


def low_kernel(idx, grad, master, fm, fs, sm, ss, low_out):
    def chosen(ref):
        scales = ref[...]
        parts = [scales[:, k * QB : (k + 1) * QB] for k in range(4)]
        low = jnp.where(idx[0] == 0, parts[0], parts[1])
        high = jnp.where(idx[0] == 2, parts[2], parts[3])
        return jnp.where(idx[0] < 2, low, high)

    fscale, sscale = chosen(fs), chosen(ss)
    for b in range(QB):
        cols = slice(b * BLOCK, (b + 1) * BLOCK)
        first_old = fm[:, cols].astype(f32) * fscale[:, b : b + 1]
        second_old = sm[:, cols].astype(f32) * sscale[:, b : b + 1]
        _, _, updated = adam(grad[:, cols], master[:, cols], first_old, second_old)
        low = updated.astype(bf16)
        for i in range(NZ * NY):
            low_out[i, :, cols] = low


def low_weights(quarter, grad, master, fm, fs, sm, ss):
    part = pl.BlockSpec((YR, QUARTER), lambda i, s: (0, s[0]))
    whole = pl.BlockSpec((YR, QUARTER), lambda i, s: (0, 0))
    scale = pl.BlockSpec((YR, NB), lambda i, s: (0, 0))
    return pl.pallas_call(
        low_kernel,
        grid_spec=pltpu.PrefetchScalarGridSpec(
            num_scalar_prefetch=1,
            grid=(1,),
            in_specs=[whole, part, part, scale, part, scale],
            out_specs=pl.BlockSpec((NZ * NY, YR, QUARTER), lambda i, s: (0, 0, 0)),
        ),
        out_shape=jax.ShapeDtypeStruct((NZ * NY, YR, QUARTER), bf16),
        compiler_params=params(),
        cost_estimate=cost(30 * YR * QUARTER, 40 * YR * QUARTER),
        name="low_weights",
    )(quarter, grad, master, fm, fs, sm, ss)


def state_kernel(
    idx, mine, other, master, fm, fs, sm, ss, om, of, ofs, os, oss, firsts, seconds
):
    first_half = idx[0] == 0

    def stacked(ref, b):
        halves = [ref[:, k * BLOCK : (k + 1) * BLOCK] for k in (b, b + HB)]
        return jnp.concatenate([half.astype(f32) for half in halves], axis=0)

    def scales_of(ref):
        return jnp.concatenate([ref[:, :HB], ref[:, HB:]], axis=0)

    def store(ref, b, value):
        for k, rows in ((b, slice(0, YR)), (b + HB, slice(YR, 2 * YR))):
            ref[:, k * BLOCK : (k + 1) * BLOCK] = value[rows].astype(ref.dtype)

    fscale, sscale = scales_of(fs), scales_of(ss)
    lane = lax.broadcasted_iota(jnp.int32, (2 * YR, HB), 1)
    fpeaks = jnp.zeros((2 * YR, HB), f32)
    speaks = jnp.zeros((2 * YR, HB), f32)
    for b in range(HB):
        cols = slice(b * BLOCK, (b + 1) * BLOCK)
        one, two = mine[:, cols], other[:, cols]
        gradient = jnp.concatenate(
            [jnp.where(first_half, one, two), jnp.where(first_half, two, one)], axis=0
        )
        first_old = stacked(fm, b) * fscale[:, b : b + 1]
        second_old = stacked(sm, b) * sscale[:, b : b + 1]
        first, second, updated = adam(
            gradient, stacked(master, b), first_old, second_old
        )
        store(om, b, updated)
        firsts[:, cols] = first
        seconds[:, cols] = second
        fpeak = jnp.max(jnp.abs(first), axis=1, keepdims=True)
        speak = jnp.max(second, axis=1, keepdims=True)
        fpeaks = jnp.where(lane == b, fpeak, fpeaks)
        speaks = jnp.where(lane == b, speak, speaks)
    fpeaks = fpeaks + scale_eps
    speaks = speaks + scale_eps
    for ref, peaks in ((ofs, fpeaks), (oss, speaks)):
        ref[:, :HB] = peaks[:YR]
        ref[:, HB:] = peaks[YR:]
    finverse, sinverse = 1.0 / fpeaks, 1.0 / speaks
    for b in range(HB):
        cols = slice(b * BLOCK, (b + 1) * BLOCK)
        store(of, b, firsts[:, cols] * finverse[:, b : b + 1])
        store(os, b, seconds[:, cols] * sinverse[:, b : b + 1])


def states(core, mine, other, master, fm, fs, sm, ss):
    half = pl.BlockSpec((YR, HALF), lambda i, s: (0, 0))
    whole = pl.BlockSpec((YR, D), lambda i, s: (0, 0))
    scale = pl.BlockSpec((YR, NB), lambda i, s: (0, 0))
    shape = jax.ShapeDtypeStruct
    return pl.pallas_call(
        state_kernel,
        grid_spec=pltpu.PrefetchScalarGridSpec(
            num_scalar_prefetch=1,
            grid=(1,),
            in_specs=[half, half, whole, whole, scale, whole, scale],
            out_specs=[whole, whole, scale, whole, scale],
            scratch_shapes=[pltpu.VMEM((2 * YR, HALF), f32)] * 2,
        ),
        out_shape=[
            shape((YR, D), f32),
            shape((YR, D), bf16),
            shape((YR, NB), f32),
            shape((YR, D), bf16),
            shape((YR, NB), f32),
        ],
        compiler_params=params(),
        cost_estimate=cost(60 * YR * D, 20 * YR * D),
        name="new_states",
    )(core, mine, other, master, fm, fs, sm, ss)


def place_kernel(idx, *refs):
    pieces, (weights, transposed, rows) = refs[:NX], refs[-3:]
    for shift, ref in enumerate(pieces):
        start = pl.multiple_of(lax.rem(idx[1] + NX - shift, NX) * XR, XR)
        low = ref[...].astype(f32).reshape(XR, QUARTER).astype(bf16)
        rows[pl.ds(start, XR), :] = low
    low = rows[...]
    weights[...] = low
    transposed[...] = low.T


def place(idx, pieces, before=()):
    ins, args = [], []
    for piece in pieces:
        if isinstance(piece, tuple):
            k, piece = piece
            ins.append(
                pl.BlockSpec((None, NY, YR, QUARTER), lambda j, s, k=k: (k, j, 0, 0))
            )
        else:
            ins.append(pl.BlockSpec((NY, YR, QUARTER), lambda j, s: (j, 0, 0)))
        args.append(piece)
    return pl.pallas_call(
        place_kernel,
        grid_spec=pltpu.PrefetchScalarGridSpec(
            num_scalar_prefetch=1,
            grid=(NZ,),
            in_specs=ins + [pl.BlockSpec(memory_space=pl.ANY)] * len(before),
            out_specs=[
                pl.BlockSpec((ROWS, QUARTER), lambda j, s: (0, s[0] * NZ + j)),
                pl.BlockSpec((QUARTER, ROWS), lambda j, s: (s[0] * NZ + j, 0)),
            ],
            scratch_shapes=[pltpu.VMEM((ROWS, QUARTER), bf16)],
        ),
        out_shape=[
            jax.ShapeDtypeStruct((ROWS, D), bf16),
            jax.ShapeDtypeStruct((D, ROWS), bf16),
        ],
        input_output_aliases={1 + NX: 0, 2 + NX: 1} if before else {},
        compiler_params=params(),
        cost_estimate=cost(0, 3 * ROWS * HALF * 2),
        name="place_weights",
    )(idx, *args, *before)


def shift_x(value, shift):
    return lax.ppermute(value, "x", [(i, (i + shift) % NX) for i in range(NX)])


def exchange(value, axis):
    return lax.all_to_all(value, axis, 0, 0, tiled=True)


def swap(value, axis):
    return lax.ppermute(value, axis, [(0, 1), (1, 0)])


def on_device(gv, gs, master, fm, fs, sm, ss):
    gv, gs = gv.reshape(ROWS, D), jnp.swapaxes(gs.reshape(ROWS, NB), 0, 1)
    master, fm, sm = master.reshape(YR, D), fm.reshape(YR, D), sm.reshape(YR, D)
    fs, ss = fs.reshape(YR, NB), ss.reshape(YR, NB)
    x = lax.axis_index("x").astype(jnp.int32)
    core = lax.axis_index("c").astype(jnp.int32)
    plane = lax.axis_index("zl").astype(jnp.int32)
    half = core.reshape(1)

    packed, scales = pack(1 - half, gv, gs)
    there = swap(packed, "c")
    arrived = []
    for shift in (2, 1, 3):
        target = jnp.stack([lax.rem(x + shift, NX), core])
        arrived.append(shift_x(chip_sum(target, gv, scales, there, True), shift))
    own = chip_sum(jnp.stack([x, core]), gv, scales, there, False)
    quarter = last_sum(exchange(row_sum(own, arrived), ("zl", "y")))
    low = low_weights((2 * core + plane).reshape(1), quarter, master, fm, fs, sm, ss)
    low_y = exchange(low, ("zl", "y"))

    from_z = swap(quarter, "zl")
    left = jnp.where(plane == 0, quarter, from_z)
    right = jnp.where(plane == 0, from_z, quarter)
    gradient = jnp.concatenate([left, right], axis=1)
    new = states(half, gradient, swap(gradient, "c"), master, fm, fs, sm, ss)
    low_y, new = lax.optimization_barrier((low_y, new))

    two, one, three = [shift_x(low_y, shift) for shift in (2, 1, 3)]
    other_y = swap(low_y, "c")
    rest = [swap(piece, "c") for piece in (one, two, three)]
    placed = place(jnp.stack([core, x]), [low_y, one, two, three])
    weights, transposed = place(jnp.stack([1 - core, x]), [other_y] + rest, placed)
    om, of, ofs, os, oss = [a[None] for a in new]
    return om, of, ofs, os, oss, weights[None], transposed[None]


def solution(mesh):
    fine = Mesh(
        mesh.devices.reshape(NZ, 2, NX, NY, mesh.devices.shape[-1]),
        ("zl", "c", "x", "y", "zh"),
    )
    grads = P(("zl", "c"), ("x", "y"), "zh", None, None)
    rows = P("zh", ("x", "y"), None)
    shard = P("zh", None, None)
    return jax.shard_map(
        on_device,
        mesh=fine,
        in_specs=(grads, grads, rows, rows, rows, rows, rows),
        out_specs=(rows,) * 5 + (shard, shard),
        check_vma=False,
    )
```

time: 124 us -> 112 us (0.903)
  blocking collectives: 30.8 us -> 14.5 us
  starting transfers between devices: 43.3 us -> 58.6 us
  waiting for transfers between devices: 21.2 us -> 15.1 us
  Pallas kernels: 23.4 us -> 17.5 us
    all_to_all x2 -> x1, blocking collectives: 30.8 us -> 14.5 us  [exchange(): return lax.all_to_all(value, axis, 0, 0, tiled=True)]
    ppermute x7, starting transfers between devices: 26.5 us -> 34.8 us  [swap(): return lax.ppermute(value, axis, [(0, 1), (1, 0)])]
    all_to_all x0 -> x1, starting transfers between devices: none -> 6.02 us  [exchange(): return lax.all_to_all(value, axis, 0, 0, tiled=True)]
    ppermute x7, waiting for transfers between devices: 8.91 us -> 3.76 us  [swap(): return lax.ppermute(value, axis, [(0, 1), (1, 0)])]
    pallas_call x1, Pallas kernels: 3.68 us -> 0.26 us  [pack(): pl.pallas_call(pack_kernel, grid_spec=pltpu.PrefetchScalarGridSpec(num_sc...]
    pallas_call x1, Pallas kernels: 7.81 us -> 4.51 us  [states(): pl.pallas_call(state_kernel, grid_spec=pltpu.PrefetchScalarGridSpec(num_s...]
    unnamed x15 -> x16, local copies, waits for them, and re-layouts: 3.37 us -> 4.54 us
    pallas_call x6 -> x8, Pallas kernels: 11.6 us -> 11.6 us  [the longest x2 5.22 us: place(): pl.pallas_call(place_kernel, grid_spec=pltpu.PrefetchScalarGridSpec(num_s...]
  transfers between devices with their start and end apart: 13 -> 14, of which waited for: 6 -> 4; matrix products, arithmetic and copies ran while one was open for 0% -> 0% of each run, Pallas kernels for 8% -> 10%
where the time goes in v3:
time: 112 us
  starting transfers between devices  58.6 us (52%)
  Pallas kernels  17.5 us (16%)
  waiting for transfers between devices  15.1 us (13%)
  blocking collectives  14.5 us (13%)
  local copies, waits for them, and re-layouts  4.54 us (4%)
    ppermute x7, starting transfers between devices, swap(): return lax.ppermute(value, axis, [(0, 1), (1, 0)])  34.8 us
    ppermute x6, starting transfers between devices, shift_x(): return lax.ppermute(value, 'x', [(i, (i + shift) % NX) for i in range(NX)])  17.8 us
    all_to_all x1, blocking collectives, exchange(): return lax.all_to_all(value, axis, 0, 0, tiled=True)  14.5 us
    ppermute x6, waiting for transfers between devices, shift_x(): return lax.ppermute(value, 'x', [(i, (i + shift) % NX) for i in range(NX)])  11.4 us
    all_to_all x1, starting transfers between devices, exchange(): return lax.all_to_all(value, axis, 0, 0, tiled=True)  6.02 us
    pallas_call x2, Pallas kernels, place(): pl.pallas_call(place_kernel, grid_spec=pltpu.PrefetchScalarGridSpec(num_s...  5.22 us
    unnamed x16, local copies, waits for them, and re-layouts  4.54 us
    pallas_call x1, Pallas kernels, states(): pl.pallas_call(state_kernel, grid_spec=pltpu.PrefetchScalarGridSpec(num_s...  4.51 us
  transfers between devices with their start and end apart: 14, of which 4 were waited for; matrix products, arithmetic and copies ran while one was open for 0% of the time, Pallas kernels for 10%

profile of v3, /device:TPU:1, one launch (start us, length us, event | category | flops | bytes accessed | tf_op | source)
XLA Modules:
  0.0 111.7 jit_solution(1350101043357473697)
XLA Ops:
  0.6 0.0 copy-start
  0.7 1.9 %copy-done = bf16[1,1,1,128,12288]{4,3,2,1,0:T(8,128)(2,1)S(1)} copy-done((bf16[1,1,1,128,12288]{4,3,2,1,0:T(8,128)(2,1)S(1)}, bf16[1,1,1,128,12288]{4,3,2,1,0:T(8,128)(2,1)}, u32[]{:S(2)}) %copy-start) | copy-done | bytes 3145752
  2.5 0.0 copy-start.5
  2.5 0.7 copy-done.5
  3.3 0.3 pack_rows.1
  3.5 8.8 %collective-permute-start = (bf16[128,6272]{1,0:T(8,128)(2,1)S(1)}, bf16[128,6272]{1,0:T(8,128)(2,1)S(1)}, u32[]{:S(2)}, u32[]{:S(2)}) collective-permute-start(bf16[128,6272]{1,0:T(8,128)(2,1)S(1)} %get-tuple-element.25), channel_id=1, source_target_pairs={{0,128},{128,0},{1,129},{129,1},{2,130},{130,2},{3,131},{131,3},{4... | collective-permute-start | bytes 4816904 | tf_op jit(solution)/shard_map/ppermute | solution.py:400
  12.3 0.1 pad_add_fusion.1.idx
  12.4 0.1 pad_add_fusion.2.idx
  12.5 0.1 pad_add_fusion.3.idx
  12.6 2.8 %collective-permute-done.there.there_scales = bf16[128,6272]{1,0:T(8,128)(2,1)S(1)} collective-permute-done((bf16[128,6272]{1,0:T(8,128)(2,1)S(1)}, bf16[128,6272]{1,0:T(8,128)(2,1)S(1)}, u32[]{:S(2)}, u32[]{:S(2)}) %collective-permute-start) | collective-permute-done | bytes 1605664 | tf_op jit(solution)/shard_map/ppermute | solution.py:400
  15.4 0.0 copy-start.1
  15.4 1.9 %copy-done.1 = bf16[1,1,1,128,12288]{4,3,2,1,0:T(8,128)(2,1)S(1)} copy-done((bf16[1,1,1,128,12288]{4,3,2,1,0:T(8,128)(2,1)S(1)}, bf16[1,1,1,128,12288]{4,3,2,1,0:T(8,128)(2,1)}, u32[]{:S(2)}) %copy-start.1) | copy-done | bytes 3145752
  17.3 1.2 %coded_chip_sum.3 = bf16[32,6272]{1,0:T(8,128)(2,1)S(1)} custom-call(s32[2]{0:T(128)S(1)} %pad_add_fusion.1.idx, bf16[128,12288]{1,0:T(8,128)(2,1)S(1)} %bitcast.24, bf16[128,128]{1,0:T(8,128)(2,1)S(1)} %get-tuple-element.24.scales, bf16[128,6272]{1,0:T(8,128)(2,1)S(1)} %collective-permute-done.there.there_scales, ...), custom_call_target="tpu_custom_call" | custom-call | flops 3932160 | bytes 1179648 | tf_op jit(solution)/shard_map/coded_chip_sum/pallas_call | solution.py:130
  18.5 1.9 %collective-permute-start.1 = (bf16[32,6272]{1,0:T(8,128)(2,1)S(1)}, bf16[32,6272]{1,0:T(8,128)(2,1)S(1)}, u32[]{:S(2)}, u32[]{:S(2)}) collective-permute-start(bf16[32,6272]{1,0:T(8,128)(2,1)S(1)} %coded_chip_sum.3), channel_id=1, source_target_pairs={{0,64},{32,96},{64,0},{96,32},{1,65},{33,97},{65,1},{97,33},{2,66}... | collective-permute-start | bytes 1204232 | tf_op jit(solution)/shard_map/ppermute | solution.py:392
  20.4 1.2 %coded_chip_sum.4 = bf16[32,6272]{1,0:T(8,128)(2,1)S(1)} custom-call(s32[2]{0:T(128)S(1)} %pad_add_fusion.2.idx, bf16[128,12288]{1,0:T(8,128)(2,1)S(1)} %bitcast.25, bf16[128,128]{1,0:T(8,128)(2,1)S(1)} %get-tuple-element.24.scales, bf16[128,6272]{1,0:T(8,128)(2,1)S(1)} %collective-permute-done.there.there_scales, ...), custom_call_target="tpu_custom_call" | custom-call | flops 3932160 | bytes 1179648 | tf_op jit(solution)/shard_map/coded_chip_sum/pallas_call | solution.py:130
  21.6 1.9 %collective-permute-start.2 = (bf16[32,6272]{1,0:T(8,128)(2,1)S(1)}, bf16[32,6272]{1,0:T(8,128)(2,1)S(1)}, u32[]{:S(2)}, u32[]{:S(2)}) collective-permute-start(bf16[32,6272]{1,0:T(8,128)(2,1)S(1)} %coded_chip_sum.4), channel_id=1, source_target_pairs={{0,32},{32,64},{64,96},{96,0},{1,33},{33,65},{65,97},{97,1},{2,34}... | collective-permute-start | bytes 1204232 | tf_op jit(solution)/shard_map/ppermute | solution.py:392
  23.5 1.2 %coded_chip_sum.5 = bf16[32,6272]{1,0:T(8,128)(2,1)S(1)} custom-call(s32[2]{0:T(128)S(1)} %pad_add_fusion.3.idx, bf16[128,12288]{1,0:T(8,128)(2,1)S(1)} %bitcast.26, bf16[128,128]{1,0:T(8,128)(2,1)S(1)} %get-tuple-element.24.scales, bf16[128,6272]{1,0:T(8,128)(2,1)S(1)} %collective-permute-done.there.there_scales, ...), custom_call_target="tpu_custom_call" | custom-call | flops 3932160 | bytes 1179648 | tf_op jit(solution)/shard_map/coded_chip_sum/pallas_call | solution.py:130
  24.7 4.6 %collective-permute-start.3 = (bf16[32,6272]{1,0:T(8,128)(2,1)S(1)}, bf16[32,6272]{1,0:T(8,128)(2,1)S(1)}, u32[]{:S(2)}, u32[]{:S(2)}) collective-permute-start(bf16[32,6272]{1,0:T(8,128)(2,1)S(1)} %coded_chip_sum.5), channel_id=1, source_target_pairs={{0,96},{32,0},{64,32},{96,64},{1,97},{33,1},{65,33},{97,65},{2,98}... | collective-permute-start | bytes 1204232 | tf_op jit(solution)/shard_map/ppermute | solution.py:392
  29.3 0.1 pad_add_fusion.idx
  29.4 0.9 own_chip_sum.1.own
  30.3 0.0 copy-start.2
  30.3 0.0 copy-start.3
  30.3 0.0 copy-start.4
  30.3 0.0 copy-start.6
  30.3 0.0 copy-start.7
  30.3 2.1 %collective-permute-done.1.c1.s1 = bf16[32,6272]{1,0:T(8,128)(2,1)S(1)} collective-permute-done((bf16[32,6272]{1,0:T(8,128)(2,1)S(1)}, bf16[32,6272]{1,0:T(8,128)(2,1)S(1)}, u32[]{:S(2)}, u32[]{:S(2)}) %collective-permute-start.1) | collective-permute-done | bytes 401440 | tf_op jit(solution)/shard_map/ppermute | solution.py:392
  32.4 9.3 %collective-permute-done.2.c2.s2 = bf16[32,6272]{1,0:T(8,128)(2,1)S(1)} collective-permute-done((bf16[32,6272]{1,0:T(8,128)(2,1)S(1)}, bf16[32,6272]{1,0:T(8,128)(2,1)S(1)}, u32[]{:S(2)}, u32[]{:S(2)}) %collective-permute-start.2) | collective-permute-done | bytes 401440 | tf_op jit(solution)/shard_map/ppermute | solution.py:392
  41.7 0.0 collective-permute-done.3.c3.s3
  41.7 1.3 %sum_over_x.1 = bf16[16,4,3200]{2,1,0:T(4,128)(2,1)S(1)} custom-call(f32[32,6144]{1,0:T(8,128)S(1)} %own_chip_sum.1.own, bf16[32,6272]{1,0:T(8,128)(2,1)S(1)} %collective-permute-done.1.c1.s1, bf16[32,6272]{1,0:T(8,128)(2,1)S(1)} %collective-permute-done.1.c1.s1, bf16[32,6272]{1,0:T(8,128)(2,1)S(1)} %collective-permute-done.2.c2.s2, ...), custom_call_target="tpu_custom_call" | custom-call | flops 11796480 | bytes 2359296 | tf_op jit(solution)/shard_map/sum_over_x/pallas_call | solution.py:185
  43.0 14.5 %all_to_all.10.codes.scales = bf16[16,4,3200]{2,1,0:T(4,128)(2,1)S(1)} all-to-all(bf16[16,4,3200]{2,1,0:T(4,128)(2,1)S(1)} %sum_over_x.1), channel_id=1, replica_groups=mesh['zl'=2,'c'=2,'x'=4,'y'=8,'zh'=4] {'zl','y'}, dimensions={0} | all-to-all | bytes 819200 | tf_op jit(solution)/shard_map/all_to_all | solution.py:396
  57.5 0.6 sum_over_zy.1.grad
  58.1 2.2 %collective-permute-start.4 = (f32[4,3072]{1,0:T(4,128)S(1)}, f32[4,3072]{1,0:T(4,128)S(1)}, u32[]{:S(2)}, u32[]{:S(2)}) collective-permute-start(f32[4,3072]{1,0:T(4,128)S(1)} %sum_over_zy.1.grad), channel_id=1, source_target_pairs={{0,256},{256,0},{1,257},{257,1},{2,258},{258,2},{3,259},{259,3},{4... | collective-permute-start | bytes 147464 | tf_op jit(solution)/shard_map/ppermute | solution.py:400
  60.4 0.0 copy-done.2
  60.4 0.0 copy-done.3
  60.4 0.0 copy-done.4
  60.4 0.0 copy-done.6
  60.4 0.0 copy-done.7
  60.4 1.1 low_weights.1
  61.5 6.0 %all-to-all-start.1 = ((bf16[16,4,3072]{2,1,0:T(4,128)(2,1)}), bf16[16,4,3072]{2,1,0:T(4,128)(2,1)S(1)}, u32[]{:S(2)}, u32[]{:S(2)}) async-start(bf16[16,4,3072]{2,1,0:T(4,128)(2,1)} %low_weights.1), calls=%async_computation.1 | async-start | bytes 786432 | tf_op jit(solution)/shard_map/all_to_all | solution.py:396
  67.6 0.0 collective-permute-done.4
  67.6 4.0 %collective-permute-start.5 = (f32[4,6144]{1,0:T(4,128)S(1)}, f32[4,6144]{1,0:T(4,128)S(1)}, u32[]{:S(2)}, u32[]{:S(2)}) collective-permute-start(f32[4,6144]{1,0:T(4,128)S(1)} %pad_maximum_fusion.mine), channel_id=1, source_target_pairs={{0,128},{128,0},{1,129},{129,1},{2,130},{130,2},{3,131},{131,3},{4... | collective-permute-start | bytes 294920 | tf_op jit(solution)/shard_map/ppermute | solution.py:400
  71.7 0.9 collective-permute-done.5.other
  72.6 4.5 %new_states.1 = (f32[4,12288]{1,0:T(4,128)}, bf16[4,12288]{1,0:T(4,128)(2,1)}, f32[4,96]{1,0:T(4,128)}, bf16[4,12288]{1,0:T(4,128)(2,1)}, f32[4,96]{1,0:T(4,128)}) custom-call(s32[1]{0:T(128)} %bitcast.2.idx, f32[4,6144]{1,0:T(4,128)S(1)} %pad_maximum_fusion.mine, f32[4,6144]{1,0:T(4,128)S(1)} %collective-permute-done.5.other, f32[4,12288]{1,0:T(4,128)S(1)} %bitcast.29, ...), custom_call_target="tpu_custom_call" | custom-call | flops 2949120 | bytes 983040 | tf_op jit(solution)/shard_map/new_states/pallas_call | solution.py:324
  77.1 0.0 all-to-all-done.1.refs_0_
  77.1 4.0 %collective-permute-start.11 = (bf16[16,4,3072]{2,1,0:T(4,128)(2,1)S(1)}, bf16[16,4,3072]{2,1,0:T(4,128)(2,1)S(1)}, u32[]{:S(2)}, u32[]{:S(2)}) collective-permute-start(bf16[16,4,3072]{2,1,0:T(4,128)(2,1)S(1)} %all-to-all-done.1.refs_0_), channel_id=1, source_target_pairs={{0,96},{32,0},{64,32},{96,64},{1,97},{33,1},{65,33},{97,65},{2,98}... | collective-permute-start | bytes 1179656 | tf_op jit(solution)/shard_map/ppermute | solution.py:392
  81.1 2.8 %collective-permute-start.9 = (bf16[16,4,3072]{2,1,0:T(4,128)(2,1)S(1)}, bf16[16,4,3072]{2,1,0:T(4,128)(2,1)S(1)}, u32[]{:S(2)}, u32[]{:S(2)}) collective-permute-start(bf16[16,4,3072]{2,1,0:T(4,128)(2,1)S(1)} %all-to-all-done.1.refs_0_), channel_id=1, source_target_pairs={{0,64},{32,96},{64,0},{96,32},{1,65},{33,97},{65,1},{97,33},{2,66}... | collective-permute-start | bytes 1179656 | tf_op jit(solution)/shard_map/ppermute | solution.py:392
  83.9 2.6 %collective-permute-start.7 = (bf16[16,4,3072]{2,1,0:T(4,128)(2,1)S(1)}, bf16[16,4,3072]{2,1,0:T(4,128)(2,1)S(1)}, u32[]{:S(2)}, u32[]{:S(2)}) collective-permute-start(bf16[16,4,3072]{2,1,0:T(4,128)(2,1)S(1)} %all-to-all-done.1.refs_0_), channel_id=1, source_target_pairs={{0,32},{32,64},{64,96},{96,0},{1,33},{33,65},{65,97},{97,1},{2,34}... | collective-permute-start | bytes 1179656 | tf_op jit(solution)/shard_map/ppermute | solution.py:392
  86.5 6.6 %collective-permute-start.6 = (bf16[16,4,3072]{2,1,0:T(4,128)(2,1)S(1)}, bf16[16,4,3072]{2,1,0:T(4,128)(2,1)S(1)}, u32[]{:S(2)}, u32[]{:S(2)}) collective-permute-start(bf16[16,4,3072]{2,1,0:T(4,128)(2,1)S(1)} %all-to-all-done.1.refs_0_), channel_id=1, source_target_pairs={{0,128},{128,0},{1,129},{129,1},{2,130},{130,2},{3,131},{131,3},{4... | collective-permute-start | bytes 1179656 | tf_op jit(solution)/shard_map/ppermute | solution.py:400
  93.1 0.0 collective-permute-done.11.refs_3_
  93.1 7.6 %collective-permute-start.12 = (bf16[16,4,3072]{2,1,0:T(4,128)(2,1)S(1)}, bf16[16,4,3072]{2,1,0:T(4,128)(2,1)S(1)}, u32[]{:S(2)}, u32[]{:S(2)}) collective-permute-start(bf16[16,4,3072]{2,1,0:T(4,128)(2,1)S(1)} %collective-permute-done.11.refs_3_), channel_id=1, source_target_pairs={{0,128},{128,0},{1,129},{129,1},{2,130},{130,2},{3,131},{131,3},{4... | collective-permute-start | bytes 1179656 | tf_op jit(solution)/shard_map/ppermute | solution.py:400
  100.7 0.0 collective-permute-done.9.refs_2_
  100.7 1.9 %collective-permute-start.10 = (bf16[16,4,3072]{2,1,0:T(4,128)(2,1)S(1)}, bf16[16,4,3072]{2,1,0:T(4,128)(2,1)S(1)}, u32[]{:S(2)}, u32[]{:S(2)}) collective-permute-start(bf16[16,4,3072]{2,1,0:T(4,128)(2,1)S(1)} %collective-permute-done.9.refs_2_), channel_id=1, source_target_pairs={{0,128},{128,0},{1,129},{129,1},{2,130},{130,2},{3,131},{131,3},{4... | collective-permute-start | bytes 1179656 | tf_op jit(solution)/shard_map/ppermute | solution.py:400
  102.7 0.0 collective-permute-done.7.refs_1_
  102.7 3.6 %collective-permute-start.8 = (bf16[16,4,3072]{2,1,0:T(4,128)(2,1)S(1)}, bf16[16,4,3072]{2,1,0:T(4,128)(2,1)S(1)}, u32[]{:S(2)}, u32[]{:S(2)}) collective-permute-start(bf16[16,4,3072]{2,1,0:T(4,128)(2,1)S(1)} %collective-permute-done.7.refs_1_), channel_id=1, source_target_pairs={{0,128},{128,0},{1,129},{129,1},{2,130},{130,2},{3,131},{131,3},{4... | collective-permute-start | bytes 1179656 | tf_op jit(solution)/shard_map/ppermute | solution.py:400
  106.3 0.1 pad_add_fusion.5.idx
  106.4 0.1 pad_add_fusion.4.idx
  106.5 2.6 %place_weights.2 = (bf16[128,12288]{1,0:T(8,128)(2,1)}, bf16[12288,128]{1,0:T(8,128)(2,1)}) custom-call(s32[2]{0:T(128)S(1)} %pad_add_fusion.5.idx, bf16[16,4,3072]{2,1,0:T(4,128)(2,1)S(1)} %all-to-all-done.1.refs_0_, bf16[16,4,3072]{2,1,0:T(4,128)(2,1)S(1)} %collective-permute-done.7.refs_1_, bf16[16,4,3072]{2,1,0:T(4,128)(2,1)S(1)} %collective-permute-done.9.refs_2_, ...), custom_call_target="tpu_custom_call" | custom-call | bytes 4718592 | tf_op jit(solution)/shard_map/place_weights/pallas_call | solution.py:368
  109.1 0.0 collective-permute-done.6.refs_0_
  109.1 0.0 collective-permute-done.12.refs_3_
  109.1 0.0 collective-permute-done.10.refs_2_
  109.1 0.0 collective-permute-done.8.refs_1_
  109.1 2.6 %place_weights.3 = (bf16[128,12288]{1,0:T(8,128)(2,1)}, bf16[12288,128]{1,0:T(8,128)(2,1)}) custom-call(s32[2]{0:T(128)S(1)} %pad_add_fusion.4.idx, bf16[16,4,3072]{2,1,0:T(4,128)(2,1)S(1)} %collective-permute-done.6.refs_0_, bf16[16,4,3072]{2,1,0:T(4,128)(2,1)S(1)} %collective-permute-done.8.refs_1_, ...), custom_call_target="tpu_custom_call", output_to_operand_aliasing={{0}: (5, {}), {1}: (6, {})} | custom-call | bytes 4718592 | tf_op jit(solution)/shard_map/place_weights/pallas_call | solution.py:368
  (2 shorter events, 0.0 us)
Async XLA Ops:
  0.6 1.9 %copy-start = (bf16[1,1,1,128,12288]{4,3,2,1,0:T(8,128)(2,1)S(1)}, bf16[1,1,1,128,12288]{4,3,2,1,0:T(8,128)(2,1)}, u32[]{:S(2)}) copy-start(bf16[1,1,1,128,12288]{4,3,2,1,0:T(8,128)(2,1)} %param.7) | copy-start | bytes 9437188
  2.5 0.7 copy-start.5
  3.5 11.9 %collective-permute-start = (bf16[128,6272]{1,0:T(8,128)(2,1)S(1)}, bf16[128,6272]{1,0:T(8,128)(2,1)S(1)}, u32[]{:S(2)}, u32[]{:S(2)}) collective-permute-start(bf16[128,6272]{1,0:T(8,128)(2,1)S(1)} %get-tuple-element.25), channel_id=1, source_target_pairs={{0,128},{128,0},{1,129},{129,1},{2,130},{130,2},{3,131},{131,3},{4... | collective-permute-start | bytes 4816904 | tf_op jit(solution)/shard_map/ppermute | solution.py:400
  15.4 1.9 %copy-start.1 = (bf16[1,1,1,128,12288]{4,3,2,1,0:T(8,128)(2,1)S(1)}, bf16[1,1,1,128,12288]{4,3,2,1,0:T(8,128)(2,1)}, u32[]{:S(2)}) copy-start(bf16[1,1,1,128,12288]{4,3,2,1,0:T(8,128)(2,1)} %param.7) | copy-start | bytes 9437188
  18.5 13.9 %collective-permute-start.1 = (bf16[32,6272]{1,0:T(8,128)(2,1)S(1)}, bf16[32,6272]{1,0:T(8,128)(2,1)S(1)}, u32[]{:S(2)}, u32[]{:S(2)}) collective-permute-start(bf16[32,6272]{1,0:T(8,128)(2,1)S(1)} %coded_chip_sum.3), channel_id=1, source_target_pairs={{0,64},{32,96},{64,0},{96,32},{1,65},{33,97},{65,1},{97,33},{2,66}... | collective-permute-start | bytes 1204232 | tf_op jit(solution)/shard_map/ppermute | solution.py:392
  21.6 20.1 %collective-permute-start.2 = (bf16[32,6272]{1,0:T(8,128)(2,1)S(1)}, bf16[32,6272]{1,0:T(8,128)(2,1)S(1)}, u32[]{:S(2)}, u32[]{:S(2)}) collective-permute-start(bf16[32,6272]{1,0:T(8,128)(2,1)S(1)} %coded_chip_sum.4), channel_id=1, source_target_pairs={{0,32},{32,64},{64,96},{96,0},{1,33},{33,65},{65,97},{97,1},{2,34}... | collective-permute-start | bytes 1204232 | tf_op jit(solution)/shard_map/ppermute | solution.py:392
  24.7 17.0 %collective-permute-start.3 = (bf16[32,6272]{1,0:T(8,128)(2,1)S(1)}, bf16[32,6272]{1,0:T(8,128)(2,1)S(1)}, u32[]{:S(2)}, u32[]{:S(2)}) collective-permute-start(bf16[32,6272]{1,0:T(8,128)(2,1)S(1)} %coded_chip_sum.5), channel_id=1, source_target_pairs={{0,96},{32,0},{64,32},{96,64},{1,97},{33,1},{65,33},{97,65},{2,98}... | collective-permute-start | bytes 1204232 | tf_op jit(solution)/shard_map/ppermute | solution.py:392
  30.3 30.1 %copy-start.2 = (f32[1,4,12288]{2,1,0:T(4,128)S(1)}, f32[1,4,12288]{2,1,0:T(4,128)}, u32[]{:S(2)}) copy-start(f32[1,4,12288]{2,1,0:T(4,128)} %param.9) | copy-start | bytes 589828
  30.3 30.1 %copy-start.3 = (bf16[1,4,12288]{2,1,0:T(4,128)(2,1)S(1)}, bf16[1,4,12288]{2,1,0:T(4,128)(2,1)}, u32[]{:S(2)}) copy-start(bf16[1,4,12288]{2,1,0:T(4,128)(2,1)} %param.10) | copy-start | bytes 294916
  30.3 30.1 %copy-start.4 = (bf16[1,4,12288]{2,1,0:T(4,128)(2,1)S(1)}, bf16[1,4,12288]{2,1,0:T(4,128)(2,1)}, u32[]{:S(2)}) copy-start(bf16[1,4,12288]{2,1,0:T(4,128)(2,1)} %param.12) | copy-start | bytes 294916
  30.3 30.1 %copy-start.6 = (f32[1,4,96]{2,1,0:T(4,128)S(1)}, f32[1,4,96]{2,1,0:T(4,128)}, u32[]{:S(2)}) copy-start(f32[1,4,96]{2,1,0:T(4,128)} %param.11) | copy-start | bytes 4612
  30.3 30.1 %copy-start.7 = (f32[1,4,96]{2,1,0:T(4,128)S(1)}, f32[1,4,96]{2,1,0:T(4,128)}, u32[]{:S(2)}) copy-start(f32[1,4,96]{2,1,0:T(4,128)} %param.13) | copy-start | bytes 4612
  58.1 9.4 %collective-permute-start.4 = (f32[4,3072]{1,0:T(4,128)S(1)}, f32[4,3072]{1,0:T(4,128)S(1)}, u32[]{:S(2)}, u32[]{:S(2)}) collective-permute-start(f32[4,3072]{1,0:T(4,128)S(1)} %sum_over_zy.1.grad), channel_id=1, source_target_pairs={{0,256},{256,0},{1,257},{257,1},{2,258},{258,2},{3,259},{259,3},{4... | collective-permute-start | bytes 147464 | tf_op jit(solution)/shard_map/ppermute | solution.py:400
  61.5 15.6 %all-to-all-start.1 = ((bf16[16,4,3072]{2,1,0:T(4,128)(2,1)}), bf16[16,4,3072]{2,1,0:T(4,128)(2,1)S(1)}, u32[]{:S(2)}, u32[]{:S(2)}) async-start(bf16[16,4,3072]{2,1,0:T(4,128)(2,1)} %low_weights.1), calls=%async_computation.1 | async-start | bytes 786432 | tf_op jit(solution)/shard_map/all_to_all | solution.py:396
  67.6 5.0 %collective-permute-start.5 = (f32[4,6144]{1,0:T(4,128)S(1)}, f32[4,6144]{1,0:T(4,128)S(1)}, u32[]{:S(2)}, u32[]{:S(2)}) collective-permute-start(f32[4,6144]{1,0:T(4,128)S(1)} %pad_maximum_fusion.mine), channel_id=1, source_target_pairs={{0,128},{128,0},{1,129},{129,1},{2,130},{130,2},{3,131},{131,3},{4... | collective-permute-start | bytes 294920 | tf_op jit(solution)/shard_map/ppermute | solution.py:400
  77.1 16.0 %collective-permute-start.11 = (bf16[16,4,3072]{2,1,0:T(4,128)(2,1)S(1)}, bf16[16,4,3072]{2,1,0:T(4,128)(2,1)S(1)}, u32[]{:S(2)}, u32[]{:S(2)}) collective-permute-start(bf16[16,4,3072]{2,1,0:T(4,128)(2,1)S(1)} %all-to-all-done.1.refs_0_), channel_id=1, source_target_pairs={{0,96},{32,0},{64,32},{96,64},{1,97},{33,1},{65,33},{97,65},{2,98}... | collective-permute-start | bytes 1179656 | tf_op jit(solution)/shard_map/ppermute | solution.py:392
  81.1 19.7 %collective-permute-start.9 = (bf16[16,4,3072]{2,1,0:T(4,128)(2,1)S(1)}, bf16[16,4,3072]{2,1,0:T(4,128)(2,1)S(1)}, u32[]{:S(2)}, u32[]{:S(2)}) collective-permute-start(bf16[16,4,3072]{2,1,0:T(4,128)(2,1)S(1)} %all-to-all-done.1.refs_0_), channel_id=1, source_target_pairs={{0,64},{32,96},{64,0},{96,32},{1,65},{33,97},{65,1},{97,33},{2,66}... | collective-permute-start | bytes 1179656 | tf_op jit(solution)/shard_map/ppermute | solution.py:392
  83.9 18.8 %collective-permute-start.7 = (bf16[16,4,3072]{2,1,0:T(4,128)(2,1)S(1)}, bf16[16,4,3072]{2,1,0:T(4,128)(2,1)S(1)}, u32[]{:S(2)}, u32[]{:S(2)}) collective-permute-start(bf16[16,4,3072]{2,1,0:T(4,128)(2,1)S(1)} %all-to-all-done.1.refs_0_), channel_id=1, source_target_pairs={{0,32},{32,64},{64,96},{96,0},{1,33},{33,65},{65,97},{97,1},{2,34}... | collective-permute-start | bytes 1179656 | tf_op jit(solution)/shard_map/ppermute | solution.py:392
  86.5 22.6 %collective-permute-start.6 = (bf16[16,4,3072]{2,1,0:T(4,128)(2,1)S(1)}, bf16[16,4,3072]{2,1,0:T(4,128)(2,1)S(1)}, u32[]{:S(2)}, u32[]{:S(2)}) collective-permute-start(bf16[16,4,3072]{2,1,0:T(4,128)(2,1)S(1)} %all-to-all-done.1.refs_0_), channel_id=1, source_target_pairs={{0,128},{128,0},{1,129},{129,1},{2,130},{130,2},{3,131},{131,3},{4... | collective-permute-start | bytes 1179656 | tf_op jit(solution)/shard_map/ppermute | solution.py:400
  93.1 16.0 %collective-permute-start.12 = (bf16[16,4,3072]{2,1,0:T(4,128)(2,1)S(1)}, bf16[16,4,3072]{2,1,0:T(4,128)(2,1)S(1)}, u32[]{:S(2)}, u32[]{:S(2)}) collective-permute-start(bf16[16,4,3072]{2,1,0:T(4,128)(2,1)S(1)} %collective-permute-done.11.refs_3_), channel_id=1, source_target_pairs={{0,128},{128,0},{1,129},{129,1},{2,130},{130,2},{3,131},{131,3},{4... | collective-permute-start | bytes 1179656 | tf_op jit(solution)/shard_map/ppermute | solution.py:400
  100.7 8.3 %collective-permute-start.10 = (bf16[16,4,3072]{2,1,0:T(4,128)(2,1)S(1)}, bf16[16,4,3072]{2,1,0:T(4,128)(2,1)S(1)}, u32[]{:S(2)}, u32[]{:S(2)}) collective-permute-start(bf16[16,4,3072]{2,1,0:T(4,128)(2,1)S(1)} %collective-permute-done.9.refs_2_), channel_id=1, source_target_pairs={{0,128},{128,0},{1,129},{129,1},{2,130},{130,2},{3,131},{131,3},{4... | collective-permute-start | bytes 1179656 | tf_op jit(solution)/shard_map/ppermute | solution.py:400
  102.7 6.4 %collective-permute-start.8 = (bf16[16,4,3072]{2,1,0:T(4,128)(2,1)S(1)}, bf16[16,4,3072]{2,1,0:T(4,128)(2,1)S(1)}, u32[]{:S(2)}, u32[]{:S(2)}) collective-permute-start(bf16[16,4,3072]{2,1,0:T(4,128)(2,1)S(1)} %collective-permute-done.7.refs_1_), channel_id=1, source_target_pairs={{0,128},{128,0},{1,129},{129,1},{2,130},{130,2},{3,131},{131,3},{4... | collective-permute-start | bytes 1179656 | tf_op jit(solution)/shard_map/ppermute | solution.py:400

commit v4 on v3

--- a/solution.py
+++ b/solution.py
@@ -20,6 +20,7 @@
 QB = NB // 4
 PAD = HALF + BLOCK
 QPAD = QUARTER + BLOCK
+CH = 3072
 SPAN = 172.0
 OFFSET = 86.0
 
@@ -57,41 +58,41 @@
     return jnp.maximum(peak * (1.0 + 2.0**-7), 1e-30).astype(bf16)
 
 
-def pack_kernel(idx, values, scales, out, own):
-    rows = scales[...].astype(f32).T
-    low, high = rows[:, :HB], rows[:, HB:NB]
-    pad = jnp.zeros((ROWS, BLOCK - HB), bf16)
-    first = idx[0] == 0
-    out[:, :HALF] = values[...]
-    out[:, HALF : HALF + HB] = jnp.where(first, low, high).astype(bf16)
-    out[:, HALF + HB :] = pad
-    own[:, :HB] = jnp.where(first, high, low).astype(bf16)
-    own[:, HB:] = pad
-
-
-def pack(half, values, scales):
+def pack_kernel(idx, v0, v1, v2, v3, scales, out, rows):
+    rows[...] = scales[...].astype(f32).T
+    pad = jnp.zeros((XR, BLOCK - HB), bf16)
+    for k, values in enumerate((v0, v1, v2, v3)):
+        start = pl.multiple_of(idx[1 + k] * XR, XR)
+        block = rows[pl.ds(start, XR), :]
+        chosen = jnp.where(idx[0] == 0, block[:, :HB], block[:, HB:])
+        out[k, :, :HALF] = values[...]
+        out[k, :, HALF : HALF + HB] = chosen.astype(bf16)
+        out[k, :, HALF + HB :] = pad
+
+
+def pack(idx, values, scales, name):
+    values = in_hbm(values)
+    rows = [
+        pl.BlockSpec((XR, HALF), lambda i, s, k=k: (s[1 + k], s[0])) for k in range(NX)
+    ]
     return pl.pallas_call(
         pack_kernel,
         grid_spec=pltpu.PrefetchScalarGridSpec(
             num_scalar_prefetch=1,
             grid=(1,),
-            in_specs=[
-                pl.BlockSpec((ROWS, HALF), lambda i, s: (0, s[0])),
-                pl.BlockSpec((NB, ROWS), lambda i, s: (0, 0)),
-            ],
-            out_specs=[
-                pl.BlockSpec((ROWS, PAD), lambda i, s: (0, 0)),
-                pl.BlockSpec((ROWS, BLOCK), lambda i, s: (0, 0)),
-            ],
+            in_specs=rows + [pl.BlockSpec((NB, ROWS), lambda i, s: (0, 0))],
+            out_specs=pl.BlockSpec((NX, XR, PAD), lambda i, s: (0, 0, 0)),
+            scratch_shapes=[pltpu.VMEM((ROWS, NB), f32)],
         ),
-        out_shape=[
-            jax.ShapeDtypeStruct((ROWS, PAD), bf16),
-            jax.ShapeDtypeStruct((ROWS, BLOCK), bf16),
-        ],
-        compiler_params=params(),
-        cost_estimate=cost(0, 2 * ROWS * HALF * 2),
-        name="pack_rows",
-    )(half, values, scales)
+        out_shape=jax.ShapeDtypeStruct((NX, XR, PAD), bf16),
+        compiler_params=params(),
+        cost_estimate=cost(0, 4 * ROWS * HALF * 2),
+        name=name,
+    )(idx, *([values] * NX), in_hbm(scales))
+
+
+def in_hbm(value):
+    return pltpu.with_memory_space_constraint(value, pltpu.HBM)
 
 
 def add_cores(values, scales, there, there_scales, totals):
@@ -107,7 +108,7 @@
     return peak
 
 
-def code_kernel(idx, values, scales, there, there_scales, out, totals):
+def code_kernel(values, scales, there, there_scales, out, totals):
     scale = scale_of(add_cores(values, scales, there, there_scales, totals))
     out[:, HALF:] = scale
     factor = SPAN / scale.astype(f32)
@@ -116,36 +117,30 @@
         out[:, cols] = encode(totals[:, cols], factor).astype(bf16)
 
 
-def own_kernel(idx, values, scales, there, there_scales, out):
+def own_kernel(values, scales, there, there_scales, out):
     add_cores(values, scales, there, there_scales, out)
 
 
-def chip_sum(idx, values, scales, there, coded):
+def chip_sum(k, own, there, coded):
     if coded:
         kernel, width, kind, name = code_kernel, PAD, bf16, "coded_chip_sum"
         scratch = [pltpu.VMEM((XR, HALF), f32)]
     else:
         kernel, width, kind, name = own_kernel, HALF, f32, "own_chip_sum"
         scratch = []
+    value = pl.BlockSpec((None, XR, HALF), lambda i: (k, 0, 0))
+    scale = pl.BlockSpec((None, XR, BLOCK), lambda i: (k, 0, HB))
     return pl.pallas_call(
         kernel,
-        grid_spec=pltpu.PrefetchScalarGridSpec(
-            num_scalar_prefetch=1,
-            grid=(1,),
-            in_specs=[
-                pl.BlockSpec((XR, HALF), lambda i, s: (s[0], s[1])),
-                pl.BlockSpec((XR, BLOCK), lambda i, s: (s[0], 0)),
-                pl.BlockSpec((XR, HALF), lambda i, s: (s[0], 0)),
-                pl.BlockSpec((XR, BLOCK), lambda i, s: (s[0], HB)),
-            ],
-            out_specs=pl.BlockSpec((XR, width), lambda i, s: (0, 0)),
-            scratch_shapes=scratch,
-        ),
+        grid=(1,),
+        in_specs=[value, scale, value, scale],
+        out_specs=pl.BlockSpec((XR, width), lambda i: (0, 0)),
+        scratch_shapes=scratch,
         out_shape=jax.ShapeDtypeStruct((XR, width), kind),
         compiler_params=params(),
         cost_estimate=cost(20 * XR * HALF, 6 * XR * HALF),
         name=name,
-    )(idx, values, scales, there, there)
+    )(own, own, there, there)
 
 
 def row_kernel(own, c1, s1, c2, s2, c3, s3, out, totals):
@@ -195,32 +190,6 @@
     )(*args)
 
 
-def last_kernel(codes, scales, out):
-    parts = NZ * NY * YR
-    step = scales[...].astype(f32).reshape(parts, BLOCK) * (1.0 / SPAN)
-    for b in range(QB):
-        cols = slice(b * BLOCK, (b + 1) * BLOCK)
-        code = codes[:, :, cols].astype(f32).reshape(parts, BLOCK)
-        term = decode(code, step)
-        out[:, cols] = jnp.sum(term.reshape(NZ * NY, YR, BLOCK), axis=0)
-
-
-def last_sum(codes):
-    return pl.pallas_call(
-        last_kernel,
-        grid=(1,),
-        in_specs=[
-            pl.BlockSpec((NZ * NY, YR, QUARTER), lambda i: (0, 0, 0)),
-            pl.BlockSpec((NZ * NY, YR, BLOCK), lambda i: (0, 0, QB)),
-        ],
-        out_specs=pl.BlockSpec((YR, QUARTER), lambda i: (0, 0)),
-        out_shape=jax.ShapeDtypeStruct((YR, QUARTER), f32),
-        compiler_params=params(),
-        cost_estimate=cost(20 * XR * HALF, 3 * XR * HALF),
-        name="sum_over_zy",
-    )(codes, codes)
-
-
 def adam(gradient, master, first_old, second_old):
     first = beta_one * first_old + (1.0 - beta_one) * gradient
     second = beta_two * second_old + (1.0 - beta_two) * gradient * gradient
@@ -228,7 +197,7 @@
     return first, second, master - rate * direction
 
 
-def low_kernel(idx, grad, master, fm, fs, sm, ss, low_out):
+def low_kernel(idx, codes, steps, master, fm, fs, sm, ss, grad_out, low_out):
     def chosen(ref):
         scales = ref[...]
         parts = [scales[:, k * QB : (k + 1) * QB] for k in range(4)]
@@ -236,34 +205,53 @@
         high = jnp.where(idx[0] == 2, parts[2], parts[3])
         return jnp.where(idx[0] < 2, low, high)
 
+    parts = NZ * NY * YR
+    step = steps[...].astype(f32).reshape(parts, BLOCK) * (1.0 / SPAN)
     fscale, sscale = chosen(fs), chosen(ss)
     for b in range(QB):
         cols = slice(b * BLOCK, (b + 1) * BLOCK)
+        code = codes[:, :, cols].astype(f32).reshape(parts, BLOCK)
+        term = decode(code, step).reshape(NZ * NY, YR, BLOCK)
+        gradient = jnp.sum(term, axis=0)
+        grad_out[:, cols] = gradient
         first_old = fm[:, cols].astype(f32) * fscale[:, b : b + 1]
         second_old = sm[:, cols].astype(f32) * sscale[:, b : b + 1]
-        _, _, updated = adam(grad[:, cols], master[:, cols], first_old, second_old)
+        _, _, updated = adam(gradient, master[:, cols], first_old, second_old)
         low = updated.astype(bf16)
         for i in range(NZ * NY):
             low_out[i, :, cols] = low
 
 
-def low_weights(quarter, grad, master, fm, fs, sm, ss):
+def low_weights(quarter, codes, master, fm, fs, sm, ss):
     part = pl.BlockSpec((YR, QUARTER), lambda i, s: (0, s[0]))
-    whole = pl.BlockSpec((YR, QUARTER), lambda i, s: (0, 0))
     scale = pl.BlockSpec((YR, NB), lambda i, s: (0, 0))
     return pl.pallas_call(
         low_kernel,
         grid_spec=pltpu.PrefetchScalarGridSpec(
             num_scalar_prefetch=1,
             grid=(1,),
-            in_specs=[whole, part, part, scale, part, scale],
-            out_specs=pl.BlockSpec((NZ * NY, YR, QUARTER), lambda i, s: (0, 0, 0)),
+            in_specs=[
+                pl.BlockSpec((NZ * NY, YR, QUARTER), lambda i, s: (0, 0, 0)),
+                pl.BlockSpec((NZ * NY, YR, BLOCK), lambda i, s: (0, 0, QB)),
+                part,
+                part,
+                scale,
+                part,
+                scale,
+            ],
+            out_specs=[
+                pl.BlockSpec((YR, QUARTER), lambda i, s: (0, 0)),
+                pl.BlockSpec((NZ * NY, YR, QUARTER), lambda i, s: (0, 0, 0)),
+            ],
         ),
-        out_shape=jax.ShapeDtypeStruct((NZ * NY, YR, QUARTER), bf16),
-        compiler_params=params(),
-        cost_estimate=cost(30 * YR * QUARTER, 40 * YR * QUARTER),
-        name="low_weights",
-    )(quarter, grad, master, fm, fs, sm, ss)
+        out_shape=[
+            jax.ShapeDtypeStruct((YR, QUARTER), f32),
+            jax.ShapeDtypeStruct((NZ * NY, YR, QUARTER), bf16),
+        ],
+        compiler_params=params(),
+        cost_estimate=cost(30 * XR * HALF, 8 * XR * HALF),
+        name="sum_and_low_weights",
+    )(quarter, codes, codes, master, fm, fs, sm, ss)
 
 
 def state_kernel(
@@ -338,54 +326,62 @@
             shape((YR, NB), f32),
         ],
         compiler_params=params(),
-        cost_estimate=cost(60 * YR * D, 20 * YR * D),
+        cost_estimate=cost(YR * D, YR * D),
         name="new_states",
     )(core, mine, other, master, fm, fs, sm, ss)
 
 
-def place_kernel(idx, *refs):
-    pieces, (weights, transposed, rows) = refs[:NX], refs[-3:]
-    for shift, ref in enumerate(pieces):
-        start = pl.multiple_of(lax.rem(idx[1] + NX - shift, NX) * XR, XR)
-        low = ref[...].astype(f32).reshape(XR, QUARTER).astype(bf16)
-        rows[pl.ds(start, XR), :] = low
-    low = rows[...]
+def spread_kernel(low, out):
+    for z in range(NZ):
+        cols = slice(z * QUARTER, (z + 1) * QUARTER)
+        rows = low[z * NY : (z + 1) * NY].astype(f32).reshape(XR, QUARTER)
+        for k in range(NX):
+            out[k, :, cols] = rows.astype(bf16)
+
+
+def spread(low):
+    return pl.pallas_call(
+        spread_kernel,
+        grid=(1,),
+        in_specs=[pl.BlockSpec((NZ * NY, YR, QUARTER), lambda i: (0, 0, 0))],
+        out_specs=pl.BlockSpec((NX, XR, HALF), lambda i: (0, 0, 0)),
+        out_shape=jax.ShapeDtypeStruct((NX, XR, HALF), bf16),
+        compiler_params=params(),
+        cost_estimate=cost(0, 10 * XR * HALF),
+        name="spread_rows",
+    )(low)
+
+
+def place_kernel(idx, piece, *refs):
+    weights, transposed = refs[-2:]
+    low = piece[...].reshape(ROWS, CH)
     weights[...] = low
     transposed[...] = low.T
 
 
-def place(idx, pieces, before=()):
-    ins, args = [], []
-    for piece in pieces:
-        if isinstance(piece, tuple):
-            k, piece = piece
-            ins.append(
-                pl.BlockSpec((None, NY, YR, QUARTER), lambda j, s, k=k: (k, j, 0, 0))
-            )
-        else:
-            ins.append(pl.BlockSpec((NY, YR, QUARTER), lambda j, s: (j, 0, 0)))
-        args.append(piece)
+def place(half, piece, before=()):
+    steps = HALF // CH
     return pl.pallas_call(
         place_kernel,
         grid_spec=pltpu.PrefetchScalarGridSpec(
             num_scalar_prefetch=1,
-            grid=(NZ,),
-            in_specs=ins + [pl.BlockSpec(memory_space=pl.ANY)] * len(before),
+            grid=(steps,),
+            in_specs=[pl.BlockSpec((NX, XR, CH), lambda j, s: (0, 0, j))]
+            + [pl.BlockSpec(memory_space=pl.ANY)] * len(before),
             out_specs=[
-                pl.BlockSpec((ROWS, QUARTER), lambda j, s: (0, s[0] * NZ + j)),
-                pl.BlockSpec((QUARTER, ROWS), lambda j, s: (s[0] * NZ + j, 0)),
+                pl.BlockSpec((ROWS, CH), lambda j, s: (0, s[0] * steps + j)),
+                pl.BlockSpec((CH, ROWS), lambda j, s: (s[0] * steps + j, 0)),
             ],
-            scratch_shapes=[pltpu.VMEM((ROWS, QUARTER), bf16)],
         ),
         out_shape=[
             jax.ShapeDtypeStruct((ROWS, D), bf16),
             jax.ShapeDtypeStruct((D, ROWS), bf16),
         ],
-        input_output_aliases={1 + NX: 0, 2 + NX: 1} if before else {},
+        input_output_aliases={2: 0, 3: 1} if before else {},
         compiler_params=params(),
         cost_estimate=cost(0, 3 * ROWS * HALF * 2),
         name="place_weights",
-    )(idx, *args, *before)
+    )(half, piece, *before)
 
 
 def shift_x(value, shift):
@@ -409,29 +405,36 @@
     plane = lax.axis_index("zl").astype(jnp.int32)
     half = core.reshape(1)
 
-    packed, scales = pack(1 - half, gv, gs)
+    def blocks(*shifts):
+        return [lax.rem(x + shift, NX) for shift in shifts]
+
+    order = blocks(2, 1, 3, 0)
+    packed = pack(jnp.stack([1 - core] + order), gv, gs, "pack_theirs")
+    mine = pack(jnp.stack([core] + order), gv, gs, "pack_mine")
     there = swap(packed, "c")
-    arrived = []
-    for shift in (2, 1, 3):
-        target = jnp.stack([lax.rem(x + shift, NX), core])
-        arrived.append(shift_x(chip_sum(target, gv, scales, there, True), shift))
-    own = chip_sum(jnp.stack([x, core]), gv, scales, there, False)
-    quarter = last_sum(exchange(row_sum(own, arrived), ("zl", "y")))
-    low = low_weights((2 * core + plane).reshape(1), quarter, master, fm, fs, sm, ss)
+    arrived = [
+        shift_x(chip_sum(k, mine, there, True), shift)
+        for k, shift in enumerate((2, 1, 3))
+    ]
+    own = chip_sum(3, mine, there, False)
+    codes = exchange(row_sum(own, arrived), ("zl", "y"))
+    quarter, low = low_weights(
+        (2 * core + plane).reshape(1), codes, master, fm, fs, sm, ss
+    )
     low_y = exchange(low, ("zl", "y"))
 
     from_z = swap(quarter, "zl")
     left = jnp.where(plane == 0, quarter, from_z)
     right = jnp.where(plane == 0, from_z, quarter)
     gradient = jnp.concatenate([left, right], axis=1)
-    new = states(half, gradient, swap(gradient, "c"), master, fm, fs, sm, ss)
-    low_y, new = lax.optimization_barrier((low_y, new))
-
-    two, one, three = [shift_x(low_y, shift) for shift in (2, 1, 3)]
-    other_y = swap(low_y, "c")
-    rest = [swap(piece, "c") for piece in (one, two, three)]
-    placed = place(jnp.stack([core, x]), [low_y, one, two, three])
-    weights, transposed = place(jnp.stack([1 - core, x]), [other_y] + rest, placed)
+    low_y, gradient = lax.optimization_barrier((low_y, gradient))
+    other_gradient = swap(gradient, "c")
+    new = states(half, gradient, other_gradient, master, fm, fs, sm, ss)
+
+    near = exchange(spread(low_y), "x")
+    near, new = lax.optimization_barrier((near, new))
+    far = swap(near, "c")
+    weights, transposed = place(1 - half, far, place(half, near))
     om, of, ofs, os, oss = [a[None] for a in new]
     return om, of, ofs, os, oss, weights[None], transposed[None]
 

time: 112 us -> 110 us (0.982); the launches traced: 112 us -> 108 us
  waiting for transfers between devices: 15.1 us -> 41 us
  blocking collectives: 14.5 us -> 0 us
  starting transfers between devices: 58.6 us -> 46.5 us
  local copies, waits for them, and re-layouts: 4.54 us -> 0.2 us
  Pallas kernels: 17.5 us -> 19.9 us
    all_to_all x1 -> x3, waiting for transfers between devices: 0.01 us -> 25.1 us  [exchange(): return lax.all_to_all(value, axis, 0, 0, tiled=True)]
    all_to_all x1 -> x0, blocking collectives: 14.5 us -> none  [exchange(): return lax.all_to_all(value, axis, 0, 0, tiled=True)]
    ppermute x7 -> x4, starting transfers between devices: 34.8 us -> 24.9 us  [swap(): return lax.ppermute(value, axis, [(0, 1), (1, 0)])]
    ppermute x6 -> x3, starting transfers between devices: 17.8 us -> 8.41 us  [shift_x(): return lax.ppermute(value, 'x', [(i, (i + shift) % NX) for i in range(NX)])]
    all_to_all x1 -> x3, starting transfers between devices: 6.02 us -> 13.1 us  [exchange(): return lax.all_to_all(value, axis, 0, 0, tiled=True)]
    unnamed x16 -> x10, local copies, waits for them, and re-layouts: 4.54 us -> 0.03 us
    pallas_call x1 -> x2, Pallas kernels: 0.26 us -> 4.37 us  [pack(): pl.pallas_call(pack_kernel, grid_spec=pltpu.PrefetchScalarGridSpec(num_sc...]
    ppermute x6 -> x3, waiting for transfers between devices: 11.4 us -> 13.1 us  [shift_x(): return lax.ppermute(value, 'x', [(i, (i + shift) % NX) for i in range(NX)])]
  transfers between devices with their start and end apart: 14 -> 10, of which waited for: 4 -> 8; matrix products, arithmetic and copies ran while one was open for 0% -> 0% of each run, Pallas kernels for 10% -> 9%
where the time goes in v4:
time: 110 us; the launch traced here: 108 us
  starting transfers between devices  46.5 us (42%)
  waiting for transfers between devices  41 us (37%)
  Pallas kernels  19.9 us (18%)
    all_to_all x3, waiting for transfers between devices, exchange(): return lax.all_to_all(value, axis, 0, 0, tiled=True)  25.1 us
    ppermute x4, starting transfers between devices, swap(): return lax.ppermute(value, axis, [(0, 1), (1, 0)])  24.9 us
    all_to_all x3, starting transfers between devices, exchange(): return lax.all_to_all(value, axis, 0, 0, tiled=True)  13.1 us
    ppermute x3, waiting for transfers between devices, shift_x(): return lax.ppermute(value, 'x', [(i, (i + shift) % NX) for i in range(NX)])  13.1 us
    ppermute x3, starting transfers between devices, shift_x(): return lax.ppermute(value, 'x', [(i, (i + shift) % NX) for i in range(NX)])  8.41 us
    pallas_call x1, Pallas kernels, states(): pl.pallas_call(state_kernel, grid_spec=pltpu.PrefetchScalarGridSpec(num_s...  4.51 us
    pallas_call x2, Pallas kernels, pack(): pl.pallas_call(pack_kernel, grid_spec=pltpu.PrefetchScalarGridSpec(num_sc...  4.37 us
    pallas_call x2, Pallas kernels, place(): pl.pallas_call(place_kernel, grid_spec=pltpu.PrefetchScalarGridSpec(num_s...  3.87 us
  transfers between devices with their start and end apart: 10, of which 8 were waited for; matrix products, arithmetic and copies ran while one was open for 0% of the time, Pallas kernels for 9%

profile of v4, /device:TPU:1, one launch (start us, length us, event | category | flops | bytes accessed | tf_op | source)
XLA Modules:
  0.0 108.4 jit_solution(8124755476659393915)
XLA Ops:
  0.6 0.1 stack.35.idx
  0.7 2.2 %pack_theirs.1 = bf16[4,32,6272]{2,1,0:T(8,128)(2,1)S(1)} custom-call(s32[5]{0:T(128)S(1)} %stack.35.idx, bf16[128,12288]{1,0:T(8,128)(2,1)} %bitcast.33, bf16[128,12288]{1,0:T(8,128)(2,1)} %bitcast.34, bf16[128,12288]{1,0:T(8,128)(2,1)} %bitcast.35, bf16[128,12288]{1,0:T(8,128)(2,1)} %bitcast.36, bf16[96,128]{1,0:T(8,128)(2,1)} %bitcast.43), custom_call_target="tpu_custom_call" | custom-call | bytes 6291456 | tf_op jit(solution)/shard_map/pack_theirs/pallas_call | solution.py:78
  2.9 8.8 %collective-permute-start = (bf16[4,32,6272]{2,1,0:T(8,128)(2,1)S(1)}, bf16[4,32,6272]{2,1,0:T(8,128)(2,1)S(1)}, u32[]{:S(2)}, u32[]{:S(2)}) collective-permute-start(bf16[4,32,6272]{2,1,0:T(8,128)(2,1)S(1)} %pack_theirs.1), channel_id=1, source_target_pairs={{0,128},{128,0},{1,129},{129,1},{2,130},{130,2},{3,131},{131,3},{4... | collective-permute-start | bytes 4816904 | tf_op jit(solution)/shard_map/ppermute | solution.py:396
  11.7 0.1 stack.33.idx
  11.8 2.2 %pack_mine.1.values.scales = bf16[4,32,6272]{2,1,0:T(8,128)(2,1)S(1)} custom-call(s32[5]{0:T(128)S(1)} %stack.33.idx, bf16[128,12288]{1,0:T(8,128)(2,1)} %bitcast.37, bf16[128,12288]{1,0:T(8,128)(2,1)} %bitcast.38, bf16[128,12288]{1,0:T(8,128)(2,1)} %bitcast.39, bf16[128,12288]{1,0:T(8,128)(2,1)} %bitcast.40, bf16[96,128]{1,0:T(8,128)(2,1)} %bitcast.44), custom_call_target="tpu_custom_call" | custom-call | bytes 6291456 | tf_op jit(solution)/shard_map/pack_mine/pallas_call | solution.py:78
  14.0 0.8 collective-permute-done.there.there_scales
  14.8 0.6 coded_chip_sum.3
  15.4 1.9 %collective-permute-start.1 = (bf16[32,6272]{1,0:T(8,128)(2,1)S(1)}, bf16[32,6272]{1,0:T(8,128)(2,1)S(1)}, u32[]{:S(2)}, u32[]{:S(2)}) collective-permute-start(bf16[32,6272]{1,0:T(8,128)(2,1)S(1)} %coded_chip_sum.3), channel_id=1, source_target_pairs={{0,64},{32,96},{64,0},{96,32},{1,65},{33,97},{65,1},{97,33},{2,66}... | collective-permute-start | bytes 1204232 | tf_op jit(solution)/shard_map/ppermute | solution.py:388
  17.3 0.6 coded_chip_sum.4
  18.0 1.9 %collective-permute-start.2 = (bf16[32,6272]{1,0:T(8,128)(2,1)S(1)}, bf16[32,6272]{1,0:T(8,128)(2,1)S(1)}, u32[]{:S(2)}, u32[]{:S(2)}) collective-permute-start(bf16[32,6272]{1,0:T(8,128)(2,1)S(1)} %coded_chip_sum.4), channel_id=1, source_target_pairs={{0,32},{32,64},{64,96},{96,0},{1,33},{33,65},{65,97},{97,1},{2,34}... | collective-permute-start | bytes 1204232 | tf_op jit(solution)/shard_map/ppermute | solution.py:388
  19.9 0.6 coded_chip_sum.5
  20.5 4.6 %collective-permute-start.3 = (bf16[32,6272]{1,0:T(8,128)(2,1)S(1)}, bf16[32,6272]{1,0:T(8,128)(2,1)S(1)}, u32[]{:S(2)}, u32[]{:S(2)}) collective-permute-start(bf16[32,6272]{1,0:T(8,128)(2,1)S(1)} %coded_chip_sum.5), channel_id=1, source_target_pairs={{0,96},{32,0},{64,32},{96,64},{1,97},{33,1},{65,33},{97,65},{2,98}... | collective-permute-start | bytes 1204232 | tf_op jit(solution)/shard_map/ppermute | solution.py:388
  25.1 0.4 own_chip_sum.1.own
  25.5 0.0 copy-start
  25.5 0.0 copy-start.1
  25.5 0.0 copy-start.2
  25.5 0.0 copy-start.3
  25.5 0.0 copy-start.4
  25.5 3.8 %collective-permute-done.1.c1.s1 = bf16[32,6272]{1,0:T(8,128)(2,1)S(1)} collective-permute-done((bf16[32,6272]{1,0:T(8,128)(2,1)S(1)}, bf16[32,6272]{1,0:T(8,128)(2,1)S(1)}, u32[]{:S(2)}, u32[]{:S(2)}) %collective-permute-start.1) | collective-permute-done | bytes 401440 | tf_op jit(solution)/shard_map/ppermute | solution.py:388
  29.4 9.3 %collective-permute-done.2.c2.s2 = bf16[32,6272]{1,0:T(8,128)(2,1)S(1)} collective-permute-done((bf16[32,6272]{1,0:T(8,128)(2,1)S(1)}, bf16[32,6272]{1,0:T(8,128)(2,1)S(1)}, u32[]{:S(2)}, u32[]{:S(2)}) %collective-permute-start.2) | collective-permute-done | bytes 401440 | tf_op jit(solution)/shard_map/ppermute | solution.py:388
  38.6 0.0 collective-permute-done.3.c3.s3
  38.6 2.0 %sum_over_x.1 = bf16[16,4,3200]{2,1,0:T(4,128)(2,1)} custom-call(f32[32,6144]{1,0:T(8,128)S(1)} %own_chip_sum.1.own, bf16[32,6272]{1,0:T(8,128)(2,1)S(1)} %collective-permute-done.1.c1.s1, bf16[32,6272]{1,0:T(8,128)(2,1)S(1)} %collective-permute-done.1.c1.s1, bf16[32,6272]{1,0:T(8,128)(2,1)S(1)} %collective-permute-done.2.c2.s2, ...), custom_call_target="tpu_custom_call" | custom-call | flops 11796480 | bytes 2359296 | tf_op jit(solution)/shard_map/sum_over_x/pallas_call | solution.py:180
  40.7 3.6 %all-to-all-start = ((bf16[16,4,3200]{2,1,0:T(4,128)(2,1)}), bf16[16,4,3200]{2,1,0:T(4,128)(2,1)S(1)}, u32[]{:S(2)}, u32[]{:S(2)}) async-start(bf16[16,4,3200]{2,1,0:T(4,128)(2,1)} %sum_over_x.1), calls=%async_computation | async-start | bytes 819200 | tf_op jit(solution)/shard_map/all_to_all | solution.py:392
  44.3 11.3 %all-to-all-done.codes.steps = bf16[16,4,3200]{2,1,0:T(4,128)(2,1)S(1)} async-done(((bf16[16,4,3200]{2,1,0:T(4,128)(2,1)}), bf16[16,4,3200]{2,1,0:T(4,128)(2,1)S(1)}, u32[]{:S(2)}, u32[]{:S(2)}) %all-to-all-start) | async-done | bytes 409632 | tf_op jit(solution)/shard_map/all_to_all | solution.py:392
  55.5 0.0 copy-done
  55.5 0.0 copy-done.1
  55.5 0.0 copy-done.2
  55.6 0.0 copy-done.3
  55.6 0.0 copy-done.4
  55.6 1.6 %sum_and_low_weights.1 = (f32[4,3072]{1,0:T(4,128)S(1)}, bf16[16,4,3072]{2,1,0:T(4,128)(2,1)}) custom-call(s32[1]{0:T(128)} %bitcast.idx, bf16[16,4,3200]{2,1,0:T(4,128)(2,1)S(1)} %all-to-all-done.codes.steps, bf16[16,4,3200]{2,1,0:T(4,128)(2,1)S(1)} %all-to-all-done.codes.steps, f32[4,12288]{1,0:T(4,128)S(1)} %bitcast.23, bf16[4,12288]{1,0:T(4,128)(2,1)S(1)} %bitcast.25, ...), custom_call_target="tpu_custom_call" | custom-call | flops 5898240 | bytes 1572864 | tf_op jit(solution)/shard_map/sum_and_low_weights/pallas_call | solution.py:228
  57.2 2.5 %collective-permute-start.4 = (f32[4,3072]{1,0:T(4,128)S(1)}, f32[4,3072]{1,0:T(4,128)S(1)}, u32[]{:S(2)}, u32[]{:S(2)}) collective-permute-start(f32[4,3072]{1,0:T(4,128)S(1)} %get-tuple-element.27), channel_id=1, source_target_pairs={{0,256},{256,0},{1,257},{257,1},{2,258},{258,2},{3,259},{259,3},{4... | collective-permute-start | bytes 147464 | tf_op jit(solution)/shard_map/ppermute | solution.py:396
  59.7 5.9 %all-to-all-start.1 = ((bf16[16,4,3072]{2,1,0:T(4,128)(2,1)}), bf16[16,4,3072]{2,1,0:T(4,128)(2,1)S(1)}, u32[]{:S(2)}, u32[]{:S(2)}) async-start(bf16[16,4,3072]{2,1,0:T(4,128)(2,1)} %get-tuple-element.26), calls=%async_computation.1 | async-start | bytes 786432 | tf_op jit(solution)/shard_map/all_to_all | solution.py:392
  65.6 0.0 collective-permute-done.4
  65.6 9.3 %all-to-all-done.1.low = bf16[16,4,3072]{2,1,0:T(4,128)(2,1)S(1)} async-done(((bf16[16,4,3072]{2,1,0:T(4,128)(2,1)}), bf16[16,4,3072]{2,1,0:T(4,128)(2,1)S(1)}, u32[]{:S(2)}, u32[]{:S(2)}) %all-to-all-start.1) | async-done | bytes 393248 | tf_op jit(solution)/shard_map/all_to_all | solution.py:392
  75.0 1.2 %spread_rows.1 = bf16[4,32,6144]{2,1,0:T(8,128)(2,1)} custom-call(bf16[16,4,3072]{2,1,0:T(4,128)(2,1)S(1)} %all-to-all-done.1.low), custom_call_target="tpu_custom_call" | custom-call | bytes 1966080 | tf_op jit(solution)/shard_map/spread_rows/pallas_call | solution.py:343
  76.2 3.7 %all-to-all-start.2 = ((bf16[4,32,6144]{2,1,0:T(8,128)(2,1)}), bf16[4,32,6144]{2,1,0:T(8,128)(2,1)S(1)}, u32[]{:S(2)}, u32[]{:S(2)}) async-start(bf16[4,32,6144]{2,1,0:T(8,128)(2,1)} %spread_rows.1), calls=%async_computation.2 | async-start | bytes 3145728 | tf_op jit(solution)/shard_map/all_to_all | solution.py:392
  79.9 6.2 %collective-permute-start.5 = (f32[4,6144]{1,0:T(4,128)S(1)}, f32[4,6144]{1,0:T(4,128)S(1)}, u32[]{:S(2)}, u32[]{:S(2)}) collective-permute-start(f32[4,6144]{1,0:T(4,128)S(1)} %pad_maximum_fusion.mine), channel_id=1, source_target_pairs={{0,128},{128,0},{1,129},{129,1},{2,130},{130,2},{3,131},{131,3},{4... | collective-permute-start | bytes 294920 | tf_op jit(solution)/shard_map/ppermute | solution.py:396
  86.2 0.9 collective-permute-done.5.other
  87.1 4.5 %new_states.1 = (f32[4,12288]{1,0:T(4,128)}, bf16[4,12288]{1,0:T(4,128)(2,1)}, f32[4,96]{1,0:T(4,128)}, bf16[4,12288]{1,0:T(4,128)(2,1)}, f32[4,96]{1,0:T(4,128)}) custom-call(s32[1]{0:T(128)} %bitcast.1.idx, f32[4,6144]{1,0:T(4,128)S(1)} %pad_maximum_fusion.mine, f32[4,6144]{1,0:T(4,128)S(1)} %collective-permute-done.5.other, f32[4,12288]{1,0:T(4,128)S(1)} %bitcast.24, ...), custom_call_target="tpu_custom_call" | custom-call | flops 49152 | bytes 49152 | tf_op jit(solution)/shard_map/new_states/pallas_call | solution.py:312
  91.6 4.5 %all-to-all-done.2.piece = bf16[4,32,6144]{2,1,0:T(8,128)(2,1)S(1)} async-done(((bf16[4,32,6144]{2,1,0:T(8,128)(2,1)}), bf16[4,32,6144]{2,1,0:T(8,128)(2,1)S(1)}, u32[]{:S(2)}, u32[]{:S(2)}) %all-to-all-start.2) | async-done | bytes 1572896 | tf_op jit(solution)/shard_map/all_to_all | solution.py:392
  96.1 7.4 %collective-permute-start.6 = (bf16[4,32,6144]{2,1,0:T(8,128)(2,1)S(1)}, bf16[4,32,6144]{2,1,0:T(8,128)(2,1)S(1)}, u32[]{:S(2)}, u32[]{:S(2)}) collective-permute-start(bf16[4,32,6144]{2,1,0:T(8,128)(2,1)S(1)} %all-to-all-done.2.piece), channel_id=1, source_target_pairs={{0,128},{128,0},{1,129},{129,1},{2,130},{130,2},{3,131},{131,3},{4... | collective-permute-start | bytes 4718600 | tf_op jit(solution)/shard_map/ppermute | solution.py:396
  103.5 1.9 %place_weights.2 = (bf16[128,12288]{1,0:T(8,128)(2,1)}, bf16[12288,128]{1,0:T(8,128)(2,1)}) custom-call(s32[1]{0:T(128)} %bitcast.1.idx, bf16[4,32,6144]{2,1,0:T(8,128)(2,1)S(1)} %all-to-all-done.2.piece), custom_call_target="tpu_custom_call" | custom-call | bytes 4718592 | tf_op jit(solution)/shard_map/place_weights/pallas_call | solution.py:364
  105.4 1.1 collective-permute-done.6.piece
  106.5 1.9 %place_weights.3 = (bf16[128,12288]{1,0:T(8,128)(2,1)}, bf16[12288,128]{1,0:T(8,128)(2,1)}) custom-call(s32[1]{0:T(128)S(6)} %sub.7.idx, bf16[4,32,6144]{2,1,0:T(8,128)(2,1)S(1)} %collective-permute-done.6.piece, bf16[128,12288]{1,0:T(8,128)(2,1)} %get-tuple-element.41.refs_0_, ...), custom_call_target="tpu_custom_call", output_to_operand_aliasing={{0}: (2, {}), {1}: (3, {})} | custom-call | bytes 4718592 | tf_op jit(solution)/shard_map/place_weights/pallas_call | solution.py:364
  (2 shorter events, 0.0 us)
Async XLA Ops:
  2.9 11.9 %collective-permute-start = (bf16[4,32,6272]{2,1,0:T(8,128)(2,1)S(1)}, bf16[4,32,6272]{2,1,0:T(8,128)(2,1)S(1)}, u32[]{:S(2)}, u32[]{:S(2)}) collective-permute-start(bf16[4,32,6272]{2,1,0:T(8,128)(2,1)S(1)} %pack_theirs.1), channel_id=1, source_target_pairs={{0,128},{128,0},{1,129},{129,1},{2,130},{130,2},{3,131},{131,3},{4... | collective-permute-start | bytes 4816904 | tf_op jit(solution)/shard_map/ppermute | solution.py:396
  15.4 13.9 %collective-permute-start.1 = (bf16[32,6272]{1,0:T(8,128)(2,1)S(1)}, bf16[32,6272]{1,0:T(8,128)(2,1)S(1)}, u32[]{:S(2)}, u32[]{:S(2)}) collective-permute-start(bf16[32,6272]{1,0:T(8,128)(2,1)S(1)} %coded_chip_sum.3), channel_id=1, source_target_pairs={{0,64},{32,96},{64,0},{96,32},{1,65},{33,97},{65,1},{97,33},{2,66}... | collective-permute-start | bytes 1204232 | tf_op jit(solution)/shard_map/ppermute | solution.py:388
  18.0 20.7 %collective-permute-start.2 = (bf16[32,6272]{1,0:T(8,128)(2,1)S(1)}, bf16[32,6272]{1,0:T(8,128)(2,1)S(1)}, u32[]{:S(2)}, u32[]{:S(2)}) collective-permute-start(bf16[32,6272]{1,0:T(8,128)(2,1)S(1)} %coded_chip_sum.4), channel_id=1, source_target_pairs={{0,32},{32,64},{64,96},{96,0},{1,33},{33,65},{65,97},{97,1},{2,34}... | collective-permute-start | bytes 1204232 | tf_op jit(solution)/shard_map/ppermute | solution.py:388
  20.5 18.1 %collective-permute-start.3 = (bf16[32,6272]{1,0:T(8,128)(2,1)S(1)}, bf16[32,6272]{1,0:T(8,128)(2,1)S(1)}, u32[]{:S(2)}, u32[]{:S(2)}) collective-permute-start(bf16[32,6272]{1,0:T(8,128)(2,1)S(1)} %coded_chip_sum.5), channel_id=1, source_target_pairs={{0,96},{32,0},{64,32},{96,64},{1,97},{33,1},{65,33},{97,65},{2,98}... | collective-permute-start | bytes 1204232 | tf_op jit(solution)/shard_map/ppermute | solution.py:388
  25.5 30.1 %copy-start = (f32[1,4,12288]{2,1,0:T(4,128)S(1)}, f32[1,4,12288]{2,1,0:T(4,128)}, u32[]{:S(2)}) copy-start(f32[1,4,12288]{2,1,0:T(4,128)} %param.9) | copy-start | bytes 589828
  25.5 30.1 %copy-start.1 = (bf16[1,4,12288]{2,1,0:T(4,128)(2,1)S(1)}, bf16[1,4,12288]{2,1,0:T(4,128)(2,1)}, u32[]{:S(2)}) copy-start(bf16[1,4,12288]{2,1,0:T(4,128)(2,1)} %param.10) | copy-start | bytes 294916
  25.5 30.1 %copy-start.2 = (bf16[1,4,12288]{2,1,0:T(4,128)(2,1)S(1)}, bf16[1,4,12288]{2,1,0:T(4,128)(2,1)}, u32[]{:S(2)}) copy-start(bf16[1,4,12288]{2,1,0:T(4,128)(2,1)} %param.12) | copy-start | bytes 294916
  25.5 30.0 %copy-start.3 = (f32[1,4,96]{2,1,0:T(4,128)S(1)}, f32[1,4,96]{2,1,0:T(4,128)}, u32[]{:S(2)}) copy-start(f32[1,4,96]{2,1,0:T(4,128)} %param.11) | copy-start | bytes 4612
  25.5 30.0 %copy-start.4 = (f32[1,4,96]{2,1,0:T(4,128)S(1)}, f32[1,4,96]{2,1,0:T(4,128)}, u32[]{:S(2)}) copy-start(f32[1,4,96]{2,1,0:T(4,128)} %param.13) | copy-start | bytes 4612
  40.7 14.9 %all-to-all-start = ((bf16[16,4,3200]{2,1,0:T(4,128)(2,1)}), bf16[16,4,3200]{2,1,0:T(4,128)(2,1)S(1)}, u32[]{:S(2)}, u32[]{:S(2)}) async-start(bf16[16,4,3200]{2,1,0:T(4,128)(2,1)} %sum_over_x.1), calls=%async_computation | async-start | bytes 819200 | tf_op jit(solution)/shard_map/all_to_all | solution.py:392
  57.2 8.4 %collective-permute-start.4 = (f32[4,3072]{1,0:T(4,128)S(1)}, f32[4,3072]{1,0:T(4,128)S(1)}, u32[]{:S(2)}, u32[]{:S(2)}) collective-permute-start(f32[4,3072]{1,0:T(4,128)S(1)} %get-tuple-element.27), channel_id=1, source_target_pairs={{0,256},{256,0},{1,257},{257,1},{2,258},{258,2},{3,259},{259,3},{4... | collective-permute-start | bytes 147464 | tf_op jit(solution)/shard_map/ppermute | solution.py:396
  59.7 15.3 %all-to-all-start.1 = ((bf16[16,4,3072]{2,1,0:T(4,128)(2,1)}), bf16[16,4,3072]{2,1,0:T(4,128)(2,1)S(1)}, u32[]{:S(2)}, u32[]{:S(2)}) async-start(bf16[16,4,3072]{2,1,0:T(4,128)(2,1)} %get-tuple-element.26), calls=%async_computation.1 | async-start | bytes 786432 | tf_op jit(solution)/shard_map/all_to_all | solution.py:392
  76.2 19.8 %all-to-all-start.2 = ((bf16[4,32,6144]{2,1,0:T(8,128)(2,1)}), bf16[4,32,6144]{2,1,0:T(8,128)(2,1)S(1)}, u32[]{:S(2)}, u32[]{:S(2)}) async-start(bf16[4,32,6144]{2,1,0:T(8,128)(2,1)} %spread_rows.1), calls=%async_computation.2 | async-start | bytes 3145728 | tf_op jit(solution)/shard_map/all_to_all | solution.py:392
  79.9 7.1 %collective-permute-start.5 = (f32[4,6144]{1,0:T(4,128)S(1)}, f32[4,6144]{1,0:T(4,128)S(1)}, u32[]{:S(2)}, u32[]{:S(2)}) collective-permute-start(f32[4,6144]{1,0:T(4,128)S(1)} %pad_maximum_fusion.mine), channel_id=1, source_target_pairs={{0,128},{128,0},{1,129},{129,1},{2,130},{130,2},{3,131},{131,3},{4... | collective-permute-start | bytes 294920 | tf_op jit(solution)/shard_map/ppermute | solution.py:396
  96.1 10.5 %collective-permute-start.6 = (bf16[4,32,6144]{2,1,0:T(8,128)(2,1)S(1)}, bf16[4,32,6144]{2,1,0:T(8,128)(2,1)S(1)}, u32[]{:S(2)}, u32[]{:S(2)}) collective-permute-start(bf16[4,32,6144]{2,1,0:T(8,128)(2,1)S(1)} %all-to-all-done.2.piece), channel_id=1, source_target_pairs={{0,128},{128,0},{1,129},{129,1},{2,130},{130,2},{3,131},{131,3},{4... | collective-permute-start | bytes 4718600 | tf_op jit(solution)/shard_map/ppermute | solution.py:396

commit v5 on v4

--- a/solution.py
+++ b/solution.py
@@ -9,6 +9,7 @@
 
 D = 12288
 HALF = D // 2
+OLD_BYTES = 24 * 1024 * 1024
 BLOCK = 128
 NB = D // BLOCK
 HB = NB // 2
@@ -254,8 +255,34 @@
     )(quarter, codes, codes, master, fm, fs, sm, ss)
 
 
+def old_kernel(fm, fs, sm, ss, of, os):
+    for moment, scales, out in ((fm, fs, of), (sm, ss, os)):
+        scale = jnp.concatenate([scales[:, :HB], scales[:, HB:]], axis=0)
+        for b in range(HB):
+            cols = slice(b * BLOCK, (b + 1) * BLOCK)
+            halves = [moment[:, k * BLOCK : (k + 1) * BLOCK] for k in (b, b + HB)]
+            both = jnp.concatenate([half.astype(f32) for half in halves], axis=0)
+            out[:, cols] = both * scale[:, b : b + 1]
+
+
+def old_moments(fm, fs, sm, ss):
+    whole = pl.BlockSpec((YR, D), lambda i: (0, 0))
+    scale = pl.BlockSpec((YR, NB), lambda i: (0, 0))
+    stacked = pl.BlockSpec((2 * YR, HALF), lambda i: (0, 0))
+    return pl.pallas_call(
+        old_kernel,
+        grid=(1,),
+        in_specs=[whole, scale, whole, scale],
+        out_specs=[stacked, stacked],
+        out_shape=[jax.ShapeDtypeStruct((2 * YR, HALF), f32)] * 2,
+        compiler_params=params(),
+        cost_estimate=cost(2 * YR * D, OLD_BYTES),
+        name="old_moments",
+    )(fm, fs, sm, ss)
+
+
 def state_kernel(
-    idx, mine, other, master, fm, fs, sm, ss, om, of, ofs, os, oss, firsts, seconds
+    idx, mine, other, master, fold, sold, om, of, ofs, os, oss, firsts, seconds
 ):
     first_half = idx[0] == 0
 
@@ -263,14 +290,10 @@
         halves = [ref[:, k * BLOCK : (k + 1) * BLOCK] for k in (b, b + HB)]
         return jnp.concatenate([half.astype(f32) for half in halves], axis=0)
 
-    def scales_of(ref):
-        return jnp.concatenate([ref[:, :HB], ref[:, HB:]], axis=0)
-
     def store(ref, b, value):
         for k, rows in ((b, slice(0, YR)), (b + HB, slice(YR, 2 * YR))):
             ref[:, k * BLOCK : (k + 1) * BLOCK] = value[rows].astype(ref.dtype)
 
-    fscale, sscale = scales_of(fs), scales_of(ss)
     lane = lax.broadcasted_iota(jnp.int32, (2 * YR, HB), 1)
     fpeaks = jnp.zeros((2 * YR, HB), f32)
     speaks = jnp.zeros((2 * YR, HB), f32)
@@ -280,10 +303,8 @@
         gradient = jnp.concatenate(
             [jnp.where(first_half, one, two), jnp.where(first_half, two, one)], axis=0
         )
-        first_old = stacked(fm, b) * fscale[:, b : b + 1]
-        second_old = stacked(sm, b) * sscale[:, b : b + 1]
         first, second, updated = adam(
-            gradient, stacked(master, b), first_old, second_old
+            gradient, stacked(master, b), fold[:, cols], sold[:, cols]
         )
         store(om, b, updated)
         firsts[:, cols] = first
@@ -304,17 +325,18 @@
         store(os, b, seconds[:, cols] * sinverse[:, b : b + 1])
 
 
-def states(core, mine, other, master, fm, fs, sm, ss):
+def states(core, mine, other, master, fold, sold):
     half = pl.BlockSpec((YR, HALF), lambda i, s: (0, 0))
     whole = pl.BlockSpec((YR, D), lambda i, s: (0, 0))
     scale = pl.BlockSpec((YR, NB), lambda i, s: (0, 0))
+    stacked = pl.BlockSpec((2 * YR, HALF), lambda i, s: (0, 0))
     shape = jax.ShapeDtypeStruct
     return pl.pallas_call(
         state_kernel,
         grid_spec=pltpu.PrefetchScalarGridSpec(
             num_scalar_prefetch=1,
             grid=(1,),
-            in_specs=[half, half, whole, whole, scale, whole, scale],
+            in_specs=[half, half, whole, stacked, stacked],
             out_specs=[whole, whole, scale, whole, scale],
             scratch_shapes=[pltpu.VMEM((2 * YR, HALF), f32)] * 2,
         ),
@@ -328,7 +350,7 @@
         compiler_params=params(),
         cost_estimate=cost(YR * D, YR * D),
         name="new_states",
-    )(core, mine, other, master, fm, fs, sm, ss)
+    )(core, mine, other, master, fold, sold)
 
 
 def spread_kernel(low, out):
@@ -422,14 +444,15 @@
         (2 * core + plane).reshape(1), codes, master, fm, fs, sm, ss
     )
     low_y = exchange(low, ("zl", "y"))
+    quarter, fm, fs, sm, ss = lax.optimization_barrier((quarter, fm, fs, sm, ss))
+    fold, sold = old_moments(fm, fs, sm, ss)
 
     from_z = swap(quarter, "zl")
     left = jnp.where(plane == 0, quarter, from_z)
     right = jnp.where(plane == 0, from_z, quarter)
     gradient = jnp.concatenate([left, right], axis=1)
-    low_y, gradient = lax.optimization_barrier((low_y, gradient))
     other_gradient = swap(gradient, "c")
-    new = states(half, gradient, other_gradient, master, fm, fs, sm, ss)
+    new = states(half, gradient, other_gradient, master, fold, sold)
 
     near = exchange(spread(low_y), "x")
     near, new = lax.optimization_barrier((near, new))

time: 110 us -> 109 us (level)
  waiting for transfers between devices: 41 us -> 45 us
  Pallas kernels: 19.9 us -> 16.9 us
  starting transfers between devices: 46.5 us -> 44.7 us
    all_to_all x3, waiting for transfers between devices: 25.1 us -> 29.4 us  [exchange(): return lax.all_to_all(value, axis, 0, 0, tiled=True)]
    pallas_call x1, Pallas kernels: 4.51 us -> 1.19 us  [states(): pl.pallas_call(state_kernel, grid_spec=pltpu.PrefetchScalarGridSpec(num_s...]
    ppermute x4, starting transfers between devices: 24.9 us -> 22.9 us  [swap(): return lax.ppermute(value, axis, [(0, 1), (1, 0)])]
  transfers between devices with their start and end apart: 10 -> 10, of which waited for: 8 -> 8; matrix products, arithmetic and copies ran while one was open for 0% -> 0% of each run, Pallas kernels for 9% -> 8%
where the time goes in v5:
time: 109 us; the launch traced here: 108 us
  waiting for transfers between devices  45 us (41%)
  starting transfers between devices  44.7 us (41%)
  Pallas kernels  16.9 us (16%)
    all_to_all x3, waiting for transfers between devices, exchange(): return lax.all_to_all(value, axis, 0, 0, tiled=True)  29.4 us
    ppermute x4, starting transfers between devices, swap(): return lax.ppermute(value, axis, [(0, 1), (1, 0)])  22.9 us
    all_to_all x3, starting transfers between devices, exchange(): return lax.all_to_all(value, axis, 0, 0, tiled=True)  13.4 us
    ppermute x3, waiting for transfers between devices, shift_x(): return lax.ppermute(value, 'x', [(i, (i + shift) % NX) for i in range(NX)])  13.1 us
    ppermute x3, starting transfers between devices, shift_x(): return lax.ppermute(value, 'x', [(i, (i + shift) % NX) for i in range(NX)])  8.41 us
    pallas_call x2, Pallas kernels, pack(): pl.pallas_call(pack_kernel, grid_spec=pltpu.PrefetchScalarGridSpec(num_sc...  4.37 us
    pallas_call x2, Pallas kernels, place(): pl.pallas_call(place_kernel, grid_spec=pltpu.PrefetchScalarGridSpec(num_s...  3.87 us
    ppermute x4, waiting for transfers between devices, swap(): return lax.ppermute(value, axis, [(0, 1), (1, 0)])  2.47 us
  transfers between devices with their start and end apart: 10, of which 8 were waited for; matrix products, arithmetic and copies ran while one was open for 0% of the time, Pallas kernels for 8%

profile of v5, /device:TPU:1, one launch (start us, length us, event | category | flops | bytes accessed | tf_op | source)
XLA Modules:
  0.0 107.6 jit_solution(16633984200569108710)
XLA Ops:
  0.6 0.1 stack.35.idx
  0.7 2.2 %pack_theirs.1 = bf16[4,32,6272]{2,1,0:T(8,128)(2,1)S(1)} custom-call(s32[5]{0:T(128)S(1)} %stack.35.idx, bf16[128,12288]{1,0:T(8,128)(2,1)} %bitcast.33, bf16[128,12288]{1,0:T(8,128)(2,1)} %bitcast.34, bf16[128,12288]{1,0:T(8,128)(2,1)} %bitcast.35, bf16[128,12288]{1,0:T(8,128)(2,1)} %bitcast.36, bf16[96,128]{1,0:T(8,128)(2,1)} %bitcast.43), custom_call_target="tpu_custom_call" | custom-call | bytes 6291456 | tf_op jit(solution)/shard_map/pack_theirs/pallas_call | solution.py:79
  2.9 8.8 %collective-permute-start = (bf16[4,32,6272]{2,1,0:T(8,128)(2,1)S(1)}, bf16[4,32,6272]{2,1,0:T(8,128)(2,1)S(1)}, u32[]{:S(2)}, u32[]{:S(2)}) collective-permute-start(bf16[4,32,6272]{2,1,0:T(8,128)(2,1)S(1)} %pack_theirs.1), channel_id=1, source_target_pairs={{0,128},{128,0},{1,129},{129,1},{2,130},{130,2},{3,131},{131,3},{4... | collective-permute-start | bytes 4816904 | tf_op jit(solution)/shard_map/ppermute | solution.py:418
  11.7 0.1 stack.33.idx
  11.8 2.2 %pack_mine.1.values.scales = bf16[4,32,6272]{2,1,0:T(8,128)(2,1)S(1)} custom-call(s32[5]{0:T(128)S(1)} %stack.33.idx, bf16[128,12288]{1,0:T(8,128)(2,1)} %bitcast.37, bf16[128,12288]{1,0:T(8,128)(2,1)} %bitcast.38, bf16[128,12288]{1,0:T(8,128)(2,1)} %bitcast.39, bf16[128,12288]{1,0:T(8,128)(2,1)} %bitcast.40, bf16[96,128]{1,0:T(8,128)(2,1)} %bitcast.44), custom_call_target="tpu_custom_call" | custom-call | bytes 6291456 | tf_op jit(solution)/shard_map/pack_mine/pallas_call | solution.py:79
  14.0 0.8 collective-permute-done.there.there_scales
  14.8 0.6 coded_chip_sum.3
  15.4 1.9 %collective-permute-start.1 = (bf16[32,6272]{1,0:T(8,128)(2,1)S(1)}, bf16[32,6272]{1,0:T(8,128)(2,1)S(1)}, u32[]{:S(2)}, u32[]{:S(2)}) collective-permute-start(bf16[32,6272]{1,0:T(8,128)(2,1)S(1)} %coded_chip_sum.3), channel_id=1, source_target_pairs={{0,64},{32,96},{64,0},{96,32},{1,65},{33,97},{65,1},{97,33},{2,66}... | collective-permute-start | bytes 1204232 | tf_op jit(solution)/shard_map/ppermute | solution.py:410
  17.3 0.6 coded_chip_sum.4
  18.0 1.9 %collective-permute-start.2 = (bf16[32,6272]{1,0:T(8,128)(2,1)S(1)}, bf16[32,6272]{1,0:T(8,128)(2,1)S(1)}, u32[]{:S(2)}, u32[]{:S(2)}) collective-permute-start(bf16[32,6272]{1,0:T(8,128)(2,1)S(1)} %coded_chip_sum.4), channel_id=1, source_target_pairs={{0,32},{32,64},{64,96},{96,0},{1,33},{33,65},{65,97},{97,1},{2,34}... | collective-permute-start | bytes 1204232 | tf_op jit(solution)/shard_map/ppermute | solution.py:410
  19.9 0.6 coded_chip_sum.5
  20.5 4.6 %collective-permute-start.3 = (bf16[32,6272]{1,0:T(8,128)(2,1)S(1)}, bf16[32,6272]{1,0:T(8,128)(2,1)S(1)}, u32[]{:S(2)}, u32[]{:S(2)}) collective-permute-start(bf16[32,6272]{1,0:T(8,128)(2,1)S(1)} %coded_chip_sum.5), channel_id=1, source_target_pairs={{0,96},{32,0},{64,32},{96,64},{1,97},{33,1},{65,33},{97,65},{2,98}... | collective-permute-start | bytes 1204232 | tf_op jit(solution)/shard_map/ppermute | solution.py:410
  25.1 0.4 own_chip_sum.1.own
  25.5 0.0 copy-start
  25.5 0.0 copy-start.1
  25.5 0.0 copy-start.2
  25.5 0.0 copy-start.3
  25.5 0.0 copy-start.4
  25.5 3.8 %collective-permute-done.1.c1.s1 = bf16[32,6272]{1,0:T(8,128)(2,1)S(1)} collective-permute-done((bf16[32,6272]{1,0:T(8,128)(2,1)S(1)}, bf16[32,6272]{1,0:T(8,128)(2,1)S(1)}, u32[]{:S(2)}, u32[]{:S(2)}) %collective-permute-start.1) | collective-permute-done | bytes 401440 | tf_op jit(solution)/shard_map/ppermute | solution.py:410
  29.4 9.3 %collective-permute-done.2.c2.s2 = bf16[32,6272]{1,0:T(8,128)(2,1)S(1)} collective-permute-done((bf16[32,6272]{1,0:T(8,128)(2,1)S(1)}, bf16[32,6272]{1,0:T(8,128)(2,1)S(1)}, u32[]{:S(2)}, u32[]{:S(2)}) %collective-permute-start.2) | collective-permute-done | bytes 401440 | tf_op jit(solution)/shard_map/ppermute | solution.py:410
  38.6 0.0 collective-permute-done.3.c3.s3
  38.6 2.0 %sum_over_x.1 = bf16[16,4,3200]{2,1,0:T(4,128)(2,1)} custom-call(f32[32,6144]{1,0:T(8,128)S(1)} %own_chip_sum.1.own, bf16[32,6272]{1,0:T(8,128)(2,1)S(1)} %collective-permute-done.1.c1.s1, bf16[32,6272]{1,0:T(8,128)(2,1)S(1)} %collective-permute-done.1.c1.s1, bf16[32,6272]{1,0:T(8,128)(2,1)S(1)} %collective-permute-done.2.c2.s2, ...), custom_call_target="tpu_custom_call" | custom-call | flops 11796480 | bytes 2359296 | tf_op jit(solution)/shard_map/sum_over_x/pallas_call | solution.py:181
  40.7 3.6 %all-to-all-start = ((bf16[16,4,3200]{2,1,0:T(4,128)(2,1)}), bf16[16,4,3200]{2,1,0:T(4,128)(2,1)S(1)}, u32[]{:S(2)}, u32[]{:S(2)}) async-start(bf16[16,4,3200]{2,1,0:T(4,128)(2,1)} %sum_over_x.1), calls=%async_computation | async-start | bytes 819200 | tf_op jit(solution)/shard_map/all_to_all | solution.py:414
  44.3 11.3 %all-to-all-done.codes.steps = bf16[16,4,3200]{2,1,0:T(4,128)(2,1)S(1)} async-done(((bf16[16,4,3200]{2,1,0:T(4,128)(2,1)}), bf16[16,4,3200]{2,1,0:T(4,128)(2,1)S(1)}, u32[]{:S(2)}, u32[]{:S(2)}) %all-to-all-start) | async-done | bytes 409632 | tf_op jit(solution)/shard_map/all_to_all | solution.py:414
  55.5 0.0 copy-done
  55.5 0.0 copy-done.1
  55.5 0.0 copy-done.2
  55.6 0.0 copy-done.3
  55.6 0.0 copy-done.4
  55.6 1.6 %sum_and_low_weights.1 = (f32[4,3072]{1,0:T(4,128)S(1)}, bf16[16,4,3072]{2,1,0:T(4,128)(2,1)}) custom-call(s32[1]{0:T(128)} %bitcast.idx, bf16[16,4,3200]{2,1,0:T(4,128)(2,1)S(1)} %all-to-all-done.codes.steps, bf16[16,4,3200]{2,1,0:T(4,128)(2,1)S(1)} %all-to-all-done.codes.steps, f32[4,12288]{1,0:T(4,128)S(1)} %bitcast.23, bf16[4,12288]{1,0:T(4,128)(2,1)S(1)} %bitcast.25, ...), custom_call_target="tpu_custom_call" | custom-call | flops 5898240 | bytes 1572864 | tf_op jit(solution)/shard_map/sum_and_low_weights/pallas_call | solution.py:229
  57.2 6.1 %all-to-all-start.1 = ((bf16[16,4,3072]{2,1,0:T(4,128)(2,1)}), bf16[16,4,3072]{2,1,0:T(4,128)(2,1)S(1)}, u32[]{:S(2)}, u32[]{:S(2)}) async-start(bf16[16,4,3072]{2,1,0:T(4,128)(2,1)} %get-tuple-element.31), calls=%async_computation.1 | async-start | bytes 786432 | tf_op jit(solution)/shard_map/all_to_all | solution.py:414
  63.3 3.3 %collective-permute-start.4 = (f32[4,3072]{1,0:T(4,128)S(1)}, f32[4,3072]{1,0:T(4,128)S(1)}, u32[]{:S(2)}, u32[]{:S(2)}) collective-permute-start(f32[4,3072]{1,0:T(4,128)S(1)} %get-tuple-element.33), channel_id=1, source_target_pairs={{0,256},{256,0},{1,257},{257,1},{2,258},{258,2},{3,259},{259,3},{4... | collective-permute-start | bytes 147464 | tf_op jit(solution)/shard_map/ppermute | solution.py:418
  66.6 7.6 %all-to-all-done.1.low = bf16[16,4,3072]{2,1,0:T(4,128)(2,1)S(1)} async-done(((bf16[16,4,3072]{2,1,0:T(4,128)(2,1)}), bf16[16,4,3072]{2,1,0:T(4,128)(2,1)S(1)}, u32[]{:S(2)}, u32[]{:S(2)}) %all-to-all-start.1) | async-done | bytes 393248 | tf_op jit(solution)/shard_map/all_to_all | solution.py:414
  74.1 1.2 %spread_rows.1 = bf16[4,32,6144]{2,1,0:T(8,128)(2,1)} custom-call(bf16[16,4,3072]{2,1,0:T(4,128)(2,1)S(1)} %all-to-all-done.1.low), custom_call_target="tpu_custom_call" | custom-call | bytes 1966080 | tf_op jit(solution)/shard_map/spread_rows/pallas_call | solution.py:365
  75.4 3.7 %all-to-all-start.2 = ((bf16[4,32,6144]{2,1,0:T(8,128)(2,1)}), bf16[4,32,6144]{2,1,0:T(8,128)(2,1)S(1)}, u32[]{:S(2)}, u32[]{:S(2)}) async-start(bf16[4,32,6144]{2,1,0:T(8,128)(2,1)} %spread_rows.1), calls=%async_computation.2 | async-start | bytes 3145728 | tf_op jit(solution)/shard_map/all_to_all | solution.py:414
  79.1 0.0 collective-permute-done.4
  79.2 5.0 %collective-permute-start.5 = (f32[4,6144]{1,0:T(4,128)S(1)}, f32[4,6144]{1,0:T(4,128)S(1)}, u32[]{:S(2)}, u32[]{:S(2)}) collective-permute-start(f32[4,6144]{1,0:T(4,128)S(1)} %pad_maximum_fusion.mine), channel_id=1, source_target_pairs={{0,128},{128,0},{1,129},{129,1},{2,130},{130,2},{3,131},{131,3},{4... | collective-permute-start | bytes 294920 | tf_op jit(solution)/shard_map/ppermute | solution.py:418
  84.1 0.3 old_moments.1
  84.5 0.6 collective-permute-done.5.other
  85.1 1.2 %new_states.1 = (f32[4,12288]{1,0:T(4,128)}, bf16[4,12288]{1,0:T(4,128)(2,1)}, f32[4,96]{1,0:T(4,128)}, bf16[4,12288]{1,0:T(4,128)(2,1)}, f32[4,96]{1,0:T(4,128)}) custom-call(s32[1]{0:T(128)} %bitcast.1.idx, f32[4,6144]{1,0:T(4,128)S(1)} %pad_maximum_fusion.mine, f32[4,6144]{1,0:T(4,128)S(1)} %collective-permute-done.5.other, f32[4,12288]{1,0:T(4,128)S(1)} %bitcast.24, ...), custom_call_target="tpu_custom_call" | custom-call | flops 49152 | bytes 49152 | tf_op jit(solution)/shard_map/new_states/pallas_call | solution.py:334
  86.3 10.6 %all-to-all-done.2.piece = bf16[4,32,6144]{2,1,0:T(8,128)(2,1)S(1)} async-done(((bf16[4,32,6144]{2,1,0:T(8,128)(2,1)}), bf16[4,32,6144]{2,1,0:T(8,128)(2,1)S(1)}, u32[]{:S(2)}, u32[]{:S(2)}) %all-to-all-start.2) | async-done | bytes 1572896 | tf_op jit(solution)/shard_map/all_to_all | solution.py:414
  96.8 5.9 %collective-permute-start.6 = (bf16[4,32,6144]{2,1,0:T(8,128)(2,1)S(1)}, bf16[4,32,6144]{2,1,0:T(8,128)(2,1)S(1)}, u32[]{:S(2)}, u32[]{:S(2)}) collective-permute-start(bf16[4,32,6144]{2,1,0:T(8,128)(2,1)S(1)} %all-to-all-done.2.piece), channel_id=1, source_target_pairs={{0,128},{128,0},{1,129},{129,1},{2,130},{130,2},{3,131},{131,3},{4... | collective-permute-start | bytes 4718600 | tf_op jit(solution)/shard_map/ppermute | solution.py:418
  102.7 1.9 %place_weights.2 = (bf16[128,12288]{1,0:T(8,128)(2,1)}, bf16[12288,128]{1,0:T(8,128)(2,1)}) custom-call(s32[1]{0:T(128)} %bitcast.1.idx, bf16[4,32,6144]{2,1,0:T(8,128)(2,1)S(1)} %all-to-all-done.2.piece), custom_call_target="tpu_custom_call" | custom-call | bytes 4718592 | tf_op jit(solution)/shard_map/place_weights/pallas_call | solution.py:386
  104.7 1.1 collective-permute-done.6.piece
  105.7 1.9 %place_weights.3 = (bf16[128,12288]{1,0:T(8,128)(2,1)}, bf16[12288,128]{1,0:T(8,128)(2,1)}) custom-call(s32[1]{0:T(128)S(6)} %sub.7.idx, bf16[4,32,6144]{2,1,0:T(8,128)(2,1)S(1)} %collective-permute-done.6.piece, bf16[128,12288]{1,0:T(8,128)(2,1)} %get-tuple-element.51.refs_0_, ...), custom_call_target="tpu_custom_call", output_to_operand_aliasing={{0}: (2, {}), {1}: (3, {})} | custom-call | bytes 4718592 | tf_op jit(solution)/shard_map/place_weights/pallas_call | solution.py:386
  (2 shorter events, 0.0 us)
Async XLA Ops:
  2.9 11.9 %collective-permute-start = (bf16[4,32,6272]{2,1,0:T(8,128)(2,1)S(1)}, bf16[4,32,6272]{2,1,0:T(8,128)(2,1)S(1)}, u32[]{:S(2)}, u32[]{:S(2)}) collective-permute-start(bf16[4,32,6272]{2,1,0:T(8,128)(2,1)S(1)} %pack_theirs.1), channel_id=1, source_target_pairs={{0,128},{128,0},{1,129},{129,1},{2,130},{130,2},{3,131},{131,3},{4... | collective-permute-start | bytes 4816904 | tf_op jit(solution)/shard_map/ppermute | solution.py:418
  15.4 13.9 %collective-permute-start.1 = (bf16[32,6272]{1,0:T(8,128)(2,1)S(1)}, bf16[32,6272]{1,0:T(8,128)(2,1)S(1)}, u32[]{:S(2)}, u32[]{:S(2)}) collective-permute-start(bf16[32,6272]{1,0:T(8,128)(2,1)S(1)} %coded_chip_sum.3), channel_id=1, source_target_pairs={{0,64},{32,96},{64,0},{96,32},{1,65},{33,97},{65,1},{97,33},{2,66}... | collective-permute-start | bytes 1204232 | tf_op jit(solution)/shard_map/ppermute | solution.py:410
  18.0 20.7 %collective-permute-start.2 = (bf16[32,6272]{1,0:T(8,128)(2,1)S(1)}, bf16[32,6272]{1,0:T(8,128)(2,1)S(1)}, u32[]{:S(2)}, u32[]{:S(2)}) collective-permute-start(bf16[32,6272]{1,0:T(8,128)(2,1)S(1)} %coded_chip_sum.4), channel_id=1, source_target_pairs={{0,32},{32,64},{64,96},{96,0},{1,33},{33,65},{65,97},{97,1},{2,34}... | collective-permute-start | bytes 1204232 | tf_op jit(solution)/shard_map/ppermute | solution.py:410
  20.5 18.1 %collective-permute-start.3 = (bf16[32,6272]{1,0:T(8,128)(2,1)S(1)}, bf16[32,6272]{1,0:T(8,128)(2,1)S(1)}, u32[]{:S(2)}, u32[]{:S(2)}) collective-permute-start(bf16[32,6272]{1,0:T(8,128)(2,1)S(1)} %coded_chip_sum.5), channel_id=1, source_target_pairs={{0,96},{32,0},{64,32},{96,64},{1,97},{33,1},{65,33},{97,65},{2,98}... | collective-permute-start | bytes 1204232 | tf_op jit(solution)/shard_map/ppermute | solution.py:410
  25.5 30.1 %copy-start = (f32[1,4,12288]{2,1,0:T(4,128)S(1)}, f32[1,4,12288]{2,1,0:T(4,128)}, u32[]{:S(2)}) copy-start(f32[1,4,12288]{2,1,0:T(4,128)} %param.9) | copy-start | bytes 589828
  25.5 30.1 %copy-start.1 = (bf16[1,4,12288]{2,1,0:T(4,128)(2,1)S(1)}, bf16[1,4,12288]{2,1,0:T(4,128)(2,1)}, u32[]{:S(2)}) copy-start(bf16[1,4,12288]{2,1,0:T(4,128)(2,1)} %param.10) | copy-start | bytes 294916
  25.5 30.1 %copy-start.2 = (bf16[1,4,12288]{2,1,0:T(4,128)(2,1)S(1)}, bf16[1,4,12288]{2,1,0:T(4,128)(2,1)}, u32[]{:S(2)}) copy-start(bf16[1,4,12288]{2,1,0:T(4,128)(2,1)} %param.12) | copy-start | bytes 294916
  25.5 30.0 %copy-start.3 = (f32[1,4,96]{2,1,0:T(4,128)S(1)}, f32[1,4,96]{2,1,0:T(4,128)}, u32[]{:S(2)}) copy-start(f32[1,4,96]{2,1,0:T(4,128)} %param.11) | copy-start | bytes 4612
  25.5 30.0 %copy-start.4 = (f32[1,4,96]{2,1,0:T(4,128)S(1)}, f32[1,4,96]{2,1,0:T(4,128)}, u32[]{:S(2)}) copy-start(f32[1,4,96]{2,1,0:T(4,128)} %param.13) | copy-start | bytes 4612
  40.7 14.9 %all-to-all-start = ((bf16[16,4,3200]{2,1,0:T(4,128)(2,1)}), bf16[16,4,3200]{2,1,0:T(4,128)(2,1)S(1)}, u32[]{:S(2)}, u32[]{:S(2)}) async-start(bf16[16,4,3200]{2,1,0:T(4,128)(2,1)} %sum_over_x.1), calls=%async_computation | async-start | bytes 819200 | tf_op jit(solution)/shard_map/all_to_all | solution.py:414
  57.2 17.0 %all-to-all-start.1 = ((bf16[16,4,3072]{2,1,0:T(4,128)(2,1)}), bf16[16,4,3072]{2,1,0:T(4,128)(2,1)S(1)}, u32[]{:S(2)}, u32[]{:S(2)}) async-start(bf16[16,4,3072]{2,1,0:T(4,128)(2,1)} %get-tuple-element.31), calls=%async_computation.1 | async-start | bytes 786432 | tf_op jit(solution)/shard_map/all_to_all | solution.py:414
  63.3 15.8 %collective-permute-start.4 = (f32[4,3072]{1,0:T(4,128)S(1)}, f32[4,3072]{1,0:T(4,128)S(1)}, u32[]{:S(2)}, u32[]{:S(2)}) collective-permute-start(f32[4,3072]{1,0:T(4,128)S(1)} %get-tuple-element.33), channel_id=1, source_target_pairs={{0,256},{256,0},{1,257},{257,1},{2,258},{258,2},{3,259},{259,3},{4... | collective-permute-start | bytes 147464 | tf_op jit(solution)/shard_map/ppermute | solution.py:418
  75.4 21.4 %all-to-all-start.2 = ((bf16[4,32,6144]{2,1,0:T(8,128)(2,1)}), bf16[4,32,6144]{2,1,0:T(8,128)(2,1)S(1)}, u32[]{:S(2)}, u32[]{:S(2)}) async-start(bf16[4,32,6144]{2,1,0:T(8,128)(2,1)} %spread_rows.1), calls=%async_computation.2 | async-start | bytes 3145728 | tf_op jit(solution)/shard_map/all_to_all | solution.py:414
  79.2 5.9 %collective-permute-start.5 = (f32[4,6144]{1,0:T(4,128)S(1)}, f32[4,6144]{1,0:T(4,128)S(1)}, u32[]{:S(2)}, u32[]{:S(2)}) collective-permute-start(f32[4,6144]{1,0:T(4,128)S(1)} %pad_maximum_fusion.mine), channel_id=1, source_target_pairs={{0,128},{128,0},{1,129},{129,1},{2,130},{130,2},{3,131},{131,3},{4... | collective-permute-start | bytes 294920 | tf_op jit(solution)/shard_map/ppermute | solution.py:418
  96.8 8.9 %collective-permute-start.6 = (bf16[4,32,6144]{2,1,0:T(8,128)(2,1)S(1)}, bf16[4,32,6144]{2,1,0:T(8,128)(2,1)S(1)}, u32[]{:S(2)}, u32[]{:S(2)}) collective-permute-start(bf16[4,32,6144]{2,1,0:T(8,128)(2,1)S(1)} %all-to-all-done.2.piece), channel_id=1, source_target_pairs={{0,128},{128,0},{1,129},{129,1},{2,130},{130,2},{3,131},{131,3},{4... | collective-permute-start | bytes 4718600 | tf_op jit(solution)/shard_map/ppermute | solution.py:418

commit v6 on v5

--- a/solution.py
+++ b/solution.py
@@ -454,8 +454,8 @@
     other_gradient = swap(gradient, "c")
     new = states(half, gradient, other_gradient, master, fold, sold)
 
+    low_y, new = lax.optimization_barrier((low_y, new))
     near = exchange(spread(low_y), "x")
-    near, new = lax.optimization_barrier((near, new))
     far = swap(near, "c")
     weights, transposed = place(1 - half, far, place(half, near))
     om, of, ofs, os, oss = [a[None] for a in new]

time: 109 us -> 108 us (level)
  blocking collectives: 0 us -> 19.8 us
  waiting for transfers between devices: 45 us -> 30.1 us
  starting transfers between devices: 44.7 us -> 40.4 us
  Pallas kernels: 16.9 us -> 15.7 us
    all_to_all x0 -> x1, blocking collectives: none -> 19.8 us  [exchange(): return lax.all_to_all(value, axis, 0, 0, tiled=True)]
    all_to_all x3 -> x2, waiting for transfers between devices: 29.4 us -> 14.5 us  [exchange(): return lax.all_to_all(value, axis, 0, 0, tiled=True)]
    all_to_all x3 -> x2, starting transfers between devices: 13.4 us -> 9.44 us  [exchange(): return lax.all_to_all(value, axis, 0, 0, tiled=True)]
    pallas_call x1, Pallas kernels: 1.25 us -> 0.11 us  [spread(): pl.pallas_call(spread_kernel, grid=(1,), in_specs=[pl.BlockSpec((NZ * NY,...]
  transfers between devices with their start and end apart: 10 -> 9, of which waited for: 8 -> 7; matrix products, arithmetic and copies ran while one was open for 0% -> 0% of each run, Pallas kernels for 8% -> 7%
where the time goes in v6:
time: 108 us; the launch traced here: 107 us
  starting transfers between devices  40.4 us (37%)
  waiting for transfers between devices  30.1 us (28%)
  blocking collectives  19.8 us (18%)
  Pallas kernels  15.7 us (15%)
    ppermute x4, starting transfers between devices, swap(): return lax.ppermute(value, axis, [(0, 1), (1, 0)])  22.6 us
    all_to_all x1, blocking collectives, exchange(): return lax.all_to_all(value, axis, 0, 0, tiled=True)  19.8 us
    all_to_all x2, waiting for transfers between devices, exchange(): return lax.all_to_all(value, axis, 0, 0, tiled=True)  14.5 us
    ppermute x3, waiting for transfers between devices, shift_x(): return lax.ppermute(value, 'x', [(i, (i + shift) % NX) for i in range(NX)])  13.1 us
    all_to_all x2, starting transfers between devices, exchange(): return lax.all_to_all(value, axis, 0, 0, tiled=True)  9.44 us
    ppermute x3, starting transfers between devices, shift_x(): return lax.ppermute(value, 'x', [(i, (i + shift) % NX) for i in range(NX)])  8.41 us
    pallas_call x2, Pallas kernels, pack(): pl.pallas_call(pack_kernel, grid_spec=pltpu.PrefetchScalarGridSpec(num_sc...  4.37 us
    pallas_call x2, Pallas kernels, place(): pl.pallas_call(place_kernel, grid_spec=pltpu.PrefetchScalarGridSpec(num_s...  3.87 us
  transfers between devices with their start and end apart: 9, of which 7 were waited for; matrix products, arithmetic and copies ran while one was open for 0% of the time, Pallas kernels for 7%

profile of v6, /device:TPU:1, one launch (start us, length us, event | category | flops | bytes accessed | tf_op | source)
XLA Modules:
  0.0 107.1 jit_solution(6124823874146232303)
XLA Ops:
  0.6 0.1 stack.35.idx
  0.7 2.2 %pack_theirs.1 = bf16[4,32,6272]{2,1,0:T(8,128)(2,1)S(1)} custom-call(s32[5]{0:T(128)S(1)} %stack.35.idx, bf16[128,12288]{1,0:T(8,128)(2,1)} %bitcast.33, bf16[128,12288]{1,0:T(8,128)(2,1)} %bitcast.34, bf16[128,12288]{1,0:T(8,128)(2,1)} %bitcast.35, bf16[128,12288]{1,0:T(8,128)(2,1)} %bitcast.36, bf16[96,128]{1,0:T(8,128)(2,1)} %bitcast.43), custom_call_target="tpu_custom_call" | custom-call | bytes 6291456 | tf_op jit(solution)/shard_map/pack_theirs/pallas_call | solution.py:79
  2.9 8.8 %collective-permute-start = (bf16[4,32,6272]{2,1,0:T(8,128)(2,1)S(1)}, bf16[4,32,6272]{2,1,0:T(8,128)(2,1)S(1)}, u32[]{:S(2)}, u32[]{:S(2)}) collective-permute-start(bf16[4,32,6272]{2,1,0:T(8,128)(2,1)S(1)} %pack_theirs.1), channel_id=1, source_target_pairs={{0,128},{128,0},{1,129},{129,1},{2,130},{130,2},{3,131},{131,3},{4... | collective-permute-start | bytes 4816904 | tf_op jit(solution)/shard_map/ppermute | solution.py:418
  11.7 0.1 stack.33.idx
  11.8 2.2 %pack_mine.1.values.scales = bf16[4,32,6272]{2,1,0:T(8,128)(2,1)S(1)} custom-call(s32[5]{0:T(128)S(1)} %stack.33.idx, bf16[128,12288]{1,0:T(8,128)(2,1)} %bitcast.37, bf16[128,12288]{1,0:T(8,128)(2,1)} %bitcast.38, bf16[128,12288]{1,0:T(8,128)(2,1)} %bitcast.39, bf16[128,12288]{1,0:T(8,128)(2,1)} %bitcast.40, bf16[96,128]{1,0:T(8,128)(2,1)} %bitcast.44), custom_call_target="tpu_custom_call" | custom-call | bytes 6291456 | tf_op jit(solution)/shard_map/pack_mine/pallas_call | solution.py:79
  14.0 0.8 collective-permute-done.there.there_scales
  14.8 0.6 coded_chip_sum.3
  15.4 1.9 %collective-permute-start.1 = (bf16[32,6272]{1,0:T(8,128)(2,1)S(1)}, bf16[32,6272]{1,0:T(8,128)(2,1)S(1)}, u32[]{:S(2)}, u32[]{:S(2)}) collective-permute-start(bf16[32,6272]{1,0:T(8,128)(2,1)S(1)} %coded_chip_sum.3), channel_id=1, source_target_pairs={{0,64},{32,96},{64,0},{96,32},{1,65},{33,97},{65,1},{97,33},{2,66}... | collective-permute-start | bytes 1204232 | tf_op jit(solution)/shard_map/ppermute | solution.py:410
  17.3 0.6 coded_chip_sum.4
  18.0 1.9 %collective-permute-start.2 = (bf16[32,6272]{1,0:T(8,128)(2,1)S(1)}, bf16[32,6272]{1,0:T(8,128)(2,1)S(1)}, u32[]{:S(2)}, u32[]{:S(2)}) collective-permute-start(bf16[32,6272]{1,0:T(8,128)(2,1)S(1)} %coded_chip_sum.4), channel_id=1, source_target_pairs={{0,32},{32,64},{64,96},{96,0},{1,33},{33,65},{65,97},{97,1},{2,34}... | collective-permute-start | bytes 1204232 | tf_op jit(solution)/shard_map/ppermute | solution.py:410
  19.9 0.6 coded_chip_sum.5
  20.5 4.6 %collective-permute-start.3 = (bf16[32,6272]{1,0:T(8,128)(2,1)S(1)}, bf16[32,6272]{1,0:T(8,128)(2,1)S(1)}, u32[]{:S(2)}, u32[]{:S(2)}) collective-permute-start(bf16[32,6272]{1,0:T(8,128)(2,1)S(1)} %coded_chip_sum.5), channel_id=1, source_target_pairs={{0,96},{32,0},{64,32},{96,64},{1,97},{33,1},{65,33},{97,65},{2,98}... | collective-permute-start | bytes 1204232 | tf_op jit(solution)/shard_map/ppermute | solution.py:410
  25.1 0.4 own_chip_sum.1.own
  25.5 0.0 copy-start
  25.5 0.0 copy-start.1
  25.5 0.0 copy-start.2
  25.5 0.0 copy-start.3
  25.5 0.0 copy-start.4
  25.5 3.8 %collective-permute-done.1.c1.s1 = bf16[32,6272]{1,0:T(8,128)(2,1)S(1)} collective-permute-done((bf16[32,6272]{1,0:T(8,128)(2,1)S(1)}, bf16[32,6272]{1,0:T(8,128)(2,1)S(1)}, u32[]{:S(2)}, u32[]{:S(2)}) %collective-permute-start.1) | collective-permute-done | bytes 401440 | tf_op jit(solution)/shard_map/ppermute | solution.py:410
  29.4 9.3 %collective-permute-done.2.c2.s2 = bf16[32,6272]{1,0:T(8,128)(2,1)S(1)} collective-permute-done((bf16[32,6272]{1,0:T(8,128)(2,1)S(1)}, bf16[32,6272]{1,0:T(8,128)(2,1)S(1)}, u32[]{:S(2)}, u32[]{:S(2)}) %collective-permute-start.2) | collective-permute-done | bytes 401440 | tf_op jit(solution)/shard_map/ppermute | solution.py:410
  38.6 0.0 collective-permute-done.3.c3.s3
  38.6 2.0 %sum_over_x.1 = bf16[16,4,3200]{2,1,0:T(4,128)(2,1)} custom-call(f32[32,6144]{1,0:T(8,128)S(1)} %own_chip_sum.1.own, bf16[32,6272]{1,0:T(8,128)(2,1)S(1)} %collective-permute-done.1.c1.s1, bf16[32,6272]{1,0:T(8,128)(2,1)S(1)} %collective-permute-done.1.c1.s1, bf16[32,6272]{1,0:T(8,128)(2,1)S(1)} %collective-permute-done.2.c2.s2, ...), custom_call_target="tpu_custom_call" | custom-call | flops 11796480 | bytes 2359296 | tf_op jit(solution)/shard_map/sum_over_x/pallas_call | solution.py:181
  40.7 3.6 %all-to-all-start = ((bf16[16,4,3200]{2,1,0:T(4,128)(2,1)}), bf16[16,4,3200]{2,1,0:T(4,128)(2,1)S(1)}, u32[]{:S(2)}, u32[]{:S(2)}) async-start(bf16[16,4,3200]{2,1,0:T(4,128)(2,1)} %sum_over_x.1), calls=%async_computation | async-start | bytes 819200 | tf_op jit(solution)/shard_map/all_to_all | solution.py:414
  44.3 11.3 %all-to-all-done.codes.steps = bf16[16,4,3200]{2,1,0:T(4,128)(2,1)S(1)} async-done(((bf16[16,4,3200]{2,1,0:T(4,128)(2,1)}), bf16[16,4,3200]{2,1,0:T(4,128)(2,1)S(1)}, u32[]{:S(2)}, u32[]{:S(2)}) %all-to-all-start) | async-done | bytes 409632 | tf_op jit(solution)/shard_map/all_to_all | solution.py:414
  55.5 0.0 copy-done
  55.5 0.0 copy-done.1
  55.5 0.0 copy-done.2
  55.6 0.0 copy-done.3
  55.6 0.0 copy-done.4
  55.6 1.6 %sum_and_low_weights.1 = (f32[4,3072]{1,0:T(4,128)S(1)}, bf16[16,4,3072]{2,1,0:T(4,128)(2,1)}) custom-call(s32[1]{0:T(128)} %bitcast.idx, bf16[16,4,3200]{2,1,0:T(4,128)(2,1)S(1)} %all-to-all-done.codes.steps, bf16[16,4,3200]{2,1,0:T(4,128)(2,1)S(1)} %all-to-all-done.codes.steps, f32[4,12288]{1,0:T(4,128)S(1)} %bitcast.23, bf16[4,12288]{1,0:T(4,128)(2,1)S(1)} %bitcast.25, ...), custom_call_target="tpu_custom_call" | custom-call | flops 5898240 | bytes 1572864 | tf_op jit(solution)/shard_map/sum_and_low_weights/pallas_call | solution.py:229
  57.2 2.5 %collective-permute-start.4 = (f32[4,3072]{1,0:T(4,128)S(1)}, f32[4,3072]{1,0:T(4,128)S(1)}, u32[]{:S(2)}, u32[]{:S(2)}) collective-permute-start(f32[4,3072]{1,0:T(4,128)S(1)} %get-tuple-element.33), channel_id=1, source_target_pairs={{0,256},{256,0},{1,257},{257,1},{2,258},{258,2},{3,259},{259,3},{4... | collective-permute-start | bytes 147464 | tf_op jit(solution)/shard_map/ppermute | solution.py:418
  59.7 5.9 %all-to-all-start.1 = ((bf16[16,4,3072]{2,1,0:T(4,128)(2,1)}), bf16[16,4,3072]{2,1,0:T(4,128)(2,1)S(1)}, u32[]{:S(2)}, u32[]{:S(2)}) async-start(bf16[16,4,3072]{2,1,0:T(4,128)(2,1)} %get-tuple-element.31), calls=%async_computation.1 | async-start | bytes 786432 | tf_op jit(solution)/shard_map/all_to_all | solution.py:414
  65.6 0.0 collective-permute-done.4
  65.6 4.0 %collective-permute-start.5 = (f32[4,6144]{1,0:T(4,128)S(1)}, f32[4,6144]{1,0:T(4,128)S(1)}, u32[]{:S(2)}, u32[]{:S(2)}) collective-permute-start(f32[4,6144]{1,0:T(4,128)S(1)} %pad_maximum_fusion.mine), channel_id=1, source_target_pairs={{0,128},{128,0},{1,129},{129,1},{2,130},{130,2},{3,131},{131,3},{4... | collective-permute-start | bytes 294920 | tf_op jit(solution)/shard_map/ppermute | solution.py:418
  69.7 0.3 old_moments.1
  70.0 0.6 collective-permute-done.5.other
  70.6 1.2 %new_states.1 = (f32[4,12288]{1,0:T(4,128)}, bf16[4,12288]{1,0:T(4,128)(2,1)}, f32[4,96]{1,0:T(4,128)}, bf16[4,12288]{1,0:T(4,128)(2,1)}, f32[4,96]{1,0:T(4,128)}) custom-call(s32[1]{0:T(128)} %bitcast.1.idx, f32[4,6144]{1,0:T(4,128)S(1)} %pad_maximum_fusion.mine, f32[4,6144]{1,0:T(4,128)S(1)} %collective-permute-done.5.other, f32[4,12288]{1,0:T(4,128)S(1)} %bitcast.24, ...), custom_call_target="tpu_custom_call" | custom-call | flops 49152 | bytes 49152 | tf_op jit(solution)/shard_map/new_states/pallas_call | solution.py:334
  71.8 3.2 %all-to-all-done.1.low = bf16[16,4,3072]{2,1,0:T(4,128)(2,1)S(1)} async-done(((bf16[16,4,3072]{2,1,0:T(4,128)(2,1)}), bf16[16,4,3072]{2,1,0:T(4,128)(2,1)S(1)}, u32[]{:S(2)}, u32[]{:S(2)}) %all-to-all-start.1) | async-done | bytes 393248 | tf_op jit(solution)/shard_map/all_to_all | solution.py:414
  75.0 0.1 spread_rows.1
  75.1 19.8 %all_to_all.15.piece = bf16[4,32,6144]{2,1,0:T(8,128)(2,1)S(1)} all-to-all(bf16[4,32,6144]{2,1,0:T(8,128)(2,1)S(1)} %spread_rows.1), channel_id=1, replica_groups=mesh['zl'=2,'c'=2,'x'=4,'y'=8,'zh'=4] {'x'}, dimensions={0} | all-to-all | bytes 3145728 | tf_op jit(solution)/shard_map/all_to_all | solution.py:414
  94.9 7.3 %collective-permute-start.6 = (bf16[4,32,6144]{2,1,0:T(8,128)(2,1)S(1)}, bf16[4,32,6144]{2,1,0:T(8,128)(2,1)S(1)}, u32[]{:S(2)}, u32[]{:S(2)}) collective-permute-start(bf16[4,32,6144]{2,1,0:T(8,128)(2,1)S(1)} %all_to_all.15.piece), channel_id=1, source_target_pairs={{0,128},{128,0},{1,129},{129,1},{2,130},{130,2},{3,131},{131,3},{4... | collective-permute-start | bytes 4718600 | tf_op jit(solution)/shard_map/ppermute | solution.py:418
  102.2 1.9 %place_weights.2 = (bf16[128,12288]{1,0:T(8,128)(2,1)}, bf16[12288,128]{1,0:T(8,128)(2,1)}) custom-call(s32[1]{0:T(128)} %bitcast.1.idx, bf16[4,32,6144]{2,1,0:T(8,128)(2,1)S(1)} %all_to_all.15.piece), custom_call_target="tpu_custom_call" | custom-call | bytes 4718592 | tf_op jit(solution)/shard_map/place_weights/pallas_call | solution.py:386
  104.1 1.1 collective-permute-done.6.piece
  105.2 1.9 %place_weights.3 = (bf16[128,12288]{1,0:T(8,128)(2,1)}, bf16[12288,128]{1,0:T(8,128)(2,1)}) custom-call(s32[1]{0:T(128)S(6)} %sub.7.idx, bf16[4,32,6144]{2,1,0:T(8,128)(2,1)S(1)} %collective-permute-done.6.piece, bf16[128,12288]{1,0:T(8,128)(2,1)} %get-tuple-element.51.refs_0_, ...), custom_call_target="tpu_custom_call", output_to_operand_aliasing={{0}: (2, {}), {1}: (3, {})} | custom-call | bytes 4718592 | tf_op jit(solution)/shard_map/place_weights/pallas_call | solution.py:386
  (2 shorter events, 0.0 us)
Async XLA Ops:
  2.9 11.9 %collective-permute-start = (bf16[4,32,6272]{2,1,0:T(8,128)(2,1)S(1)}, bf16[4,32,6272]{2,1,0:T(8,128)(2,1)S(1)}, u32[]{:S(2)}, u32[]{:S(2)}) collective-permute-start(bf16[4,32,6272]{2,1,0:T(8,128)(2,1)S(1)} %pack_theirs.1), channel_id=1, source_target_pairs={{0,128},{128,0},{1,129},{129,1},{2,130},{130,2},{3,131},{131,3},{4... | collective-permute-start | bytes 4816904 | tf_op jit(solution)/shard_map/ppermute | solution.py:418
  15.4 13.9 %collective-permute-start.1 = (bf16[32,6272]{1,0:T(8,128)(2,1)S(1)}, bf16[32,6272]{1,0:T(8,128)(2,1)S(1)}, u32[]{:S(2)}, u32[]{:S(2)}) collective-permute-start(bf16[32,6272]{1,0:T(8,128)(2,1)S(1)} %coded_chip_sum.3), channel_id=1, source_target_pairs={{0,64},{32,96},{64,0},{96,32},{1,65},{33,97},{65,1},{97,33},{2,66}... | collective-permute-start | bytes 1204232 | tf_op jit(solution)/shard_map/ppermute | solution.py:410
  18.0 20.7 %collective-permute-start.2 = (bf16[32,6272]{1,0:T(8,128)(2,1)S(1)}, bf16[32,6272]{1,0:T(8,128)(2,1)S(1)}, u32[]{:S(2)}, u32[]{:S(2)}) collective-permute-start(bf16[32,6272]{1,0:T(8,128)(2,1)S(1)} %coded_chip_sum.4), channel_id=1, source_target_pairs={{0,32},{32,64},{64,96},{96,0},{1,33},{33,65},{65,97},{97,1},{2,34}... | collective-permute-start | bytes 1204232 | tf_op jit(solution)/shard_map/ppermute | solution.py:410
  20.5 18.1 %collective-permute-start.3 = (bf16[32,6272]{1,0:T(8,128)(2,1)S(1)}, bf16[32,6272]{1,0:T(8,128)(2,1)S(1)}, u32[]{:S(2)}, u32[]{:S(2)}) collective-permute-start(bf16[32,6272]{1,0:T(8,128)(2,1)S(1)} %coded_chip_sum.5), channel_id=1, source_target_pairs={{0,96},{32,0},{64,32},{96,64},{1,97},{33,1},{65,33},{97,65},{2,98}... | collective-permute-start | bytes 1204232 | tf_op jit(solution)/shard_map/ppermute | solution.py:410
  25.5 30.1 %copy-start = (f32[1,4,12288]{2,1,0:T(4,128)S(1)}, f32[1,4,12288]{2,1,0:T(4,128)}, u32[]{:S(2)}) copy-start(f32[1,4,12288]{2,1,0:T(4,128)} %param.9) | copy-start | bytes 589828
  25.5 30.1 %copy-start.1 = (bf16[1,4,12288]{2,1,0:T(4,128)(2,1)S(1)}, bf16[1,4,12288]{2,1,0:T(4,128)(2,1)}, u32[]{:S(2)}) copy-start(bf16[1,4,12288]{2,1,0:T(4,128)(2,1)} %param.10) | copy-start | bytes 294916
  25.5 30.1 %copy-start.2 = (bf16[1,4,12288]{2,1,0:T(4,128)(2,1)S(1)}, bf16[1,4,12288]{2,1,0:T(4,128)(2,1)}, u32[]{:S(2)}) copy-start(bf16[1,4,12288]{2,1,0:T(4,128)(2,1)} %param.12) | copy-start | bytes 294916
  25.5 30.0 %copy-start.3 = (f32[1,4,96]{2,1,0:T(4,128)S(1)}, f32[1,4,96]{2,1,0:T(4,128)}, u32[]{:S(2)}) copy-start(f32[1,4,96]{2,1,0:T(4,128)} %param.11) | copy-start | bytes 4612
  25.5 30.0 %copy-start.4 = (f32[1,4,96]{2,1,0:T(4,128)S(1)}, f32[1,4,96]{2,1,0:T(4,128)}, u32[]{:S(2)}) copy-start(f32[1,4,96]{2,1,0:T(4,128)} %param.13) | copy-start | bytes 4612
  40.7 14.9 %all-to-all-start = ((bf16[16,4,3200]{2,1,0:T(4,128)(2,1)}), bf16[16,4,3200]{2,1,0:T(4,128)(2,1)S(1)}, u32[]{:S(2)}, u32[]{:S(2)}) async-start(bf16[16,4,3200]{2,1,0:T(4,128)(2,1)} %sum_over_x.1), calls=%async_computation | async-start | bytes 819200 | tf_op jit(solution)/shard_map/all_to_all | solution.py:414
  57.2 8.4 %collective-permute-start.4 = (f32[4,3072]{1,0:T(4,128)S(1)}, f32[4,3072]{1,0:T(4,128)S(1)}, u32[]{:S(2)}, u32[]{:S(2)}) collective-permute-start(f32[4,3072]{1,0:T(4,128)S(1)} %get-tuple-element.33), channel_id=1, source_target_pairs={{0,256},{256,0},{1,257},{257,1},{2,258},{258,2},{3,259},{259,3},{4... | collective-permute-start | bytes 147464 | tf_op jit(solution)/shard_map/ppermute | solution.py:418
  59.7 15.3 %all-to-all-start.1 = ((bf16[16,4,3072]{2,1,0:T(4,128)(2,1)}), bf16[16,4,3072]{2,1,0:T(4,128)(2,1)S(1)}, u32[]{:S(2)}, u32[]{:S(2)}) async-start(bf16[16,4,3072]{2,1,0:T(4,128)(2,1)} %get-tuple-element.31), calls=%async_computation.1 | async-start | bytes 786432 | tf_op jit(solution)/shard_map/all_to_all | solution.py:414
  65.6 5.0 %collective-permute-start.5 = (f32[4,6144]{1,0:T(4,128)S(1)}, f32[4,6144]{1,0:T(4,128)S(1)}, u32[]{:S(2)}, u32[]{:S(2)}) collective-permute-start(f32[4,6144]{1,0:T(4,128)S(1)} %pad_maximum_fusion.mine), channel_id=1, source_target_pairs={{0,128},{128,0},{1,129},{129,1},{2,130},{130,2},{3,131},{131,3},{4... | collective-permute-start | bytes 294920 | tf_op jit(solution)/shard_map/ppermute | solution.py:418
  94.9 10.3 %collective-permute-start.6 = (bf16[4,32,6144]{2,1,0:T(8,128)(2,1)S(1)}, bf16[4,32,6144]{2,1,0:T(8,128)(2,1)S(1)}, u32[]{:S(2)}, u32[]{:S(2)}) collective-permute-start(bf16[4,32,6144]{2,1,0:T(8,128)(2,1)S(1)} %all_to_all.15.piece), channel_id=1, source_target_pairs={{0,128},{128,0},{1,129},{129,1},{2,130},{130,2},{3,131},{131,3},{4... | collective-permute-start | bytes 4718600 | tf_op jit(solution)/shard_map/ppermute | solution.py:418

commit v7 on v6

--- a/solution.py
+++ b/solution.py
@@ -21,7 +21,7 @@
 QB = NB // 4
 PAD = HALF + BLOCK
 QPAD = QUARTER + BLOCK
-CH = 3072
+CH = 2048
 SPAN = 172.0
 OFFSET = 86.0
 

time: 108 us -> 109 us (level)
  no operation moved by 1% of the time
where the time goes in v7:
time: 109 us; the launch traced here: 107 us
  starting transfers between devices  40.4 us (37%)
  waiting for transfers between devices  29.8 us (27%)
  blocking collectives  19.8 us (18%)
  Pallas kernels  16.2 us (15%)
    ppermute x4, starting transfers between devices, swap(): return lax.ppermute(value, axis, [(0, 1), (1, 0)])  22.6 us
    all_to_all x1, blocking collectives, exchange(): return lax.all_to_all(value, axis, 0, 0, tiled=True)  19.8 us
    all_to_all x2, waiting for transfers between devices, exchange(): return lax.all_to_all(value, axis, 0, 0, tiled=True)  14.5 us
    ppermute x3, waiting for transfers between devices, shift_x(): return lax.ppermute(value, 'x', [(i, (i + shift) % NX) for i in range(NX)])  13.1 us
    all_to_all x2, starting transfers between devices, exchange(): return lax.all_to_all(value, axis, 0, 0, tiled=True)  9.44 us
    ppermute x3, starting transfers between devices, shift_x(): return lax.ppermute(value, 'x', [(i, (i + shift) % NX) for i in range(NX)])  8.41 us
    pallas_call x2, Pallas kernels, place(): pl.pallas_call(place_kernel, grid_spec=pltpu.PrefetchScalarGridSpec(num_s...  4.39 us
    pallas_call x2, Pallas kernels, pack(): pl.pallas_call(pack_kernel, grid_spec=pltpu.PrefetchScalarGridSpec(num_sc...  4.37 us
  transfers between devices with their start and end apart: 9, of which 7 were waited for; matrix products, arithmetic and copies ran while one was open for 0% of the time, Pallas kernels for 7%

profile of v7, /device:TPU:1, one launch (start us, length us, event | category | flops | bytes accessed | tf_op | source)
XLA Modules:
  0.0 107.4 jit_solution(17073179550653827593)
XLA Ops:
  0.6 0.1 stack.35.idx
  0.7 2.2 %pack_theirs.1 = bf16[4,32,6272]{2,1,0:T(8,128)(2,1)S(1)} custom-call(s32[5]{0:T(128)S(1)} %stack.35.idx, bf16[128,12288]{1,0:T(8,128)(2,1)} %bitcast.33, bf16[128,12288]{1,0:T(8,128)(2,1)} %bitcast.34, bf16[128,12288]{1,0:T(8,128)(2,1)} %bitcast.35, bf16[128,12288]{1,0:T(8,128)(2,1)} %bitcast.36, bf16[96,128]{1,0:T(8,128)(2,1)} %bitcast.43), custom_call_target="tpu_custom_call" | custom-call | bytes 6291456 | tf_op jit(solution)/shard_map/pack_theirs/pallas_call | solution.py:79
  2.9 8.8 %collective-permute-start = (bf16[4,32,6272]{2,1,0:T(8,128)(2,1)S(1)}, bf16[4,32,6272]{2,1,0:T(8,128)(2,1)S(1)}, u32[]{:S(2)}, u32[]{:S(2)}) collective-permute-start(bf16[4,32,6272]{2,1,0:T(8,128)(2,1)S(1)} %pack_theirs.1), channel_id=1, source_target_pairs={{0,128},{128,0},{1,129},{129,1},{2,130},{130,2},{3,131},{131,3},{4... | collective-permute-start | bytes 4816904 | tf_op jit(solution)/shard_map/ppermute | solution.py:418
  11.7 0.1 stack.33.idx
  11.8 2.2 %pack_mine.1.values.scales = bf16[4,32,6272]{2,1,0:T(8,128)(2,1)S(1)} custom-call(s32[5]{0:T(128)S(1)} %stack.33.idx, bf16[128,12288]{1,0:T(8,128)(2,1)} %bitcast.37, bf16[128,12288]{1,0:T(8,128)(2,1)} %bitcast.38, bf16[128,12288]{1,0:T(8,128)(2,1)} %bitcast.39, bf16[128,12288]{1,0:T(8,128)(2,1)} %bitcast.40, bf16[96,128]{1,0:T(8,128)(2,1)} %bitcast.44), custom_call_target="tpu_custom_call" | custom-call | bytes 6291456 | tf_op jit(solution)/shard_map/pack_mine/pallas_call | solution.py:79
  14.0 0.8 collective-permute-done.there.there_scales
  14.8 0.6 coded_chip_sum.3
  15.4 1.9 %collective-permute-start.1 = (bf16[32,6272]{1,0:T(8,128)(2,1)S(1)}, bf16[32,6272]{1,0:T(8,128)(2,1)S(1)}, u32[]{:S(2)}, u32[]{:S(2)}) collective-permute-start(bf16[32,6272]{1,0:T(8,128)(2,1)S(1)} %coded_chip_sum.3), channel_id=1, source_target_pairs={{0,64},{32,96},{64,0},{96,32},{1,65},{33,97},{65,1},{97,33},{2,66}... | collective-permute-start | bytes 1204232 | tf_op jit(solution)/shard_map/ppermute | solution.py:410
  17.3 0.6 coded_chip_sum.4
  18.0 1.9 %collective-permute-start.2 = (bf16[32,6272]{1,0:T(8,128)(2,1)S(1)}, bf16[32,6272]{1,0:T(8,128)(2,1)S(1)}, u32[]{:S(2)}, u32[]{:S(2)}) collective-permute-start(bf16[32,6272]{1,0:T(8,128)(2,1)S(1)} %coded_chip_sum.4), channel_id=1, source_target_pairs={{0,32},{32,64},{64,96},{96,0},{1,33},{33,65},{65,97},{97,1},{2,34}... | collective-permute-start | bytes 1204232 | tf_op jit(solution)/shard_map/ppermute | solution.py:410
  19.9 0.6 coded_chip_sum.5
  20.5 4.6 %collective-permute-start.3 = (bf16[32,6272]{1,0:T(8,128)(2,1)S(1)}, bf16[32,6272]{1,0:T(8,128)(2,1)S(1)}, u32[]{:S(2)}, u32[]{:S(2)}) collective-permute-start(bf16[32,6272]{1,0:T(8,128)(2,1)S(1)} %coded_chip_sum.5), channel_id=1, source_target_pairs={{0,96},{32,0},{64,32},{96,64},{1,97},{33,1},{65,33},{97,65},{2,98}... | collective-permute-start | bytes 1204232 | tf_op jit(solution)/shard_map/ppermute | solution.py:410
  25.1 0.4 own_chip_sum.1.own
  25.5 0.0 copy-start
  25.5 0.0 copy-start.1
  25.5 0.0 copy-start.2
  25.5 0.0 copy-start.3
  25.5 0.0 copy-start.4
  25.5 3.8 %collective-permute-done.1.c1.s1 = bf16[32,6272]{1,0:T(8,128)(2,1)S(1)} collective-permute-done((bf16[32,6272]{1,0:T(8,128)(2,1)S(1)}, bf16[32,6272]{1,0:T(8,128)(2,1)S(1)}, u32[]{:S(2)}, u32[]{:S(2)}) %collective-permute-start.1) | collective-permute-done | bytes 401440 | tf_op jit(solution)/shard_map/ppermute | solution.py:410
  29.4 9.3 %collective-permute-done.2.c2.s2 = bf16[32,6272]{1,0:T(8,128)(2,1)S(1)} collective-permute-done((bf16[32,6272]{1,0:T(8,128)(2,1)S(1)}, bf16[32,6272]{1,0:T(8,128)(2,1)S(1)}, u32[]{:S(2)}, u32[]{:S(2)}) %collective-permute-start.2) | collective-permute-done | bytes 401440 | tf_op jit(solution)/shard_map/ppermute | solution.py:410
  38.6 0.0 collective-permute-done.3.c3.s3
  38.6 2.0 %sum_over_x.1 = bf16[16,4,3200]{2,1,0:T(4,128)(2,1)} custom-call(f32[32,6144]{1,0:T(8,128)S(1)} %own_chip_sum.1.own, bf16[32,6272]{1,0:T(8,128)(2,1)S(1)} %collective-permute-done.1.c1.s1, bf16[32,6272]{1,0:T(8,128)(2,1)S(1)} %collective-permute-done.1.c1.s1, bf16[32,6272]{1,0:T(8,128)(2,1)S(1)} %collective-permute-done.2.c2.s2, ...), custom_call_target="tpu_custom_call" | custom-call | flops 11796480 | bytes 2359296 | tf_op jit(solution)/shard_map/sum_over_x/pallas_call | solution.py:181
  40.7 3.6 %all-to-all-start = ((bf16[16,4,3200]{2,1,0:T(4,128)(2,1)}), bf16[16,4,3200]{2,1,0:T(4,128)(2,1)S(1)}, u32[]{:S(2)}, u32[]{:S(2)}) async-start(bf16[16,4,3200]{2,1,0:T(4,128)(2,1)} %sum_over_x.1), calls=%async_computation | async-start | bytes 819200 | tf_op jit(solution)/shard_map/all_to_all | solution.py:414
  44.3 11.3 %all-to-all-done.codes.steps = bf16[16,4,3200]{2,1,0:T(4,128)(2,1)S(1)} async-done(((bf16[16,4,3200]{2,1,0:T(4,128)(2,1)}), bf16[16,4,3200]{2,1,0:T(4,128)(2,1)S(1)}, u32[]{:S(2)}, u32[]{:S(2)}) %all-to-all-start) | async-done | bytes 409632 | tf_op jit(solution)/shard_map/all_to_all | solution.py:414
  55.5 0.0 copy-done
  55.5 0.0 copy-done.1
  55.5 0.0 copy-done.2
  55.6 0.0 copy-done.3
  55.6 0.0 copy-done.4
  55.6 1.6 %sum_and_low_weights.1 = (f32[4,3072]{1,0:T(4,128)S(1)}, bf16[16,4,3072]{2,1,0:T(4,128)(2,1)}) custom-call(s32[1]{0:T(128)} %bitcast.idx, bf16[16,4,3200]{2,1,0:T(4,128)(2,1)S(1)} %all-to-all-done.codes.steps, bf16[16,4,3200]{2,1,0:T(4,128)(2,1)S(1)} %all-to-all-done.codes.steps, f32[4,12288]{1,0:T(4,128)S(1)} %bitcast.23, bf16[4,12288]{1,0:T(4,128)(2,1)S(1)} %bitcast.25, ...), custom_call_target="tpu_custom_call" | custom-call | flops 5898240 | bytes 1572864 | tf_op jit(solution)/shard_map/sum_and_low_weights/pallas_call | solution.py:229
  57.2 2.5 %collective-permute-start.4 = (f32[4,3072]{1,0:T(4,128)S(1)}, f32[4,3072]{1,0:T(4,128)S(1)}, u32[]{:S(2)}, u32[]{:S(2)}) collective-permute-start(f32[4,3072]{1,0:T(4,128)S(1)} %get-tuple-element.33), channel_id=1, source_target_pairs={{0,256},{256,0},{1,257},{257,1},{2,258},{258,2},{3,259},{259,3},{4... | collective-permute-start | bytes 147464 | tf_op jit(solution)/shard_map/ppermute | solution.py:418
  59.7 5.9 %all-to-all-start.1 = ((bf16[16,4,3072]{2,1,0:T(4,128)(2,1)}), bf16[16,4,3072]{2,1,0:T(4,128)(2,1)S(1)}, u32[]{:S(2)}, u32[]{:S(2)}) async-start(bf16[16,4,3072]{2,1,0:T(4,128)(2,1)} %get-tuple-element.31), calls=%async_computation.1 | async-start | bytes 786432 | tf_op jit(solution)/shard_map/all_to_all | solution.py:414
  65.6 0.0 collective-permute-done.4
  65.6 4.0 %collective-permute-start.5 = (f32[4,6144]{1,0:T(4,128)S(1)}, f32[4,6144]{1,0:T(4,128)S(1)}, u32[]{:S(2)}, u32[]{:S(2)}) collective-permute-start(f32[4,6144]{1,0:T(4,128)S(1)} %pad_maximum_fusion.mine), channel_id=1, source_target_pairs={{0,128},{128,0},{1,129},{129,1},{2,130},{130,2},{3,131},{131,3},{4... | collective-permute-start | bytes 294920 | tf_op jit(solution)/shard_map/ppermute | solution.py:418
  69.7 0.3 old_moments.1
  70.0 0.6 collective-permute-done.5.other
  70.6 1.2 %new_states.1 = (f32[4,12288]{1,0:T(4,128)}, bf16[4,12288]{1,0:T(4,128)(2,1)}, f32[4,96]{1,0:T(4,128)}, bf16[4,12288]{1,0:T(4,128)(2,1)}, f32[4,96]{1,0:T(4,128)}) custom-call(s32[1]{0:T(128)} %bitcast.1.idx, f32[4,6144]{1,0:T(4,128)S(1)} %pad_maximum_fusion.mine, f32[4,6144]{1,0:T(4,128)S(1)} %collective-permute-done.5.other, f32[4,12288]{1,0:T(4,128)S(1)} %bitcast.24, ...), custom_call_target="tpu_custom_call" | custom-call | flops 49152 | bytes 49152 | tf_op jit(solution)/shard_map/new_states/pallas_call | solution.py:334
  71.8 3.2 %all-to-all-done.1.low = bf16[16,4,3072]{2,1,0:T(4,128)(2,1)S(1)} async-done(((bf16[16,4,3072]{2,1,0:T(4,128)(2,1)}), bf16[16,4,3072]{2,1,0:T(4,128)(2,1)S(1)}, u32[]{:S(2)}, u32[]{:S(2)}) %all-to-all-start.1) | async-done | bytes 393248 | tf_op jit(solution)/shard_map/all_to_all | solution.py:414
  75.0 0.1 spread_rows.1
  75.1 19.8 %all_to_all.15.piece = bf16[4,32,6144]{2,1,0:T(8,128)(2,1)S(1)} all-to-all(bf16[4,32,6144]{2,1,0:T(8,128)(2,1)S(1)} %spread_rows.1), channel_id=1, replica_groups=mesh['zl'=2,'c'=2,'x'=4,'y'=8,'zh'=4] {'x'}, dimensions={0} | all-to-all | bytes 3145728 | tf_op jit(solution)/shard_map/all_to_all | solution.py:414
  94.9 7.3 %collective-permute-start.6 = (bf16[4,32,6144]{2,1,0:T(8,128)(2,1)S(1)}, bf16[4,32,6144]{2,1,0:T(8,128)(2,1)S(1)}, u32[]{:S(2)}, u32[]{:S(2)}) collective-permute-start(bf16[4,32,6144]{2,1,0:T(8,128)(2,1)S(1)} %all_to_all.15.piece), channel_id=1, source_target_pairs={{0,128},{128,0},{1,129},{129,1},{2,130},{130,2},{3,131},{131,3},{4... | collective-permute-start | bytes 4718600 | tf_op jit(solution)/shard_map/ppermute | solution.py:418
  102.2 2.2 %place_weights.2 = (bf16[128,12288]{1,0:T(8,128)(2,1)}, bf16[12288,128]{1,0:T(8,128)(2,1)}) custom-call(s32[1]{0:T(128)} %bitcast.1.idx, bf16[4,32,6144]{2,1,0:T(8,128)(2,1)S(1)} %all_to_all.15.piece), custom_call_target="tpu_custom_call" | custom-call | bytes 4718592 | tf_op jit(solution)/shard_map/place_weights/pallas_call | solution.py:386
  104.4 0.8 collective-permute-done.6.piece
  105.2 2.2 %place_weights.3 = (bf16[128,12288]{1,0:T(8,128)(2,1)}, bf16[12288,128]{1,0:T(8,128)(2,1)}) custom-call(s32[1]{0:T(128)S(6)} %sub.7.idx, bf16[4,32,6144]{2,1,0:T(8,128)(2,1)S(1)} %collective-permute-done.6.piece, bf16[128,12288]{1,0:T(8,128)(2,1)} %get-tuple-element.51.refs_0_, ...), custom_call_target="tpu_custom_call", output_to_operand_aliasing={{0}: (2, {}), {1}: (3, {})} | custom-call | bytes 4718592 | tf_op jit(solution)/shard_map/place_weights/pallas_call | solution.py:386
  (2 shorter events, 0.0 us)
Async XLA Ops:
  2.9 11.9 %collective-permute-start = (bf16[4,32,6272]{2,1,0:T(8,128)(2,1)S(1)}, bf16[4,32,6272]{2,1,0:T(8,128)(2,1)S(1)}, u32[]{:S(2)}, u32[]{:S(2)}) collective-permute-start(bf16[4,32,6272]{2,1,0:T(8,128)(2,1)S(1)} %pack_theirs.1), channel_id=1, source_target_pairs={{0,128},{128,0},{1,129},{129,1},{2,130},{130,2},{3,131},{131,3},{4... | collective-permute-start | bytes 4816904 | tf_op jit(solution)/shard_map/ppermute | solution.py:418
  15.4 13.9 %collective-permute-start.1 = (bf16[32,6272]{1,0:T(8,128)(2,1)S(1)}, bf16[32,6272]{1,0:T(8,128)(2,1)S(1)}, u32[]{:S(2)}, u32[]{:S(2)}) collective-permute-start(bf16[32,6272]{1,0:T(8,128)(2,1)S(1)} %coded_chip_sum.3), channel_id=1, source_target_pairs={{0,64},{32,96},{64,0},{96,32},{1,65},{33,97},{65,1},{97,33},{2,66}... | collective-permute-start | bytes 1204232 | tf_op jit(solution)/shard_map/ppermute | solution.py:410
  18.0 20.7 %collective-permute-start.2 = (bf16[32,6272]{1,0:T(8,128)(2,1)S(1)}, bf16[32,6272]{1,0:T(8,128)(2,1)S(1)}, u32[]{:S(2)}, u32[]{:S(2)}) collective-permute-start(bf16[32,6272]{1,0:T(8,128)(2,1)S(1)} %coded_chip_sum.4), channel_id=1, source_target_pairs={{0,32},{32,64},{64,96},{96,0},{1,33},{33,65},{65,97},{97,1},{2,34}... | collective-permute-start | bytes 1204232 | tf_op jit(solution)/shard_map/ppermute | solution.py:410
  20.5 18.1 %collective-permute-start.3 = (bf16[32,6272]{1,0:T(8,128)(2,1)S(1)}, bf16[32,6272]{1,0:T(8,128)(2,1)S(1)}, u32[]{:S(2)}, u32[]{:S(2)}) collective-permute-start(bf16[32,6272]{1,0:T(8,128)(2,1)S(1)} %coded_chip_sum.5), channel_id=1, source_target_pairs={{0,96},{32,0},{64,32},{96,64},{1,97},{33,1},{65,33},{97,65},{2,98}... | collective-permute-start | bytes 1204232 | tf_op jit(solution)/shard_map/ppermute | solution.py:410
  25.5 30.1 %copy-start = (f32[1,4,12288]{2,1,0:T(4,128)S(1)}, f32[1,4,12288]{2,1,0:T(4,128)}, u32[]{:S(2)}) copy-start(f32[1,4,12288]{2,1,0:T(4,128)} %param.9) | copy-start | bytes 589828
  25.5 30.1 %copy-start.1 = (bf16[1,4,12288]{2,1,0:T(4,128)(2,1)S(1)}, bf16[1,4,12288]{2,1,0:T(4,128)(2,1)}, u32[]{:S(2)}) copy-start(bf16[1,4,12288]{2,1,0:T(4,128)(2,1)} %param.10) | copy-start | bytes 294916
  25.5 30.1 %copy-start.2 = (bf16[1,4,12288]{2,1,0:T(4,128)(2,1)S(1)}, bf16[1,4,12288]{2,1,0:T(4,128)(2,1)}, u32[]{:S(2)}) copy-start(bf16[1,4,12288]{2,1,0:T(4,128)(2,1)} %param.12) | copy-start | bytes 294916
  25.5 30.0 %copy-start.3 = (f32[1,4,96]{2,1,0:T(4,128)S(1)}, f32[1,4,96]{2,1,0:T(4,128)}, u32[]{:S(2)}) copy-start(f32[1,4,96]{2,1,0:T(4,128)} %param.11) | copy-start | bytes 4612
  25.5 30.0 %copy-start.4 = (f32[1,4,96]{2,1,0:T(4,128)S(1)}, f32[1,4,96]{2,1,0:T(4,128)}, u32[]{:S(2)}) copy-start(f32[1,4,96]{2,1,0:T(4,128)} %param.13) | copy-start | bytes 4612
  40.7 14.9 %all-to-all-start = ((bf16[16,4,3200]{2,1,0:T(4,128)(2,1)}), bf16[16,4,3200]{2,1,0:T(4,128)(2,1)S(1)}, u32[]{:S(2)}, u32[]{:S(2)}) async-start(bf16[16,4,3200]{2,1,0:T(4,128)(2,1)} %sum_over_x.1), calls=%async_computation | async-start | bytes 819200 | tf_op jit(solution)/shard_map/all_to_all | solution.py:414
  57.2 8.4 %collective-permute-start.4 = (f32[4,3072]{1,0:T(4,128)S(1)}, f32[4,3072]{1,0:T(4,128)S(1)}, u32[]{:S(2)}, u32[]{:S(2)}) collective-permute-start(f32[4,3072]{1,0:T(4,128)S(1)} %get-tuple-element.33), channel_id=1, source_target_pairs={{0,256},{256,0},{1,257},{257,1},{2,258},{258,2},{3,259},{259,3},{4... | collective-permute-start | bytes 147464 | tf_op jit(solution)/shard_map/ppermute | solution.py:418
  59.7 15.3 %all-to-all-start.1 = ((bf16[16,4,3072]{2,1,0:T(4,128)(2,1)}), bf16[16,4,3072]{2,1,0:T(4,128)(2,1)S(1)}, u32[]{:S(2)}, u32[]{:S(2)}) async-start(bf16[16,4,3072]{2,1,0:T(4,128)(2,1)} %get-tuple-element.31), calls=%async_computation.1 | async-start | bytes 786432 | tf_op jit(solution)/shard_map/all_to_all | solution.py:414
  65.6 5.0 %collective-permute-start.5 = (f32[4,6144]{1,0:T(4,128)S(1)}, f32[4,6144]{1,0:T(4,128)S(1)}, u32[]{:S(2)}, u32[]{:S(2)}) collective-permute-start(f32[4,6144]{1,0:T(4,128)S(1)} %pad_maximum_fusion.mine), channel_id=1, source_target_pairs={{0,128},{128,0},{1,129},{129,1},{2,130},{130,2},{3,131},{131,3},{4... | collective-permute-start | bytes 294920 | tf_op jit(solution)/shard_map/ppermute | solution.py:418
  94.9 10.3 %collective-permute-start.6 = (bf16[4,32,6144]{2,1,0:T(8,128)(2,1)S(1)}, bf16[4,32,6144]{2,1,0:T(8,128)(2,1)S(1)}, u32[]{:S(2)}, u32[]{:S(2)}) collective-permute-start(bf16[4,32,6144]{2,1,0:T(8,128)(2,1)S(1)} %all_to_all.15.piece), channel_id=1, source_target_pairs={{0,128},{128,0},{1,129},{129,1},{2,130},{130,2},{3,131},{131,3},{4... | collective-permute-start | bytes 4718600 | tf_op jit(solution)/shard_map/ppermute | solution.py:418
